TPU v7x, 32 devices: a whole 2x2x4 slice. The times are simulated.
32 devices in a mesh: case: 2 (over x), elem: 16 (over z, y, core).
Axes of the slice: x: 2, y: 2, z: 4, core: 2. Of those that a mesh axis runs over, the one named last changes fastest.
Arguments:
- load_coef: bfloat16 [1024, 512], P(('case', 'elem')), may hold values from -13 to 13
- mantissa: bfloat16 [512, 3, 16384], P(None, None, 'elem'), may hold values from -0.25 to 0.25
- scale_exp: int32 [512, 3, 128], P(None, None, 'elem'), may hold values from -1 to 1
- lin_coef: float32 [2, 16384], P(None, 'elem'), may hold values from -0.5 to 0.5
- quad_coef: float32 [3, 16384], P(None, 'elem'), may hold values from 0.05 to 0.3
- cross_coef: float32 [16384], P('elem'), may hold values from -0.1 to 0.1
- ply_count: int32 [16384], P('elem'), may hold values from 0 to 7
- cotangent: float32 [1024], P('case'), may hold values from -6 to 6
Outputs:
- load_grad: float32 [1024, 512], P(('case', 'elem'))
- coef_grad: float32 [6, 16384], P(None, 'elem')
All inputs are finite; a program needn't handle non-finite values.
Results may differ from a plain program's by a relative error of at most 0.0065.
Values may be sent and summed in bfloat16 or wider, within the bound.
No kernel may reach another device: no remote copies, remote signals or barrier semaphores. Data moves between devices by JAX's collectives and lax.ppermute only.
A program may use at most 64 MiB of HBM per device.

v0:
```python
import jax
import jax.numpy as jnp
from jax import lax
from jax.sharding import PartitionSpec as P

rho_value = 1.0


def per_device(
    load_coef, mantissa, scale_exp, lin_coef, quad_coef, cross_coef, ply_count, cotangent
):
    units, comps, width = mantissa.shape
    blocks = scale_exp.shape[2]
    factor = jnp.exp2(scale_exp.astype(jnp.float32)).astype(jnp.bfloat16)
    fields = (mantissa.reshape(units, comps, blocks, width // blocks) * factor[..., None]).reshape(
        units, comps * width
    )
    stress = jnp.dot(
        lax.all_gather(load_coef, "elem", axis=0, tiled=True),
        fields,
        preferred_element_type=jnp.float32,
    )
    first = stress[:, :width]
    second = stress[:, width : 2 * width]
    shear = stress[:, 2 * width :]
    plies = (ply_count + 1).astype(jnp.float32)
    index = (
        lin_coef[0] * first
        + lin_coef[1] * second
        + quad_coef[0] * first * first
        + quad_coef[1] * second * second
        + quad_coef[2] * shear * shear
        + 2.0 * cross_coef * first * second
    )
    local_peak = jnp.max(index, axis=1)
    peak = lax.pmax(local_peak, "elem")
    local_total = jnp.sum(plies * jnp.exp(rho_value * (index - peak[:, None])), axis=1)
    total = lax.psum(local_total, "elem")
    envelope = peak + jnp.log(total) / rho_value
    weight = cotangent[:, None] * plies * jnp.exp(rho_value * (index - envelope[:, None]))
    grad_one = weight * (lin_coef[0] + 2.0 * quad_coef[0] * first + 2.0 * cross_coef * second)
    grad_two = weight * (lin_coef[1] + 2.0 * quad_coef[1] * second + 2.0 * cross_coef * first)
    grad_three = weight * (2.0 * quad_coef[2] * shear)
    dstress = jnp.concatenate([grad_one, grad_two, grad_three], axis=1).astype(jnp.bfloat16)
    coef_local = jnp.stack(
        [
            jnp.sum(weight * first, axis=0),
            jnp.sum(weight * second, axis=0),
            jnp.sum(weight * first * first, axis=0),
            jnp.sum(weight * second * second, axis=0),
            jnp.sum(weight * shear * shear, axis=0),
            jnp.sum(weight * 2.0 * first * second, axis=0),
        ]
    )
    terms = lax.dot_general(
        dstress, fields, (((1,), (1,)), ((), ())), preferred_element_type=jnp.float32
    )
    load_grad = lax.psum_scatter(terms, "elem", scatter_dimension=0, tiled=True)
    coef_grad = lax.psum(coef_local, "case")
    return (load_grad, coef_grad)


def solution(mesh):
    return jax.shard_map(
        per_device,
        mesh=mesh,
        in_specs=(
            P(("case", "elem"), None),
            P(None, None, "elem"),
            P(None, None, "elem"),
            P(None, "elem"),
            P(None, "elem"),
            P("elem"),
            P("elem"),
            P("case"),
        ),
        out_specs=(P(("case", "elem"), None), P(None, "elem")),
        check_vma=False,
    )
```

profile of v0, /device:TPU:0, one launch (start us, length us, event | category | flops | bytes accessed | tf_op | source)
XLA Modules:
  0.0 175.4 jit_solution(10828518914398300780)
XLA Ops:
  7.2 0.0 reduce-scatter.2.cloned.1.call-start
  7.2 0.7 broadcast_multiply_fusion.3
  7.9 0.7 add_convert_fusion
  8.6 0.8 fusion.14
  9.4 0.8 exponential_convert_fusion
  10.2 0.9 broadcast_multiply_fusion.2
  11.0 26.4 %all_gather.3 = bf16[512,512]{1,0:T(8,128)(2,1)} all-gather(bf16[32,512]{1,0:T(8,128)(2,1)} %param.8), channel_id=1, replica_groups=mesh['case'=2,'elem'=16] {'elem'}, dimensions={0}, use_global_device_ids=true | all-gather | bytes 557056 | tf_op jit(solution)/shard_map/all_gather | solution.py:19
  37.4 3.2 %copy.11 = bf16[512,3,1024]{0,2,1:T(8,128)(2,1)S(1)} copy(bf16[512,3,1024]{2,0,1:T(8,128)(2,1)} %param.9) | data formatting | bytes 6291456 | tf_op args[1]
  40.6 0.0 copy-start.3
  40.6 0.4 bitcast_multiply_fusion
  41.1 0.6 copy-done.3
  41.7 0.0 copy-start.1
  41.7 1.8 %convolution_bitcast_fusion = f32[512,3072]{1,0:T(8,128)S(1)} fusion(bf16[512,3072]{0,1:T(8,128)(2,1)S(1)} %bitcast_multiply_fusion, bf16[512,512]{1,0:T(8,128)(2,1)S(1)} %copy-done.3), kind=kOutput, calls=%fused_computation | convolution fusion | flops 1610612736 | bytes 9961472 | tf_op jit(solution)/shard_map/dot_general | solution.py:18
  43.5 0.0 copy-done.1
  43.5 0.0 copy-start
  43.5 1.4 fusion.12
  45.0 1.2 copy-done
  46.2 0.0 copy-start.4
  46.2 29.9 %pmax.7 = f32[512]{0:T(512)S(1)} all-reduce(f32[512]{0:T(512)S(1)} %get-tuple-element.8), channel_id=1, replica_groups=mesh['case'=2,'elem'=16] {'elem'}, use_global_device_ids=true, to_apply=%region_1.0 | all-reduce | flops 512 | bytes 4096 | tf_op jit(solution)/shard_map/pmax | solution.py:36
  76.1 0.5 multiply_reduce_fusion.3
  76.7 29.5 %psum.14 = f32[512]{0:T(512)S(1)} all-reduce(f32[512]{0:T(512)S(1)} %multiply_reduce_fusion.3), channel_id=1, replica_groups=mesh['case'=2,'elem'=16] {'elem'}, use_global_device_ids=true, to_apply=%region_3.0 | all-reduce | flops 512 | bytes 4096 | tf_op jit(solution)/shard_map/psum | solution.py:38
  106.2 0.0 copy-done.4
  106.2 0.0 copy-start.2
  106.2 4.8 %multiply_reduce_fusion = (f32[1024]{0:T(1024)S(1)}, f32[1024]{0:T(1024)S(1)}, f32[1024]{0:T(1024)S(1)}, f32[1024]{0:T(1024)S(1)}, f32[1024]{0:T(1024)S(1)}, /*i...) fusion(f32[512,3072]{1,0:T(8,128)} %copy-done, ...), kind=kLoop, calls=%fused_computation.17 | loop fusion | flops 17295360 | bytes 11591680 | tf_op jit(solution)/shard_map/reduce_sum | solution.py:52
  111.0 0.0 copy-done.2
  111.0 2.8 %fusion = f32[512,512]{1,0:T(8,128)} fusion(bf16[512,3072]{0,1:T(8,128)(2,1)S(1)} %copy-done.2, bf16[512,1024]{1,0:T(8,128)(2,1)S(1)} %get-tuple-element.12, bf16[512,1024]{1,0:T(8,128)(2,1)S(1)} %get-tuple-element.13, bf16[512,1024]{1,0:T(8,128)(2,1)S(1)} %get-tuple-element.14), kind=kOutput, calls=%fused_computation.1 | convolution fusion | flops 1620049920 | bytes 7340032 | tf_op jit(solution)/shard_map/dot_general | solution.py:55
  113.7 0.0 reduce-scatter.2.cloned.1.call-update
  113.8 0.1 stack.27
  113.8 8.9 %psum.15 = f32[6,1024]{1,0:T(8,128)} all-reduce(f32[6,1024]{1,0:T(8,128)S(1)} %stack.27), channel_id=1, replica_groups=mesh['case'=2,'elem'=16] {'case'}, use_global_device_ids=true, to_apply=%region_11.0 | all-reduce | flops 6144 | bytes 49152 | tf_op jit(solution)/shard_map/psum | solution.py:59
  122.8 45.7 %reduce-scatter.2.cloned.1.call-done = f32[32,512]{1,0:T(8,128)} async-done(((f32[512,512]{1,0:T(8,128)}), f32[32,512]{1,0:T(8,128)}) %reduce-scatter.2.cloned.1.call-update) | async-done | bytes 65552 | tf_op jit(solution)/shard_map/reduce_scatter | solution.py:58
  (1 shorter events, 0.0 us)
Async XLA Ops:
  7.2 161.3 %reduce-scatter.2.cloned.1.call-start = ((), (), s32[]{:S(2)}) async-start(), calls=%async_computation.1 | async-start | bytes 1114112 | tf_op jit(solution)/shard_map/reduce_scatter | solution.py:58
  40.6 1.0 copy-start.3
  41.7 1.8 %copy-start.1 = (bf16[512,3072]{0,1:T(8,128)(2,1)}, bf16[512,3072]{0,1:T(8,128)(2,1)S(1)}, u32[]{:S(2)}) copy-start(bf16[512,3072]{0,1:T(8,128)(2,1)S(1)} %bitcast_multiply_fusion) | copy-start | bytes 9437188
  43.5 2.7 %copy-start = (f32[512,3072]{1,0:T(8,128)}, f32[512,3072]{1,0:T(8,128)S(1)}, u32[]{:S(2)}) copy-start(f32[512,3072]{1,0:T(8,128)S(1)} %convolution_bitcast_fusion) | copy-start | bytes 18874372
  46.2 60.0 %copy-start.4 = (f32[512]{0:T(512)S(1)}, f32[512]{0:T(512)}, u32[]{:S(2)}) copy-start(f32[512]{0:T(512)} %param.15) | copy-start | bytes 6148
  106.2 4.8 %copy-start.2 = (bf16[512,3072]{0,1:T(8,128)(2,1)S(1)}, bf16[512,3072]{0,1:T(8,128)(2,1)}, u32[]{:S(2)}) copy-start(bf16[512,3072]{0,1:T(8,128)(2,1)} %copy-done.1) | copy-start | bytes 9437188
Sparse Core Ops, SparseCore 0:
  113.9 54.5 reduce-scatter.1
where the time goes:
time: 176 us; the launch traced here: 175 us
  blocking collectives  94.8 us (54%)
  waiting for transfers between devices  45.8 us (26%)
  between operations  14.1 us (8%)
  other arithmetic  10.2 us (6%)
  local copies, waits for them, and re-layouts  5.85 us (3%)
  matrix products  4.6 us (3%)
    reduce_scatter x1, waiting for transfers between devices, per_device(): load_grad = lax.psum_scatter(terms, 'elem', scatter_dimension=0, tiled=True)  45.7 us
    pmax x1, blocking collectives, per_device(): peak = lax.pmax(local_peak, 'elem')  29.9 us
    psum x1, blocking collectives, per_device(): total = lax.psum(local_total, 'elem')  29.5 us
    all_gather x1, blocking collectives, per_device(): lax.all_gather(load_coef, 'elem', axis=0, tiled=True)  26.4 us
    psum x1, blocking collectives, per_device(): coef_grad = lax.psum(coef_local, 'case')  8.94 us
    unnamed x11, local copies, waits for them, and re-layouts  5.02 us
    reduce_sum x1, other arithmetic, per_device(): jnp.sum(weight * 2.0 * first * second, axis=0)  4.79 us
  transfers between devices with their start and end apart: 1, of which 1 were waited for; matrix products, arithmetic and copies ran while one was open for 0% of the time, Pallas kernels for 0%

commit v1 on v0

v1 whole, which is shorter than its diff:
```python
import functools

import jax
import jax.numpy as jnp
from jax import lax
from jax.experimental import pallas as pl
from jax.experimental.pallas import tpu as pltpu
from jax.sharding import PartitionSpec as P

JB = 256
VMEM = pltpu.VMEM


def vmem_call(kernel, out_shape, scratch_shapes=(), flops=0, nbytes=0, exps=0, n_in=0, smem=(), limit=40):
    return pl.pallas_call(
        kernel,
        out_shape=out_shape,
        in_specs=[
            pl.BlockSpec(memory_space=pltpu.SMEM if i in smem else VMEM) for i in range(n_in)
        ],
        out_specs=jax.tree.map(lambda _: pl.BlockSpec(memory_space=VMEM), out_shape),
        scratch_shapes=list(scratch_shapes),
        cost_estimate=pl.CostEstimate(flops=flops, bytes_accessed=nbytes, transcendentals=exps),
        compiler_params=pltpu.CompilerParams(vmem_limit_bytes=limit << 20),
    )


def to_lanes(column, rows):
    step = min(rows, 128)
    parts = []
    for at in range(0, rows, step):
        square = jnp.broadcast_to(column[at : at + step], (step, 128))
        parts.append(jnp.transpose(square)[0:1, :])
    return jnp.concatenate(parts, axis=1)


def to_rows(row, at):
    return jnp.transpose(jnp.broadcast_to(row[:, at : at + 128], (128, 128)))


def prep_kernel(mant_ref, exp_ref, out_ref):
    comps, units, width = mant_ref.shape
    blocks = exp_ref.shape[1]
    span = width // blocks
    factor = jnp.exp2(exp_ref[...].astype(jnp.float32)).reshape(comps * blocks, units)
    pad = jnp.zeros((128 - comps * blocks, units), jnp.float32)
    columns = jnp.transpose(jnp.concatenate([factor, pad], axis=0))
    for k in range(comps):
        for b in range(blocks):
            gain = jnp.broadcast_to(columns[:, k * blocks + b : k * blocks + b + 1], (units, span))
            value = mant_ref[k, :, b * span : (b + 1) * span] * gain.astype(jnp.bfloat16)
            first = b * span
            at = (first // JB) * (comps * JB) + k * JB + first % JB
            out_ref[:, at : at + span] = value


def main_kernel(n, a_ref, f_ref, lin_ref, quad_ref, cross_ref, ply_ref, *refs):
    own_ref = refs[0]
    send_refs = refs[1:n]
    stat_ref, s_ref, w_ref, idx, d, acc = refs[n:]
    cases = a_ref.shape[0]
    width = lin_ref.shape[1]
    rows = cases // n
    tile = 32
    peak = jnp.full((cases, 128), -jnp.inf, jnp.float32)
    for jb in range(width // JB):
        cols = slice(jb * JB, (jb + 1) * JB)
        base = jb * 3 * JB
        s_ref[:, base : base + 3 * JB] = jnp.dot(
            a_ref[...], f_ref[:, base : base + 3 * JB], preferred_element_type=jnp.float32
        )
        f1, f2 = lin_ref[0:1, cols], lin_ref[1:2, cols]
        f11, f22, f66 = quad_ref[0:1, cols], quad_ref[1:2, cols], quad_ref[2:3, cols]
        f12 = 2.0 * cross_ref[0:1, cols]
        tops = []
        for at in range(0, cases, tile):
            r = slice(at, at + tile)
            s1 = s_ref[r, base : base + JB]
            s2 = s_ref[r, base + JB : base + 2 * JB]
            t = s_ref[r, base + 2 * JB : base + 3 * JB]
            index = s1 * (f1 + f11 * s1 + f12 * s2) + s2 * (f2 + f22 * s2) + f66 * (t * t)
            idx[r, cols] = index
            top = index[:, 0:128]
            for c in range(128, JB, 128):
                top = jnp.maximum(top, index[:, c : c + 128])
            tops.append(top)
        peak = jnp.maximum(peak, jnp.concatenate(tops, axis=0))
    peak = jnp.max(peak, axis=1, keepdims=True)

    total = jnp.zeros((cases, 128), jnp.float32)
    for jb in range(width // JB):
        cols = slice(jb * JB, (jb + 1) * JB)
        base = jb * 3 * JB
        f1, f2 = lin_ref[0:1, cols], lin_ref[1:2, cols]
        q11, q22, q66 = 2.0 * quad_ref[0:1, cols], 2.0 * quad_ref[1:2, cols], 2.0 * quad_ref[2:3, cols]
        f12 = 2.0 * cross_ref[0:1, cols]
        plies = (ply_ref[0:1, cols] + 1).astype(jnp.float32)
        sums = []
        for at in range(0, cases, tile):
            r = slice(at, at + tile)
            s1 = s_ref[r, base : base + JB]
            s2 = s_ref[r, base + JB : base + 2 * JB]
            t = s_ref[r, base + 2 * JB : base + 3 * JB]
            w = plies * jnp.exp(idx[r, cols] - peak[r])
            w_ref[r, cols] = w
            part = w[:, 0:128]
            for c in range(128, JB, 128):
                part = part + w[:, c : c + 128]
            sums.append(part)
            d[r, base : base + JB] = (w * (f1 + q11 * s1 + f12 * s2)).astype(jnp.bfloat16)
            d[r, base + JB : base + 2 * JB] = (w * (f2 + q22 * s2 + f12 * s1)).astype(jnp.bfloat16)
            d[r, base + 2 * JB : base + 3 * JB] = (w * (q66 * t)).astype(jnp.bfloat16)
        total = total + jnp.concatenate(sums, axis=0)
        part = lax.dot_general(
            d[:, base : base + 3 * JB],
            f_ref[:, base : base + 3 * JB],
            (((1,), (1,)), ((), ())),
            preferred_element_type=jnp.float32,
        )
        if jb == 0:
            acc[...] = part
        else:
            acc[...] += part
    total = jnp.sum(total, axis=1, keepdims=True)
    stat_ref[0:1, :] = to_lanes(peak, cases)
    stat_ref[1:2, :] = to_lanes(total, cases)
    own_ref[...] = acc[0:rows, :]
    for p in range(1, n):
        send_refs[p - 1][...] = acc[p * rows : (p + 1) * rows, :].astype(jnp.bfloat16)


def swap_lanes(x, which, rows, n):
    lane = lax.broadcasted_iota(jnp.int32, x.shape, 1)
    bit = 1
    while bit < n:
        step = bit * rows
        ahead = jnp.concatenate([x[:, step:], x[:, :step]], axis=1)
        behind = jnp.concatenate([x[:, -step:], x[:, :-step]], axis=1)
        other = jnp.where((lane & step) != 0, behind, ahead)
        x = jnp.where((which & bit) != 0, other, x)
        bit *= 2
    return x


def coef_kernel(n, me_ref, cot_ref, s_ref, w_ref, *refs):
    stat_refs = refs[:n]
    coef_ref, gain_ref, peaks, totals = refs[n:]
    cases = cot_ref.shape[1]
    width = w_ref.shape[1]
    rows = cases // n
    for p in range(n):
        peaks[p : p + 1, :] = stat_refs[p][0:1, :]
        totals[p : p + 1, :] = stat_refs[p][1:2, :]
    which = lax.broadcasted_iota(jnp.int32, (n, cases), 0)
    peak_all = swap_lanes(peaks[...], which, rows, n)
    total_all = swap_lanes(totals[...], which, rows, n)
    mine = jnp.full((8, cases), me_ref[0], jnp.int32)
    cot = swap_lanes(jnp.broadcast_to(cot_ref[...], (8, cases)), mine, rows, n)[0:1]
    peak = jnp.max(peak_all, axis=0, keepdims=True)
    total = jnp.sum(total_all * jnp.exp(peak_all - peak), axis=0, keepdims=True)
    envelope = peak + jnp.log(total)
    gain = cot * jnp.exp(peak_all - envelope)
    square = gain[:, 0:128]
    if n < 128:
        square = jnp.concatenate([square, jnp.zeros((128 - n, 128), jnp.float32)], axis=0)
    gain_ref[...] = jnp.transpose(square)[0:rows]
    mine = gain[0:1]
    scales = [to_rows(mine, at) for at in range(0, cases, 128)]
    for jb in range(width // JB):
        base = jb * 3 * JB
        for c in range(0, JB, 128):
            sums = [jnp.zeros((8, 128), jnp.float32) for _ in range(6)]
            for at in range(0, cases, 8):
                r = slice(at, at + 8)
                s1 = s_ref[r, base + c : base + c + 128]
                s2 = s_ref[r, base + JB + c : base + JB + c + 128]
                t = s_ref[r, base + 2 * JB + c : base + 2 * JB + c + 128]
                local = at % 128
                w = w_ref[r, jb * JB + c : jb * JB + c + 128] * scales[at // 128][local : local + 8]
                a, b = w * s1, w * s2
                for i, v in enumerate((a, b, a * s1, b * s2, w * t * t, a * s2)):
                    sums[i] = sums[i] + v
            for i in range(6):
                line = jnp.sum(sums[i], axis=0, keepdims=True)
                if i == 5:
                    line = 2.0 * line
                coef_ref[i : i + 1, jb * JB + c : jb * JB + c + 128] = line


def combine_kernel(n, gain_ref, own_ref, *refs):
    out_ref = refs[-1]
    value = own_ref[...] * gain_ref[:, 0:1]
    for p in range(1, n):
        value = value + refs[p - 1][...].astype(jnp.float32) * gain_ref[:, p : p + 1]
    out_ref[...] = value


def per_device(n, n_case, load_coef, mantissa, scale_exp, lin_coef, quad_coef, cross_coef, ply_count, cotangent):
    units, comps, width = mantissa.shape
    rows = load_coef.shape[0]
    cases = rows * n
    f32, bf16 = jnp.float32, jnp.bfloat16
    shape = jax.ShapeDtypeStruct

    def swap(x, axis, size, p):
        return lax.ppermute(x, axis, [(i, i ^ p) for i in range(size)])

    gathered = load_coef
    bit = n // 2
    order = [0]
    while bit:
        gathered = jnp.concatenate([gathered, swap(gathered, "elem", n, bit)], axis=0)
        order = order + [p ^ bit for p in order]
        bit //= 2
    place = {p: i for i, p in enumerate(order)}
    gathered = jnp.concatenate(
        [lax.slice_in_dim(gathered, place[p] * rows, place[p] * rows + rows) for p in range(n)]
    )

    fields = vmem_call(
        prep_kernel,
        shape((units, comps * width), bf16),
        flops=units * comps * width,
        nbytes=4 * units * comps * width,
        n_in=2,
    )(jnp.transpose(mantissa, (1, 0, 2)), jnp.transpose(scale_exp, (1, 2, 0)))

    outs = vmem_call(
        functools.partial(main_kernel, n),
        [shape((rows, units), f32)]
        + [shape((rows, units), bf16)] * (n - 1)
        + [shape((2, cases), f32), shape((cases, comps * width), f32), shape((cases, width), f32)],
        scratch_shapes=[
            VMEM((cases, width), f32),
            VMEM((cases, comps * width), bf16),
            VMEM((cases, units), f32),
        ],
        flops=4 * cases * units * comps * width,
        nbytes=2 * units * comps * width + 4 * cases * 4 * width,
        exps=cases * width,
        n_in=6,
    )(gathered, fields, lin_coef, quad_coef, cross_coef.reshape(1, width), ply_count.reshape(1, width))
    own, sends, stat, stress, weight = outs[0], outs[1:n], outs[n], outs[n + 1], outs[n + 2]

    stats = [stat] + [swap(stat, "elem", n, p) for p in range(1, n)]
    parts = [swap(sends[p - 1], "elem", n, p) for p in range(1, n)]

    me = lax.axis_index("elem").astype(jnp.int32).reshape(1)
    coef, gain = vmem_call(
        functools.partial(coef_kernel, n),
        [shape((6, width), f32), shape((rows, 128), f32)],
        scratch_shapes=[VMEM((n, cases), f32), VMEM((n, cases), f32)],
        flops=14 * cases * width,
        nbytes=16 * cases * width,
        n_in=4 + n,
        smem=(0,),
    )(me, cotangent.reshape(1, cases), stress, weight, *stats)
    bit = 1
    while bit < n_case:
        coef = coef + swap(coef, "case", n_case, bit)
        bit *= 2

    load_grad = vmem_call(
        functools.partial(combine_kernel, n),
        shape((rows, units), f32),
        flops=2 * n * rows * units,
        nbytes=2 * n * rows * units,
        n_in=1 + n,
    )(gain, own, *parts)
    return (load_grad, coef)


def solution(mesh):
    n, n_case = mesh.shape["elem"], mesh.shape["case"]
    return jax.shard_map(
        functools.partial(per_device, n, n_case),
        mesh=mesh,
        in_specs=(
            P(("case", "elem"), None),
            P(None, None, "elem"),
            P(None, None, "elem"),
            P(None, "elem"),
            P(None, "elem"),
            P("elem"),
            P("elem"),
            P("case"),
        ),
        out_specs=(P(("case", "elem"), None), P(None, "elem")),
        check_vma=False,
    )
```

time: 176 us -> 86.8 us (0.49)
  blocking collectives: 94.8 us -> 0 us
  starting transfers between devices: 0.04 us -> 51.2 us
  waiting for transfers between devices: 45.8 us -> 15.3 us
  between operations: 14.1 us -> 0.92 us
  Pallas kernels: 0 us -> 7.74 us
  other arithmetic: 10.2 us -> 2.92 us
  matrix products: 4.6 us -> 0 us
  local copies, waits for them, and re-layouts: 5.85 us -> 8.25 us
    ppermute x0 -> x35, starting transfers between devices: none -> 51.2 us  [swap(): return lax.ppermute(x, axis, [(i, i ^ p) for i in range(size)])]
    reduce_scatter x1 -> x0, waiting for transfers between devices: 45.7 us -> none  [per_device(): load_grad = lax.psum_scatter(terms, 'elem', scatter_dimension=0, tiled=True)]
    psum x2 -> x0, blocking collectives: 38.4 us -> none  [the longest x1 29.5 us: per_device(): total = lax.psum(local_total, 'elem')]
    pmax x1 -> x0, blocking collectives: 29.9 us -> none  [per_device(): peak = lax.pmax(local_peak, 'elem')]
    all_gather x1 -> x0, blocking collectives: 26.4 us -> none  [per_device(): lax.all_gather(load_coef, 'elem', axis=0, tiled=True)]
    ppermute x0 -> x35, waiting for transfers between devices: none -> 15.3 us  [swap(): return lax.ppermute(x, axis, [(i, i ^ p) for i in range(size)])]
    pallas_call x0 -> x4, Pallas kernels: none -> 7.74 us  [the longest x1 4.33 us: per_device(): vmem_call(functools.partial(main_kernel, n), [shape((rows, units), f32)]...]
    reduce_sum x2 -> x0, other arithmetic: 5.33 us -> none  [the longest x1 4.79 us: per_device(): jnp.sum(weight * 2.0 * first * second, axis=0)]
  transfers between devices with their start and end apart: 1 -> 35, of which waited for: 1 -> 8; matrix products, arithmetic and copies ran while one was open for 0% -> 1% of each run, Pallas kernels for 0% -> 1%
where the time goes in v1:
time: 86.8 us; the launch traced here: 86.3 us
  starting transfers between devices  51.2 us (59%)
  waiting for transfers between devices  15.3 us (18%)
  local copies, waits for them, and re-layouts  8.25 us (10%)
  Pallas kernels  7.74 us (9%)
  other arithmetic  2.92 us (3%)
  between operations  0.92 us (1%)
    ppermute x35, starting transfers between devices, swap(): return lax.ppermute(x, axis, [(i, i ^ p) for i in range(size)])  51.2 us
    ppermute x35, waiting for transfers between devices, swap(): return lax.ppermute(x, axis, [(i, i ^ p) for i in range(size)])  15.3 us
    unnamed x35, local copies, waits for them, and re-layouts  8.24 us
    pallas_call x1, Pallas kernels, per_device(): vmem_call(functools.partial(main_kernel, n), [shape((rows, units), f32)]...  4.33 us
    concatenate x3, other arithmetic, per_device(): jnp.concatenate([gathered, swap(gathered, 'elem', n, bit)], axis=0)  2.3 us
  transfers between devices with their start and end apart: 35, of which 8 were waited for; matrix products, arithmetic and copies ran while one was open for 1% of the time, Pallas kernels for 1%

profile of v1, /device:TPU:0, one launch (start us, length us, event | category | flops | bytes accessed | tf_op | source)
XLA Modules:
  0.0 86.3 jit_solution(17054028123602170392)
XLA Ops:
  0.6 4.1 %collective-permute-start = (bf16[32,512]{1,0:T(8,128)(2,1)}, bf16[32,512]{1,0:T(8,128)(2,1)S(1)}, u32[]{:S(2)}, u32[]{:S(2)}) collective-permute-start(bf16[32,512]{1,0:T(8,128)(2,1)} %param.8), channel_id=1, source_target_pairs={{0,8},{1,9},{2,10},{3,11},{4,12},{5,13},{6,14},{7,15},{8,0},{9,1},... | collective-permute-start | bytes 98312 | tf_op jit(solution)/shard_map/ppermute | solution.py:206
  4.7 2.5 %collective-permute-done = bf16[32,512]{1,0:T(8,128)(2,1)S(1)} collective-permute-done((bf16[32,512]{1,0:T(8,128)(2,1)}, bf16[32,512]{1,0:T(8,128)(2,1)S(1)}, u32[]{:S(2)}, u32[]{:S(2)}) %collective-permute-start) | collective-permute-done | bytes 32800 | tf_op jit(solution)/shard_map/ppermute | solution.py:206
  7.2 0.8 pad_maximum_fusion.2
  8.0 1.6 %collective-permute-start.1 = (bf16[64,512]{1,0:T(8,128)(2,1)S(1)}, bf16[64,512]{1,0:T(8,128)(2,1)S(1)}, u32[]{:S(2)}, u32[]{:S(2)}) collective-permute-start(bf16[64,512]{1,0:T(8,128)(2,1)S(1)} %pad_maximum_fusion.2), channel_id=1, source_target_pairs={{0,4},{1,5},{2,6},{3,7},{4,0},{5,1},{6,2},{7,3},{8,12},{9,13},{10,... | collective-permute-start | bytes 196616 | tf_op jit(solution)/shard_map/ppermute | solution.py:206
  9.5 2.7 %collective-permute-done.1 = bf16[64,512]{1,0:T(8,128)(2,1)S(1)} collective-permute-done((bf16[64,512]{1,0:T(8,128)(2,1)S(1)}, bf16[64,512]{1,0:T(8,128)(2,1)S(1)}, u32[]{:S(2)}, u32[]{:S(2)}) %collective-permute-start.1) | collective-permute-done | bytes 65568 | tf_op jit(solution)/shard_map/ppermute | solution.py:206
  12.2 0.8 pad_maximum_fusion.1
  13.0 1.8 %collective-permute-start.2 = (bf16[128,512]{1,0:T(8,128)(2,1)S(1)}, bf16[128,512]{1,0:T(8,128)(2,1)S(1)}, u32[]{:S(2)}, u32[]{:S(2)}) collective-permute-start(bf16[128,512]{1,0:T(8,128)(2,1)S(1)} %pad_maximum_fusion.1), channel_id=1, source_target_pairs={{0,2},{1,3},{2,0},{3,1},{4,6},{5,7},{6,4},{7,5},{8,10},{9,11},{10,... | collective-permute-start | bytes 393224 | tf_op jit(solution)/shard_map/ppermute | solution.py:206
  14.8 3.2 %collective-permute-done.2 = bf16[128,512]{1,0:T(8,128)(2,1)S(1)} collective-permute-done((bf16[128,512]{1,0:T(8,128)(2,1)S(1)}, bf16[128,512]{1,0:T(8,128)(2,1)S(1)}, u32[]{:S(2)}, u32[]{:S(2)}) %collective-permute-start.2) | collective-permute-done | bytes 131104 | tf_op jit(solution)/shard_map/ppermute | solution.py:206
  18.0 0.8 pad_maximum_fusion
  18.8 0.1 collective-permute-start.3
  18.9 0.0 copy-start.2
  18.9 1.9 %copy-done.2 = bf16[512,3,1024]{2,0,1:T(8,128)(2,1)S(1)} copy-done((bf16[512,3,1024]{2,0,1:T(8,128)(2,1)S(1)}, bf16[512,3,1024]{2,0,1:T(8,128)(2,1)}, u32[]{:S(2)}) %copy-start.2) | copy-done | bytes 3145752
  20.8 0.8 copy-done.3
  21.6 0.0 copy-start.8
  21.6 1.0 %shard_map.95.f_ref = bf16[512,3072]{1,0:T(8,128)(2,1)S(1)} custom-call(bf16[3,512,1024]{2,1,0:T(8,128)(2,1)S(1)} %bitcast.6, s32[3,8,512]{2,1,0:T(8,128)S(1)} %bitcast.7), custom_call_target="tpu_custom_call" | custom-call | flops 1572864 | bytes 6291456 | tf_op jit(solution)/shard_map/pallas_call | solution.py:220
  22.7 0.0 collective-permute-done.3
  22.9 0.0 copy-start.4
  22.9 4.3 %shard_map.96 = (f32[32,512]{1,0:T(8,128)S(1)}, bf16[32,512]{1,0:T(8,128)(2,1)S(1)}, bf16[32,512]{1,0:T(8,128)(2,1)S(1)}, bf16[32,512]{1,0:T(8,128)(2,1)S(1)}, b...) custom-call(bf16[512,512]{1,0:T(8,128)(2,1)S(1)} %constant_dynamic-u, ...), custom_call_target="tpu_custom_call" | custom-call | flops 3221225472 | bytes 11534336 | tf_op jit(solution)/shard_map/pallas_call | solution.py:228
  27.3 2.7 %copy-done = f32[512,3072]{1,0:T(8,128)} copy-done((f32[512,3072]{1,0:T(8,128)}, f32[512,3072]{1,0:T(8,128)S(1)}, u32[]{:S(2)}) %copy-start) | copy-done | bytes 6291480
  29.9 2.6 %collective-permute-start.10 = (f32[2,512]{1,0:T(2,128)S(1)}, f32[2,512]{1,0:T(2,128)S(1)}, u32[]{:S(2)}, u32[]{:S(2)}) collective-permute-start(f32[2,512]{1,0:T(2,128)S(1)} %get-tuple-element.25.refs_0_), channel_id=1, source_target_pairs={{0,7},{1,6},{2,5},{3,4},{4,3},{5,2},{6,1},{7,0},{8,15},{9,14},{10,... | collective-permute-start | bytes 12296 | tf_op jit(solution)/shard_map/ppermute | solution.py:206
  32.6 2.8 %collective-permute-start.11 = (f32[2,512]{1,0:T(2,128)S(1)}, f32[2,512]{1,0:T(2,128)S(1)}, u32[]{:S(2)}, u32[]{:S(2)}) collective-permute-start(f32[2,512]{1,0:T(2,128)S(1)} %get-tuple-element.25.refs_0_), channel_id=1, source_target_pairs={{0,8},{1,9},{2,10},{3,11},{4,12},{5,13},{6,14},{7,15},{8,0},{9,1},... | collective-permute-start | bytes 12296 | tf_op jit(solution)/shard_map/ppermute | solution.py:206
  35.4 0.0 collective-permute-start.12
  35.4 2.2 %collective-permute-start.13 = (f32[2,512]{1,0:T(2,128)S(1)}, f32[2,512]{1,0:T(2,128)S(1)}, u32[]{:S(2)}, u32[]{:S(2)}) collective-permute-start(f32[2,512]{1,0:T(2,128)S(1)} %get-tuple-element.25.refs_0_), channel_id=1, source_target_pairs={{0,10},{1,11},{2,8},{3,9},{4,14},{5,15},{6,12},{7,13},{8,2},{9,3},... | collective-permute-start | bytes 12296 | tf_op jit(solution)/shard_map/ppermute | solution.py:206
  37.6 1.2 %collective-permute-start.14 = (f32[2,512]{1,0:T(2,128)S(1)}, f32[2,512]{1,0:T(2,128)S(1)}, u32[]{:S(2)}, u32[]{:S(2)}) collective-permute-start(f32[2,512]{1,0:T(2,128)S(1)} %get-tuple-element.25.refs_0_), channel_id=1, source_target_pairs={{0,11},{1,10},{2,9},{3,8},{4,15},{5,14},{6,13},{7,12},{8,3},{9,2},... | collective-permute-start | bytes 12296 | tf_op jit(solution)/shard_map/ppermute | solution.py:206
  38.7 0.0 collective-permute-done.10.refs_7_
  38.7 2.5 %collective-permute-start.15 = (f32[2,512]{1,0:T(2,128)S(1)}, f32[2,512]{1,0:T(2,128)S(1)}, u32[]{:S(2)}, u32[]{:S(2)}) collective-permute-start(f32[2,512]{1,0:T(2,128)S(1)} %get-tuple-element.25.refs_0_), channel_id=1, source_target_pairs={{0,12},{1,13},{2,14},{3,15},{4,8},{5,9},{6,10},{7,11},{8,4},{9,5},... | collective-permute-start | bytes 12296 | tf_op jit(solution)/shard_map/ppermute | solution.py:206
  41.2 1.2 %collective-permute-start.16 = (f32[2,512]{1,0:T(2,128)S(1)}, f32[2,512]{1,0:T(2,128)S(1)}, u32[]{:S(2)}, u32[]{:S(2)}) collective-permute-start(f32[2,512]{1,0:T(2,128)S(1)} %get-tuple-element.25.refs_0_), channel_id=1, source_target_pairs={{0,13},{1,12},{2,15},{3,14},{4,9},{5,8},{6,11},{7,10},{8,5},{9,4},... | collective-permute-start | bytes 12296 | tf_op jit(solution)/shard_map/ppermute | solution.py:206
  42.5 0.0 collective-permute-done.12.refs_9_
  42.5 2.1 %collective-permute-start.17 = (f32[2,512]{1,0:T(2,128)S(1)}, f32[2,512]{1,0:T(2,128)S(1)}, u32[]{:S(2)}, u32[]{:S(2)}) collective-permute-start(f32[2,512]{1,0:T(2,128)S(1)} %get-tuple-element.25.refs_0_), channel_id=1, source_target_pairs={{0,14},{1,15},{2,12},{3,13},{4,10},{5,11},{6,8},{7,9},{8,6},{9,7},... | collective-permute-start | bytes 12296 | tf_op jit(solution)/shard_map/ppermute | solution.py:206
  44.6 0.0 collective-permute-done.13.refs_10_
  44.6 2.2 %collective-permute-start.18 = (f32[2,512]{1,0:T(2,128)S(1)}, f32[2,512]{1,0:T(2,128)S(1)}, u32[]{:S(2)}, u32[]{:S(2)}) collective-permute-start(f32[2,512]{1,0:T(2,128)S(1)} %get-tuple-element.25.refs_0_), channel_id=1, source_target_pairs={{0,15},{1,14},{2,13},{3,12},{4,11},{5,10},{6,9},{7,8},{8,7},{9,6},... | collective-permute-start | bytes 12296 | tf_op jit(solution)/shard_map/ppermute | solution.py:206
  46.8 0.6 collective-permute-start.4
  47.3 0.0 collective-permute-done.15.refs_12_
  47.3 0.5 collective-permute-start.5
  47.8 0.9 %collective-permute-start.6 = (f32[2,512]{1,0:T(2,128)S(1)}, f32[2,512]{1,0:T(2,128)S(1)}, u32[]{:S(2)}, u32[]{:S(2)}) collective-permute-start(f32[2,512]{1,0:T(2,128)S(1)} %get-tuple-element.25.refs_0_), channel_id=1, source_target_pairs={{0,3},{1,2},{2,1},{3,0},{4,7},{5,6},{6,5},{7,4},{8,11},{9,10},{10,... | collective-permute-start | bytes 12296 | tf_op jit(solution)/shard_map/ppermute | solution.py:206
  48.8 0.0 collective-permute-done.17.refs_14_
  48.8 0.0 collective-permute-start.7
  48.8 1.5 %collective-permute-done.18.refs_15_ = f32[2,512]{1,0:T(2,128)S(1)} collective-permute-done((f32[2,512]{1,0:T(2,128)S(1)}, f32[2,512]{1,0:T(2,128)S(1)}, u32[]{:S(2)}, u32[]{:S(2)}) %collective-permute-start.18) | collective-permute-done | bytes 4128 | tf_op jit(solution)/shard_map/ppermute | solution.py:206
  50.3 0.6 collective-permute-start.8
  50.9 0.0 collective-permute-done.4.refs_1_
  50.9 2.3 %collective-permute-start.9 = (f32[2,512]{1,0:T(2,128)S(1)}, f32[2,512]{1,0:T(2,128)S(1)}, u32[]{:S(2)}, u32[]{:S(2)}) collective-permute-start(f32[2,512]{1,0:T(2,128)S(1)} %get-tuple-element.25.refs_0_), channel_id=1, source_target_pairs={{0,6},{1,7},{2,4},{3,5},{4,2},{5,3},{6,0},{7,1},{8,14},{9,15},{10,... | collective-permute-start | bytes 12296 | tf_op jit(solution)/shard_map/ppermute | solution.py:206
  53.2 0.1 collective-permute-done.8.refs_5_
  53.3 2.0 %collective-permute-done.9.refs_6_ = f32[2,512]{1,0:T(2,128)S(1)} collective-permute-done((f32[2,512]{1,0:T(2,128)S(1)}, f32[2,512]{1,0:T(2,128)S(1)}, u32[]{:S(2)}, u32[]{:S(2)}) %collective-permute-start.9) | collective-permute-done | bytes 4128 | tf_op jit(solution)/shard_map/ppermute | solution.py:206
  55.4 2.8 %copy-done.1 = f32[512,3072]{1,0:T(8,128)S(1)} copy-done((f32[512,3072]{1,0:T(8,128)S(1)}, f32[512,3072]{1,0:T(8,128)}, u32[]{:S(2)}) %copy-start.1) | copy-done | bytes 6291480
  58.2 1.6 %shard_map.97 = (f32[6,1024]{1,0:T(8,128)S(1)}, f32[32,128]{1,0:T(8,128)S(1)}) custom-call(s32[1]{0:T(128)} %bitcast.me_ref, f32[1,512]{1,0:T(1,128)S(1)} %bitcast.8, f32[512,3072]{1,0:T(8,128)S(1)} %copy-done.1, f32[512,1024]{1,0:T(8,128)S(1)} %get-tuple-element.24.w_ref, f32[2,512]{1,0:T(2,128)S(1)} %get-tuple-element.25.refs_0_, ...), custom_call_target="tpu_custom_call" | custom-call | flops 7340032 | bytes 8388608 | tf_op jit(solution)/shard_map/pallas_call | solution.py:249
  59.7 1.6 %collective-permute-start.34 = (f32[6,1024]{1,0:T(8,128)S(1)}, f32[6,1024]{1,0:T(8,128)S(1)}, u32[]{:S(2)}, u32[]{:S(2)}) collective-permute-start(f32[6,1024]{1,0:T(8,128)S(1)} %get-tuple-element.43), channel_id=1, source_target_pairs={{0,16},{16,0},{1,17},{17,1},{2,18},{18,2},{3,19},{19,3},{4,20},{20... | collective-permute-start | bytes 73736 | tf_op jit(solution)/shard_map/ppermute | solution.py:206
  61.3 0.8 collective-permute-start.20
  62.0 1.1 %collective-permute-start.21 = (bf16[32,512]{1,0:T(8,128)(2,1)S(1)}, bf16[32,512]{1,0:T(8,128)(2,1)S(1)}, u32[]{:S(2)}, u32[]{:S(2)}) collective-permute-start(bf16[32,512]{1,0:T(8,128)(2,1)S(1)} %get-tuple-element.30), channel_id=1, source_target_pairs={{0,3},{1,2},{2,1},{3,0},{4,7},{5,6},{6,5},{7,4},{8,11},{9,10},{10,... | collective-permute-start | bytes 98312 | tf_op jit(solution)/shard_map/ppermute | solution.py:206
  63.1 1.4 %collective-permute-start.22 = (bf16[32,512]{1,0:T(8,128)(2,1)S(1)}, bf16[32,512]{1,0:T(8,128)(2,1)S(1)}, u32[]{:S(2)}, u32[]{:S(2)}) collective-permute-start(bf16[32,512]{1,0:T(8,128)(2,1)S(1)} %get-tuple-element.31), channel_id=1, source_target_pairs={{0,4},{1,5},{2,6},{3,7},{4,0},{5,1},{6,2},{7,3},{8,12},{9,13},{10,... | collective-permute-start | bytes 98312 | tf_op jit(solution)/shard_map/ppermute | solution.py:206
  64.5 0.3 collective-permute-start.23
  64.8 2.3 %collective-permute-start.24 = (bf16[32,512]{1,0:T(8,128)(2,1)S(1)}, bf16[32,512]{1,0:T(8,128)(2,1)S(1)}, u32[]{:S(2)}, u32[]{:S(2)}) collective-permute-start(bf16[32,512]{1,0:T(8,128)(2,1)S(1)} %get-tuple-element.33), channel_id=1, source_target_pairs={{0,6},{1,7},{2,4},{3,5},{4,2},{5,3},{6,0},{7,1},{8,14},{9,15},{10,... | collective-permute-start | bytes 98312 | tf_op jit(solution)/shard_map/ppermute | solution.py:206
  67.1 0.4 collective-permute-start.25
  67.5 1.5 %collective-permute-start.26 = (bf16[32,512]{1,0:T(8,128)(2,1)S(1)}, bf16[32,512]{1,0:T(8,128)(2,1)S(1)}, u32[]{:S(2)}, u32[]{:S(2)}) collective-permute-start(bf16[32,512]{1,0:T(8,128)(2,1)S(1)} %get-tuple-element.35), channel_id=1, source_target_pairs={{0,8},{1,9},{2,10},{3,11},{4,12},{5,13},{6,14},{7,15},{8,0},{9,1},... | collective-permute-start | bytes 98312 | tf_op jit(solution)/shard_map/ppermute | solution.py:206
  69.1 1.1 %collective-permute-start.27 = (bf16[32,512]{1,0:T(8,128)(2,1)S(1)}, bf16[32,512]{1,0:T(8,128)(2,1)S(1)}, u32[]{:S(2)}, u32[]{:S(2)}) collective-permute-start(bf16[32,512]{1,0:T(8,128)(2,1)S(1)} %get-tuple-element.36), channel_id=1, source_target_pairs={{0,9},{1,8},{2,11},{3,10},{4,13},{5,12},{6,15},{7,14},{8,1},{9,0},... | collective-permute-start | bytes 98312 | tf_op jit(solution)/shard_map/ppermute | solution.py:206
  70.2 2.3 %collective-permute-start.28 = (bf16[32,512]{1,0:T(8,128)(2,1)S(1)}, bf16[32,512]{1,0:T(8,128)(2,1)S(1)}, u32[]{:S(2)}, u32[]{:S(2)}) collective-permute-start(bf16[32,512]{1,0:T(8,128)(2,1)S(1)} %get-tuple-element.37), channel_id=1, source_target_pairs={{0,10},{1,11},{2,8},{3,9},{4,14},{5,15},{6,12},{7,13},{8,2},{9,3},... | collective-permute-start | bytes 98312 | tf_op jit(solution)/shard_map/ppermute | solution.py:206
  72.5 1.3 %collective-permute-start.29 = (bf16[32,512]{1,0:T(8,128)(2,1)S(1)}, bf16[32,512]{1,0:T(8,128)(2,1)S(1)}, u32[]{:S(2)}, u32[]{:S(2)}) collective-permute-start(bf16[32,512]{1,0:T(8,128)(2,1)S(1)} %get-tuple-element.38), channel_id=1, source_target_pairs={{0,11},{1,10},{2,9},{3,8},{4,15},{5,14},{6,13},{7,12},{8,3},{9,2},... | collective-permute-start | bytes 98312 | tf_op jit(solution)/shard_map/ppermute | solution.py:206
  73.8 1.9 %collective-permute-start.30 = (bf16[32,512]{1,0:T(8,128)(2,1)S(1)}, bf16[32,512]{1,0:T(8,128)(2,1)S(1)}, u32[]{:S(2)}, u32[]{:S(2)}) collective-permute-start(bf16[32,512]{1,0:T(8,128)(2,1)S(1)} %get-tuple-element.39), channel_id=1, source_target_pairs={{0,12},{1,13},{2,14},{3,15},{4,8},{5,9},{6,10},{7,11},{8,4},{9,5},... | collective-permute-start | bytes 98312 | tf_op jit(solution)/shard_map/ppermute | solution.py:206
  75.7 1.6 %collective-permute-start.31 = (bf16[32,512]{1,0:T(8,128)(2,1)S(1)}, bf16[32,512]{1,0:T(8,128)(2,1)S(1)}, u32[]{:S(2)}, u32[]{:S(2)}) collective-permute-start(bf16[32,512]{1,0:T(8,128)(2,1)S(1)} %get-tuple-element.40), channel_id=1, source_target_pairs={{0,13},{1,12},{2,15},{3,14},{4,9},{5,8},{6,11},{7,10},{8,5},{9,4},... | collective-permute-start | bytes 98312 | tf_op jit(solution)/shard_map/ppermute | solution.py:206
  77.3 2.2 %collective-permute-start.32 = (bf16[32,512]{1,0:T(8,128)(2,1)S(1)}, bf16[32,512]{1,0:T(8,128)(2,1)S(1)}, u32[]{:S(2)}, u32[]{:S(2)}) collective-permute-start(bf16[32,512]{1,0:T(8,128)(2,1)S(1)} %get-tuple-element.41), channel_id=1, source_target_pairs={{0,14},{1,15},{2,12},{3,13},{4,10},{5,11},{6,8},{7,9},{8,6},{9,7},... | collective-permute-start | bytes 98312 | tf_op jit(solution)/shard_map/ppermute | solution.py:206
  79.5 2.3 %collective-permute-start.33 = (bf16[32,512]{1,0:T(8,128)(2,1)S(1)}, bf16[32,512]{1,0:T(8,128)(2,1)S(1)}, u32[]{:S(2)}, u32[]{:S(2)}) collective-permute-start(bf16[32,512]{1,0:T(8,128)(2,1)S(1)} %get-tuple-element.42), channel_id=1, source_target_pairs={{0,15},{1,14},{2,13},{3,12},{4,11},{5,10},{6,9},{7,8},{8,7},{9,6},... | collective-permute-start | bytes 98312 | tf_op jit(solution)/shard_map/ppermute | solution.py:206
  81.8 0.6 add.3
  82.4 1.5 %collective-permute-done.32.refs_13_ = bf16[32,512]{1,0:T(8,128)(2,1)S(1)} collective-permute-done((bf16[32,512]{1,0:T(8,128)(2,1)S(1)}, bf16[32,512]{1,0:T(8,128)(2,1)S(1)}, u32[]{:S(2)}, u32[]{:S(2)}) %collective-permute-start.32) | collective-permute-done | bytes 32800 | tf_op jit(solution)/shard_map/ppermute | solution.py:206
  83.9 1.6 %collective-permute-done.33.refs_14_ = bf16[32,512]{1,0:T(8,128)(2,1)S(1)} collective-permute-done((bf16[32,512]{1,0:T(8,128)(2,1)S(1)}, bf16[32,512]{1,0:T(8,128)(2,1)S(1)}, u32[]{:S(2)}, u32[]{:S(2)}) %collective-permute-start.33) | collective-permute-done | bytes 32800 | tf_op jit(solution)/shard_map/ppermute | solution.py:206
  85.5 0.8 shard_map.98
  (50 shorter events, 0.2 us)
Async XLA Ops:
  0.6 6.6 %collective-permute-start = (bf16[32,512]{1,0:T(8,128)(2,1)}, bf16[32,512]{1,0:T(8,128)(2,1)S(1)}, u32[]{:S(2)}, u32[]{:S(2)}) collective-permute-start(bf16[32,512]{1,0:T(8,128)(2,1)} %param.8), channel_id=1, source_target_pairs={{0,8},{1,9},{2,10},{3,11},{4,12},{5,13},{6,14},{7,15},{8,0},{9,1},... | collective-permute-start | bytes 98312 | tf_op jit(solution)/shard_map/ppermute | solution.py:206
  8.0 4.3 %collective-permute-start.1 = (bf16[64,512]{1,0:T(8,128)(2,1)S(1)}, bf16[64,512]{1,0:T(8,128)(2,1)S(1)}, u32[]{:S(2)}, u32[]{:S(2)}) collective-permute-start(bf16[64,512]{1,0:T(8,128)(2,1)S(1)} %pad_maximum_fusion.2), channel_id=1, source_target_pairs={{0,4},{1,5},{2,6},{3,7},{4,0},{5,1},{6,2},{7,3},{8,12},{9,13},{10,... | collective-permute-start | bytes 196616 | tf_op jit(solution)/shard_map/ppermute | solution.py:206
  13.0 5.0 %collective-permute-start.2 = (bf16[128,512]{1,0:T(8,128)(2,1)S(1)}, bf16[128,512]{1,0:T(8,128)(2,1)S(1)}, u32[]{:S(2)}, u32[]{:S(2)}) collective-permute-start(bf16[128,512]{1,0:T(8,128)(2,1)S(1)} %pad_maximum_fusion.1), channel_id=1, source_target_pairs={{0,2},{1,3},{2,0},{3,1},{4,6},{5,7},{6,4},{7,5},{8,10},{9,11},{10,... | collective-permute-start | bytes 393224 | tf_op jit(solution)/shard_map/ppermute | solution.py:206
  18.8 3.9 %collective-permute-start.3 = (bf16[256,512]{1,0:T(8,128)(2,1)S(1)}, bf16[256,512]{1,0:T(8,128)(2,1)S(1)}, u32[]{:S(2)}, u32[]{:S(2)}) collective-permute-start(bf16[256,512]{1,0:T(8,128)(2,1)S(1)} %pad_maximum_fusion), channel_id=1, source_target_pairs={{0,1},{1,0},{2,3},{3,2},{4,5},{5,4},{6,7},{7,6},{8,9},{9,8},{10,11... | collective-permute-start | bytes 786440 | tf_op jit(solution)/shard_map/ppermute | solution.py:206
  18.9 1.9 %copy-start.2 = (bf16[512,3,1024]{2,0,1:T(8,128)(2,1)S(1)}, bf16[512,3,1024]{2,0,1:T(8,128)(2,1)}, u32[]{:S(2)}) copy-start(bf16[512,3,1024]{2,0,1:T(8,128)(2,1)} %param.9) | copy-start | bytes 9437188
  20.8 0.8 copy-start.3
  21.6 1.1 %copy-start.9 = (bf16[32,512]{1,0:T(8,128)(2,1)S(1)}, bf16[32,512]{1,0:T(8,128)(2,1)}, u32[]{:S(2)}) copy-start(bf16[32,512]{1,0:T(8,128)(2,1)} %param.8) | copy-start | bytes 98308
  21.6 1.3 %copy-start.5 = (f32[3,1024]{1,0:T(4,128)S(1)}, f32[3,1024]{1,0:T(4,128)}, u32[]{:S(2)}) copy-start(f32[3,1024]{1,0:T(4,128)} %quad_ref.1) | copy-start | bytes 36868
  21.6 1.3 %copy-start.6 = (f32[2,1024]{1,0:T(2,128)S(1)}, f32[2,1024]{1,0:T(2,128)}, u32[]{:S(2)}) copy-start(f32[2,1024]{1,0:T(2,128)} %lin_ref.1) | copy-start | bytes 24580
  21.6 1.3 %copy-start.7 = (f32[1024]{0:T(1024)S(1)}, f32[1024]{0:T(1024)}, u32[]{:S(2)}) copy-start(f32[1024]{0:T(1024)} %param.13) | copy-start | bytes 12292
  21.6 1.3 %copy-start.8 = (s32[1024]{0:T(1024)S(1)}, s32[1024]{0:T(1024)}, u32[]{:S(2)}) copy-start(s32[1024]{0:T(1024)} %param.14) | copy-start | bytes 12292
  22.9 32.5 %copy-start.4 = (f32[512]{0:T(512)S(1)}, f32[512]{0:T(512)}, u32[]{:S(2)}) copy-start(f32[512]{0:T(512)} %param.15) | copy-start | bytes 6148
  27.3 2.7 %copy-start = (f32[512,3072]{1,0:T(8,128)}, f32[512,3072]{1,0:T(8,128)S(1)}, u32[]{:S(2)}) copy-start(f32[512,3072]{1,0:T(8,128)S(1)} %get-tuple-element.23.s_ref) | copy-start | bytes 18874372
  29.9 8.8 %collective-permute-start.10 = (f32[2,512]{1,0:T(2,128)S(1)}, f32[2,512]{1,0:T(2,128)S(1)}, u32[]{:S(2)}, u32[]{:S(2)}) collective-permute-start(f32[2,512]{1,0:T(2,128)S(1)} %get-tuple-element.25.refs_0_), channel_id=1, source_target_pairs={{0,7},{1,6},{2,5},{3,4},{4,3},{5,2},{6,1},{7,0},{8,15},{9,14},{10,... | collective-permute-start | bytes 12296 | tf_op jit(solution)/shard_map/ppermute | solution.py:206
  32.6 8.7 %collective-permute-start.11 = (f32[2,512]{1,0:T(2,128)S(1)}, f32[2,512]{1,0:T(2,128)S(1)}, u32[]{:S(2)}, u32[]{:S(2)}) collective-permute-start(f32[2,512]{1,0:T(2,128)S(1)} %get-tuple-element.25.refs_0_), channel_id=1, source_target_pairs={{0,8},{1,9},{2,10},{3,11},{4,12},{5,13},{6,14},{7,15},{8,0},{9,1},... | collective-permute-start | bytes 12296 | tf_op jit(solution)/shard_map/ppermute | solution.py:206
  35.4 7.1 %collective-permute-start.12 = (f32[2,512]{1,0:T(2,128)S(1)}, f32[2,512]{1,0:T(2,128)S(1)}, u32[]{:S(2)}, u32[]{:S(2)}) collective-permute-start(f32[2,512]{1,0:T(2,128)S(1)} %get-tuple-element.25.refs_0_), channel_id=1, source_target_pairs={{0,9},{1,8},{2,11},{3,10},{4,13},{5,12},{6,15},{7,14},{8,1},{9,0},... | collective-permute-start | bytes 12296 | tf_op jit(solution)/shard_map/ppermute | solution.py:206
  35.4 9.2 %collective-permute-start.13 = (f32[2,512]{1,0:T(2,128)S(1)}, f32[2,512]{1,0:T(2,128)S(1)}, u32[]{:S(2)}, u32[]{:S(2)}) collective-permute-start(f32[2,512]{1,0:T(2,128)S(1)} %get-tuple-element.25.refs_0_), channel_id=1, source_target_pairs={{0,10},{1,11},{2,8},{3,9},{4,14},{5,15},{6,12},{7,13},{8,2},{9,3},... | collective-permute-start | bytes 12296 | tf_op jit(solution)/shard_map/ppermute | solution.py:206
  37.6 9.2 %collective-permute-start.14 = (f32[2,512]{1,0:T(2,128)S(1)}, f32[2,512]{1,0:T(2,128)S(1)}, u32[]{:S(2)}, u32[]{:S(2)}) collective-permute-start(f32[2,512]{1,0:T(2,128)S(1)} %get-tuple-element.25.refs_0_), channel_id=1, source_target_pairs={{0,11},{1,10},{2,9},{3,8},{4,15},{5,14},{6,13},{7,12},{8,3},{9,2},... | collective-permute-start | bytes 12296 | tf_op jit(solution)/shard_map/ppermute | solution.py:206
  38.7 8.6 %collective-permute-start.15 = (f32[2,512]{1,0:T(2,128)S(1)}, f32[2,512]{1,0:T(2,128)S(1)}, u32[]{:S(2)}, u32[]{:S(2)}) collective-permute-start(f32[2,512]{1,0:T(2,128)S(1)} %get-tuple-element.25.refs_0_), channel_id=1, source_target_pairs={{0,12},{1,13},{2,14},{3,15},{4,8},{5,9},{6,10},{7,11},{8,4},{9,5},... | collective-permute-start | bytes 12296 | tf_op jit(solution)/shard_map/ppermute | solution.py:206
  41.2 6.6 %collective-permute-start.16 = (f32[2,512]{1,0:T(2,128)S(1)}, f32[2,512]{1,0:T(2,128)S(1)}, u32[]{:S(2)}, u32[]{:S(2)}) collective-permute-start(f32[2,512]{1,0:T(2,128)S(1)} %get-tuple-element.25.refs_0_), channel_id=1, source_target_pairs={{0,13},{1,12},{2,15},{3,14},{4,9},{5,8},{6,11},{7,10},{8,5},{9,4},... | collective-permute-start | bytes 12296 | tf_op jit(solution)/shard_map/ppermute | solution.py:206
  42.5 6.3 %collective-permute-start.17 = (f32[2,512]{1,0:T(2,128)S(1)}, f32[2,512]{1,0:T(2,128)S(1)}, u32[]{:S(2)}, u32[]{:S(2)}) collective-permute-start(f32[2,512]{1,0:T(2,128)S(1)} %get-tuple-element.25.refs_0_), channel_id=1, source_target_pairs={{0,14},{1,15},{2,12},{3,13},{4,10},{5,11},{6,8},{7,9},{8,6},{9,7},... | collective-permute-start | bytes 12296 | tf_op jit(solution)/shard_map/ppermute | solution.py:206
  44.6 5.7 %collective-permute-start.18 = (f32[2,512]{1,0:T(2,128)S(1)}, f32[2,512]{1,0:T(2,128)S(1)}, u32[]{:S(2)}, u32[]{:S(2)}) collective-permute-start(f32[2,512]{1,0:T(2,128)S(1)} %get-tuple-element.25.refs_0_), channel_id=1, source_target_pairs={{0,15},{1,14},{2,13},{3,12},{4,11},{5,10},{6,9},{7,8},{8,7},{9,6},... | collective-permute-start | bytes 12296 | tf_op jit(solution)/shard_map/ppermute | solution.py:206
  46.8 4.1 %collective-permute-start.4 = (f32[2,512]{1,0:T(2,128)S(1)}, f32[2,512]{1,0:T(2,128)S(1)}, u32[]{:S(2)}, u32[]{:S(2)}) collective-permute-start(f32[2,512]{1,0:T(2,128)S(1)} %get-tuple-element.25.refs_0_), channel_id=1, source_target_pairs={{0,1},{1,0},{2,3},{3,2},{4,5},{5,4},{6,7},{7,6},{8,9},{9,8},{10,11... | collective-permute-start | bytes 12296 | tf_op jit(solution)/shard_map/ppermute | solution.py:206
  47.3 5.8 %collective-permute-start.5 = (f32[2,512]{1,0:T(2,128)S(1)}, f32[2,512]{1,0:T(2,128)S(1)}, u32[]{:S(2)}, u32[]{:S(2)}) collective-permute-start(f32[2,512]{1,0:T(2,128)S(1)} %get-tuple-element.25.refs_0_), channel_id=1, source_target_pairs={{0,2},{1,3},{2,0},{3,1},{4,6},{5,7},{6,4},{7,5},{8,10},{9,11},{10,... | collective-permute-start | bytes 12296 | tf_op jit(solution)/shard_map/ppermute | solution.py:206
  47.8 5.3 %collective-permute-start.6 = (f32[2,512]{1,0:T(2,128)S(1)}, f32[2,512]{1,0:T(2,128)S(1)}, u32[]{:S(2)}, u32[]{:S(2)}) collective-permute-start(f32[2,512]{1,0:T(2,128)S(1)} %get-tuple-element.25.refs_0_), channel_id=1, source_target_pairs={{0,3},{1,2},{2,1},{3,0},{4,7},{5,6},{6,5},{7,4},{8,11},{9,10},{10,... | collective-permute-start | bytes 12296 | tf_op jit(solution)/shard_map/ppermute | solution.py:206
  48.8 4.4 %collective-permute-start.7 = (f32[2,512]{1,0:T(2,128)S(1)}, f32[2,512]{1,0:T(2,128)S(1)}, u32[]{:S(2)}, u32[]{:S(2)}) collective-permute-start(f32[2,512]{1,0:T(2,128)S(1)} %get-tuple-element.25.refs_0_), channel_id=1, source_target_pairs={{0,4},{1,5},{2,6},{3,7},{4,0},{5,1},{6,2},{7,3},{8,12},{9,13},{10,... | collective-permute-start | bytes 12296 | tf_op jit(solution)/shard_map/ppermute | solution.py:206
  50.3 3.0 %collective-permute-start.8 = (f32[2,512]{1,0:T(2,128)S(1)}, f32[2,512]{1,0:T(2,128)S(1)}, u32[]{:S(2)}, u32[]{:S(2)}) collective-permute-start(f32[2,512]{1,0:T(2,128)S(1)} %get-tuple-element.25.refs_0_), channel_id=1, source_target_pairs={{0,5},{1,4},{2,7},{3,6},{4,1},{5,0},{6,3},{7,2},{8,13},{9,12},{10,... | collective-permute-start | bytes 12296 | tf_op jit(solution)/shard_map/ppermute | solution.py:206
  50.9 4.5 %collective-permute-start.9 = (f32[2,512]{1,0:T(2,128)S(1)}, f32[2,512]{1,0:T(2,128)S(1)}, u32[]{:S(2)}, u32[]{:S(2)}) collective-permute-start(f32[2,512]{1,0:T(2,128)S(1)} %get-tuple-element.25.refs_0_), channel_id=1, source_target_pairs={{0,6},{1,7},{2,4},{3,5},{4,2},{5,3},{6,0},{7,1},{8,14},{9,15},{10,... | collective-permute-start | bytes 12296 | tf_op jit(solution)/shard_map/ppermute | solution.py:206
  55.4 2.8 %copy-start.1 = (f32[512,3072]{1,0:T(8,128)S(1)}, f32[512,3072]{1,0:T(8,128)}, u32[]{:S(2)}) copy-start(f32[512,3072]{1,0:T(8,128)} %copy-done) | copy-start | bytes 18874372
  59.7 4.8 %collective-permute-start.34 = (f32[6,1024]{1,0:T(8,128)S(1)}, f32[6,1024]{1,0:T(8,128)S(1)}, u32[]{:S(2)}, u32[]{:S(2)}) collective-permute-start(f32[6,1024]{1,0:T(8,128)S(1)} %get-tuple-element.43), channel_id=1, source_target_pairs={{0,16},{16,0},{1,17},{17,1},{2,18},{18,2},{3,19},{19,3},{4,20},{20... | collective-permute-start | bytes 73736 | tf_op jit(solution)/shard_map/ppermute | solution.py:206
  61.3 3.5 %collective-permute-start.19 = (bf16[32,512]{1,0:T(8,128)(2,1)S(1)}, bf16[32,512]{1,0:T(8,128)(2,1)S(1)}, u32[]{:S(2)}, u32[]{:S(2)}) collective-permute-start(bf16[32,512]{1,0:T(8,128)(2,1)S(1)} %get-tuple-element.28), channel_id=1, source_target_pairs={{0,1},{1,0},{2,3},{3,2},{4,5},{5,4},{6,7},{7,6},{8,9},{9,8},{10,11... | collective-permute-start | bytes 98312 | tf_op jit(solution)/shard_map/ppermute | solution.py:206
  61.3 5.8 %collective-permute-start.20 = (bf16[32,512]{1,0:T(8,128)(2,1)S(1)}, bf16[32,512]{1,0:T(8,128)(2,1)S(1)}, u32[]{:S(2)}, u32[]{:S(2)}) collective-permute-start(bf16[32,512]{1,0:T(8,128)(2,1)S(1)} %get-tuple-element.29), channel_id=1, source_target_pairs={{0,2},{1,3},{2,0},{3,1},{4,6},{5,7},{6,4},{7,5},{8,10},{9,11},{10,... | collective-permute-start | bytes 98312 | tf_op jit(solution)/shard_map/ppermute | solution.py:206
  62.0 5.5 %collective-permute-start.21 = (bf16[32,512]{1,0:T(8,128)(2,1)S(1)}, bf16[32,512]{1,0:T(8,128)(2,1)S(1)}, u32[]{:S(2)}, u32[]{:S(2)}) collective-permute-start(bf16[32,512]{1,0:T(8,128)(2,1)S(1)} %get-tuple-element.30), channel_id=1, source_target_pairs={{0,3},{1,2},{2,1},{3,0},{4,7},{5,6},{6,5},{7,4},{8,11},{9,10},{10,... | collective-permute-start | bytes 98312 | tf_op jit(solution)/shard_map/ppermute | solution.py:206
  63.1 5.9 %collective-permute-start.22 = (bf16[32,512]{1,0:T(8,128)(2,1)S(1)}, bf16[32,512]{1,0:T(8,128)(2,1)S(1)}, u32[]{:S(2)}, u32[]{:S(2)}) collective-permute-start(bf16[32,512]{1,0:T(8,128)(2,1)S(1)} %get-tuple-element.31), channel_id=1, source_target_pairs={{0,4},{1,5},{2,6},{3,7},{4,0},{5,1},{6,2},{7,3},{8,12},{9,13},{10,... | collective-permute-start | bytes 98312 | tf_op jit(solution)/shard_map/ppermute | solution.py:206
  64.5 5.7 %collective-permute-start.23 = (bf16[32,512]{1,0:T(8,128)(2,1)S(1)}, bf16[32,512]{1,0:T(8,128)(2,1)S(1)}, u32[]{:S(2)}, u32[]{:S(2)}) collective-permute-start(bf16[32,512]{1,0:T(8,128)(2,1)S(1)} %get-tuple-element.32), channel_id=1, source_target_pairs={{0,5},{1,4},{2,7},{3,6},{4,1},{5,0},{6,3},{7,2},{8,13},{9,12},{10,... | collective-permute-start | bytes 98312 | tf_op jit(solution)/shard_map/ppermute | solution.py:206
  64.8 7.7 %collective-permute-start.24 = (bf16[32,512]{1,0:T(8,128)(2,1)S(1)}, bf16[32,512]{1,0:T(8,128)(2,1)S(1)}, u32[]{:S(2)}, u32[]{:S(2)}) collective-permute-start(bf16[32,512]{1,0:T(8,128)(2,1)S(1)} %get-tuple-element.33), channel_id=1, source_target_pairs={{0,6},{1,7},{2,4},{3,5},{4,2},{5,3},{6,0},{7,1},{8,14},{9,15},{10,... | collective-permute-start | bytes 98312 | tf_op jit(solution)/shard_map/ppermute | solution.py:206
  67.1 6.7 %collective-permute-start.25 = (bf16[32,512]{1,0:T(8,128)(2,1)S(1)}, bf16[32,512]{1,0:T(8,128)(2,1)S(1)}, u32[]{:S(2)}, u32[]{:S(2)}) collective-permute-start(bf16[32,512]{1,0:T(8,128)(2,1)S(1)} %get-tuple-element.34), channel_id=1, source_target_pairs={{0,7},{1,6},{2,5},{3,4},{4,3},{5,2},{6,1},{7,0},{8,15},{9,14},{10,... | collective-permute-start | bytes 98312 | tf_op jit(solution)/shard_map/ppermute | solution.py:206
  67.5 8.2 %collective-permute-start.26 = (bf16[32,512]{1,0:T(8,128)(2,1)S(1)}, bf16[32,512]{1,0:T(8,128)(2,1)S(1)}, u32[]{:S(2)}, u32[]{:S(2)}) collective-permute-start(bf16[32,512]{1,0:T(8,128)(2,1)S(1)} %get-tuple-element.35), channel_id=1, source_target_pairs={{0,8},{1,9},{2,10},{3,11},{4,12},{5,13},{6,14},{7,15},{8,0},{9,1},... | collective-permute-start | bytes 98312 | tf_op jit(solution)/shard_map/ppermute | solution.py:206
  69.1 8.2 %collective-permute-start.27 = (bf16[32,512]{1,0:T(8,128)(2,1)S(1)}, bf16[32,512]{1,0:T(8,128)(2,1)S(1)}, u32[]{:S(2)}, u32[]{:S(2)}) collective-permute-start(bf16[32,512]{1,0:T(8,128)(2,1)S(1)} %get-tuple-element.36), channel_id=1, source_target_pairs={{0,9},{1,8},{2,11},{3,10},{4,13},{5,12},{6,15},{7,14},{8,1},{9,0},... | collective-permute-start | bytes 98312 | tf_op jit(solution)/shard_map/ppermute | solution.py:206
  70.2 9.3 %collective-permute-start.28 = (bf16[32,512]{1,0:T(8,128)(2,1)S(1)}, bf16[32,512]{1,0:T(8,128)(2,1)S(1)}, u32[]{:S(2)}, u32[]{:S(2)}) collective-permute-start(bf16[32,512]{1,0:T(8,128)(2,1)S(1)} %get-tuple-element.37), channel_id=1, source_target_pairs={{0,10},{1,11},{2,8},{3,9},{4,14},{5,15},{6,12},{7,13},{8,2},{9,3},... | collective-permute-start | bytes 98312 | tf_op jit(solution)/shard_map/ppermute | solution.py:206
  72.5 9.9 %collective-permute-start.29 = (bf16[32,512]{1,0:T(8,128)(2,1)S(1)}, bf16[32,512]{1,0:T(8,128)(2,1)S(1)}, u32[]{:S(2)}, u32[]{:S(2)}) collective-permute-start(bf16[32,512]{1,0:T(8,128)(2,1)S(1)} %get-tuple-element.38), channel_id=1, source_target_pairs={{0,11},{1,10},{2,9},{3,8},{4,15},{5,14},{6,13},{7,12},{8,3},{9,2},... | collective-permute-start | bytes 98312 | tf_op jit(solution)/shard_map/ppermute | solution.py:206
  73.8 8.6 %collective-permute-start.30 = (bf16[32,512]{1,0:T(8,128)(2,1)S(1)}, bf16[32,512]{1,0:T(8,128)(2,1)S(1)}, u32[]{:S(2)}, u32[]{:S(2)}) collective-permute-start(bf16[32,512]{1,0:T(8,128)(2,1)S(1)} %get-tuple-element.39), channel_id=1, source_target_pairs={{0,12},{1,13},{2,14},{3,15},{4,8},{5,9},{6,10},{7,11},{8,4},{9,5},... | collective-permute-start | bytes 98312 | tf_op jit(solution)/shard_map/ppermute | solution.py:206
  75.7 6.7 %collective-permute-start.31 = (bf16[32,512]{1,0:T(8,128)(2,1)S(1)}, bf16[32,512]{1,0:T(8,128)(2,1)S(1)}, u32[]{:S(2)}, u32[]{:S(2)}) collective-permute-start(bf16[32,512]{1,0:T(8,128)(2,1)S(1)} %get-tuple-element.40), channel_id=1, source_target_pairs={{0,13},{1,12},{2,15},{3,14},{4,9},{5,8},{6,11},{7,10},{8,5},{9,4},... | collective-permute-start | bytes 98312 | tf_op jit(solution)/shard_map/ppermute | solution.py:206
  77.3 6.6 %collective-permute-start.32 = (bf16[32,512]{1,0:T(8,128)(2,1)S(1)}, bf16[32,512]{1,0:T(8,128)(2,1)S(1)}, u32[]{:S(2)}, u32[]{:S(2)}) collective-permute-start(bf16[32,512]{1,0:T(8,128)(2,1)S(1)} %get-tuple-element.41), channel_id=1, source_target_pairs={{0,14},{1,15},{2,12},{3,13},{4,10},{5,11},{6,8},{7,9},{8,6},{9,7},... | collective-permute-start | bytes 98312 | tf_op jit(solution)/shard_map/ppermute | solution.py:206
  79.5 6.0 %collective-permute-start.33 = (bf16[32,512]{1,0:T(8,128)(2,1)S(1)}, bf16[32,512]{1,0:T(8,128)(2,1)S(1)}, u32[]{:S(2)}, u32[]{:S(2)}) collective-permute-start(bf16[32,512]{1,0:T(8,128)(2,1)S(1)} %get-tuple-element.42), channel_id=1, source_target_pairs={{0,15},{1,14},{2,13},{3,12},{4,11},{5,10},{6,9},{7,8},{8,7},{9,6},... | collective-permute-start | bytes 98312 | tf_op jit(solution)/shard_map/ppermute | solution.py:206

commit v2 on v1

--- a/solution.py
+++ b/solution.py
@@ -54,13 +54,9 @@
             out_ref[:, at : at + span] = value
 
 
-def main_kernel(n, a_ref, f_ref, lin_ref, quad_ref, cross_ref, ply_ref, *refs):
-    own_ref = refs[0]
-    send_refs = refs[1:n]
-    stat_ref, s_ref, w_ref, idx, d, acc = refs[n:]
+def main_kernel(n, a_ref, f_ref, lin_ref, quad_ref, cross_ref, ply_ref, part_ref, stat_ref, s_ref, w_ref, idx, d, acc):
     cases = a_ref.shape[0]
     width = lin_ref.shape[1]
-    rows = cases // n
     tile = 32
     peak = jnp.full((cases, 128), -jnp.inf, jnp.float32)
     for jb in range(width // JB):
@@ -119,52 +115,37 @@
         )
         if jb == 0:
             acc[...] = part
+        elif jb < width // JB - 1:
+            acc[...] += part
         else:
-            acc[...] += part
+            part_ref[...] = (acc[...] + part).astype(jnp.bfloat16)
     total = jnp.sum(total, axis=1, keepdims=True)
-    stat_ref[0:1, :] = to_lanes(peak, cases)
-    stat_ref[1:2, :] = to_lanes(total, cases)
-    own_ref[...] = acc[0:rows, :]
-    for p in range(1, n):
-        send_refs[p - 1][...] = acc[p * rows : (p + 1) * rows, :].astype(jnp.bfloat16)
-
-
-def swap_lanes(x, which, rows, n):
-    lane = lax.broadcasted_iota(jnp.int32, x.shape, 1)
-    bit = 1
-    while bit < n:
-        step = bit * rows
-        ahead = jnp.concatenate([x[:, step:], x[:, :step]], axis=1)
-        behind = jnp.concatenate([x[:, -step:], x[:, :-step]], axis=1)
-        other = jnp.where((lane & step) != 0, behind, ahead)
-        x = jnp.where((which & bit) != 0, other, x)
-        bit *= 2
-    return x
-
-
-def coef_kernel(n, me_ref, cot_ref, s_ref, w_ref, *refs):
-    stat_refs = refs[:n]
-    coef_ref, gain_ref, peaks, totals = refs[n:]
+    both = jnp.concatenate([to_lanes(peak, cases), to_lanes(total, cases)], axis=0)
+    for s in range(n):
+        stat_ref[s] = both
+
+
+def coef_kernel(n, me_ref, cot_ref, s_ref, w_ref, stat_ref, coef_ref, gain_ref, peaks, totals, turned):
     cases = cot_ref.shape[1]
     width = w_ref.shape[1]
     rows = cases // n
     for p in range(n):
-        peaks[p : p + 1, :] = stat_refs[p][0:1, :]
-        totals[p : p + 1, :] = stat_refs[p][1:2, :]
-    which = lax.broadcasted_iota(jnp.int32, (n, cases), 0)
-    peak_all = swap_lanes(peaks[...], which, rows, n)
-    total_all = swap_lanes(totals[...], which, rows, n)
-    mine = jnp.full((8, cases), me_ref[0], jnp.int32)
-    cot = swap_lanes(jnp.broadcast_to(cot_ref[...], (8, cases)), mine, rows, n)[0:1]
+        peaks[p : p + 1, :] = stat_ref[p, 0:1, :]
+        totals[p : p + 1, :] = stat_ref[p, 1:2, :]
+    peak_all = peaks[...]
     peak = jnp.max(peak_all, axis=0, keepdims=True)
-    total = jnp.sum(total_all * jnp.exp(peak_all - peak), axis=0, keepdims=True)
+    total = jnp.sum(totals[...] * jnp.exp(peak_all - peak), axis=0, keepdims=True)
     envelope = peak + jnp.log(total)
-    gain = cot * jnp.exp(peak_all - envelope)
-    square = gain[:, 0:128]
-    if n < 128:
-        square = jnp.concatenate([square, jnp.zeros((128 - n, 128), jnp.float32)], axis=0)
-    gain_ref[...] = jnp.transpose(square)[0:rows]
-    mine = gain[0:1]
+    gain = cot_ref[...] * jnp.exp(peak_all - envelope)
+    peaks[...] = gain
+    for at in range(0, cases, 128):
+        square = gain[:, at : at + 128]
+        if n < 128:
+            square = jnp.concatenate([square, jnp.zeros((128 - n, 128), jnp.float32)], axis=0)
+        turned[at : at + 128, :] = jnp.transpose(square)
+    me = me_ref[0]
+    gain_ref[...] = turned[pl.ds(pl.multiple_of(me * rows, rows), rows), :]
+    mine = peaks[pl.ds(me, 1), :]
     scales = [to_rows(mine, at) for at in range(0, cases, 128)]
     for jb in range(width // JB):
         base = jb * 3 * JB
@@ -187,11 +168,11 @@
                 coef_ref[i : i + 1, jb * JB + c : jb * JB + c + 128] = line
 
 
-def combine_kernel(n, gain_ref, own_ref, *refs):
-    out_ref = refs[-1]
-    value = own_ref[...] * gain_ref[:, 0:1]
+def combine_kernel(n, gain_ref, part_ref, out_ref):
+    rows = out_ref.shape[0]
+    value = part_ref[0].astype(jnp.float32) * gain_ref[:, 0:1]
     for p in range(1, n):
-        value = value + refs[p - 1][...].astype(jnp.float32) * gain_ref[:, p : p + 1]
+        value = value + part_ref[p].astype(jnp.float32) * gain_ref[:, p : p + 1]
     out_ref[...] = value
 
 
@@ -202,20 +183,8 @@
     f32, bf16 = jnp.float32, jnp.bfloat16
     shape = jax.ShapeDtypeStruct
 
-    def swap(x, axis, size, p):
-        return lax.ppermute(x, axis, [(i, i ^ p) for i in range(size)])
-
-    gathered = load_coef
-    bit = n // 2
-    order = [0]
-    while bit:
-        gathered = jnp.concatenate([gathered, swap(gathered, "elem", n, bit)], axis=0)
-        order = order + [p ^ bit for p in order]
-        bit //= 2
-    place = {p: i for i, p in enumerate(order)}
-    gathered = jnp.concatenate(
-        [lax.slice_in_dim(gathered, place[p] * rows, place[p] * rows + rows) for p in range(n)]
-    )
+    copies = jnp.broadcast_to(load_coef[None], (n, rows, units))
+    gathered = lax.all_to_all(copies, "elem", 0, 0).reshape(cases, units)
 
     fields = vmem_call(
         prep_kernel,
@@ -225,11 +194,14 @@
         n_in=2,
     )(jnp.transpose(mantissa, (1, 0, 2)), jnp.transpose(scale_exp, (1, 2, 0)))
 
-    outs = vmem_call(
+    part, stat, stress, weight = vmem_call(
         functools.partial(main_kernel, n),
-        [shape((rows, units), f32)]
-        + [shape((rows, units), bf16)] * (n - 1)
-        + [shape((2, cases), f32), shape((cases, comps * width), f32), shape((cases, width), f32)],
+        [
+            shape((cases, units), bf16),
+            shape((n, 2, cases), f32),
+            shape((cases, comps * width), f32),
+            shape((cases, width), f32),
+        ],
         scratch_shapes=[
             VMEM((cases, width), f32),
             VMEM((cases, comps * width), bf16),
@@ -240,24 +212,23 @@
         exps=cases * width,
         n_in=6,
     )(gathered, fields, lin_coef, quad_coef, cross_coef.reshape(1, width), ply_count.reshape(1, width))
-    own, sends, stat, stress, weight = outs[0], outs[1:n], outs[n], outs[n + 1], outs[n + 2]
-
-    stats = [stat] + [swap(stat, "elem", n, p) for p in range(1, n)]
-    parts = [swap(sends[p - 1], "elem", n, p) for p in range(1, n)]
+
+    stats = lax.all_to_all(stat, "elem", 0, 0)
+    parts = lax.all_to_all(part.reshape(n, rows, units), "elem", 0, 0)
 
     me = lax.axis_index("elem").astype(jnp.int32).reshape(1)
     coef, gain = vmem_call(
         functools.partial(coef_kernel, n),
         [shape((6, width), f32), shape((rows, 128), f32)],
-        scratch_shapes=[VMEM((n, cases), f32), VMEM((n, cases), f32)],
+        scratch_shapes=[VMEM((n, cases), f32), VMEM((n, cases), f32), VMEM((cases, 128), f32)],
         flops=14 * cases * width,
         nbytes=16 * cases * width,
-        n_in=4 + n,
+        n_in=5,
         smem=(0,),
-    )(me, cotangent.reshape(1, cases), stress, weight, *stats)
+    )(me, cotangent.reshape(1, cases), stress, weight, stats)
     bit = 1
     while bit < n_case:
-        coef = coef + swap(coef, "case", n_case, bit)
+        coef = coef + lax.ppermute(coef, "case", [(i, i ^ bit) for i in range(n_case)])
         bit *= 2
 
     load_grad = vmem_call(
@@ -265,8 +236,8 @@
         shape((rows, units), f32),
         flops=2 * n * rows * units,
         nbytes=2 * n * rows * units,
-        n_in=1 + n,
-    )(gain, own, *parts)
+        n_in=2,
+    )(gain, parts)
     return (load_grad, coef)
 
 

time: 86.8 us -> 64.4 us (0.74)
  starting transfers between devices: 51.2 us -> 12.6 us
  blocking collectives: 0 us -> 10.8 us
  local copies, waits for them, and re-layouts: 8.25 us -> 13.5 us
  other arithmetic: 2.92 us -> 0.62 us
  waiting for transfers between devices: 15.3 us -> 17.3 us
    ppermute x35 -> x1, starting transfers between devices: 51.2 us -> 1.55 us  [per_device(): lax.ppermute(coef, 'case', [(i, i ^ bit) for i in range(n_case)])]
    all_to_all x0 -> x2, waiting for transfers between devices: none -> 14.8 us  [the longest x1 10.8 us: per_device(): gathered = lax.all_to_all(copies, 'elem', 0, 0).reshape(cases, units)]
    ppermute x35 -> x1, waiting for transfers between devices: 15.3 us -> 2.42 us  [per_device(): lax.ppermute(coef, 'case', [(i, i ^ bit) for i in range(n_case)])]
    all_to_all x0 -> x2, starting transfers between devices: none -> 11 us  [the longest x1 7.44 us: per_device(): gathered = lax.all_to_all(copies, 'elem', 0, 0).reshape(cases, units)]
    all_to_all x0 -> x1, blocking collectives: none -> 10.8 us  [per_device(): stats = lax.all_to_all(stat, 'elem', 0, 0)]
    unnamed x35 -> x24, local copies, waits for them, and re-layouts: 8.24 us -> 11.9 us
    concatenate x3 -> x0, other arithmetic: 2.3 us -> none  [per_device(): jnp.concatenate([gathered, swap(gathered, 'elem', n, bit)], axis=0)]
    broadcast_in_dim x0 -> x1, local copies, waits for them, and re-layouts: none -> 1.61 us  [per_device(): copies = jnp.broadcast_to(load_coef[None], (n, rows, units))]
  transfers between devices with their start and end apart: 35 -> 3, of which waited for: 8 -> 3; matrix products, arithmetic and copies ran while one was open for 1% -> 1% of each run, Pallas kernels for 1% -> 4%
where the time goes in v2:
time: 64.4 us; the launch traced here: 63.7 us
  waiting for transfers between devices  17.3 us (27%)
  local copies, waits for them, and re-layouts  13.5 us (21%)
  starting transfers between devices  12.6 us (20%)
  blocking collectives  10.8 us (17%)
  Pallas kernels  8.24 us (13%)
  between operations  0.73 us (1%)
    unnamed x24, local copies, waits for them, and re-layouts  11.9 us
    all_to_all x1, blocking collectives, per_device(): stats = lax.all_to_all(stat, 'elem', 0, 0)  10.8 us
    all_to_all x1, waiting for transfers between devices, per_device(): gathered = lax.all_to_all(copies, 'elem', 0, 0).reshape(cases, units)  10.8 us
    all_to_all x1, starting transfers between devices, per_device(): gathered = lax.all_to_all(copies, 'elem', 0, 0).reshape(cases, units)  7.44 us
    pallas_call x1, Pallas kernels, per_device(): vmem_call(functools.partial(main_kernel, n), [shape((cases, units), bf16)...  5.04 us
    all_to_all x1, waiting for transfers between devices, per_device(): parts = lax.all_to_all(part.reshape(n, rows, units), 'elem', 0, 0)  4.08 us
    all_to_all x1, starting transfers between devices, per_device(): parts = lax.all_to_all(part.reshape(n, rows, units), 'elem', 0, 0)  3.57 us
    ppermute x1, waiting for transfers between devices, per_device(): lax.ppermute(coef, 'case', [(i, i ^ bit) for i in range(n_case)])  2.42 us
  transfers between devices with their start and end apart: 3, of which 3 were waited for; matrix products, arithmetic and copies ran while one was open for 1% of the time, Pallas kernels for 4%

profile of v2, /device:TPU:0, one launch (start us, length us, event | category | flops | bytes accessed | tf_op | source)
XLA Modules:
  0.0 63.7 jit_solution(16687768643162072201)
XLA Ops:
  0.6 1.6 %broadcast_in_dim.2 = bf16[16,32,512]{2,1,0:T(8,128)(2,1)} broadcast(bf16[32,512]{1,0:T(8,128)(2,1)} %param.8), dimensions={1,2} | broadcast | bytes 557056 | tf_op jit(solution)/shard_map/broadcast_in_dim | solution.py:186
  2.2 7.4 %all-to-all-start = ((bf16[16,32,512]{2,1,0:T(8,128)(2,1)}), bf16[16,32,512]{2,1,0:T(8,128)(2,1)}, u32[]{:S(2)}, u32[]{:S(2)}) async-start(bf16[16,32,512]{2,1,0:T(8,128)(2,1)} %broadcast_in_dim.2), calls=%async_computation | async-start | bytes 1048576 | tf_op jit(solution)/shard_map/all_to_all | solution.py:187
  9.7 0.0 copy-start.2
  9.7 1.9 %copy-done.2 = bf16[512,3,1024]{2,0,1:T(8,128)(2,1)S(1)} copy-done((bf16[512,3,1024]{2,0,1:T(8,128)(2,1)S(1)}, bf16[512,3,1024]{2,0,1:T(8,128)(2,1)}, u32[]{:S(2)}) %copy-start.2) | copy-done | bytes 3145752
  11.6 0.0 copy-start.6
  11.6 0.8 %copy-done.6 = s32[512,3,8]{0,2,1:T(8,128)S(1)} copy-done((s32[512,3,8]{0,2,1:T(8,128)S(1)}, s32[512,3,8]{0,2,1:T(8,128)}, u32[]{:S(2)}) %copy-start.6) | copy-done | bytes 49176
  12.4 0.0 copy-start.8
  12.4 0.0 copy-start.9
  12.4 0.0 copy-start.10
  12.4 0.0 copy-start.11
  12.4 1.1 %shard_map.95.f_ref = bf16[512,3072]{1,0:T(8,128)(2,1)S(1)} custom-call(bf16[3,512,1024]{2,1,0:T(8,128)(2,1)S(1)} %bitcast.8, s32[3,8,512]{2,1,0:T(8,128)S(1)} %bitcast.10), custom_call_target="tpu_custom_call" | custom-call | flops 1572864 | bytes 6291456 | tf_op jit(solution)/shard_map/pallas_call | solution.py:189
  13.4 10.8 %all-to-all-done = bf16[16,32,512]{2,1,0:T(8,128)(2,1)} async-done(((bf16[16,32,512]{2,1,0:T(8,128)(2,1)}), bf16[16,32,512]{2,1,0:T(8,128)(2,1)}, u32[]{:S(2)}, u32[]{:S(2)}) %all-to-all-start) | async-done | bytes 524320 | tf_op jit(solution)/shard_map/all_to_all | solution.py:187
  24.2 0.0 copy-done.8
  24.2 0.0 copy-done.9
  24.2 0.0 copy-done.10
  24.2 0.0 copy-done.11
  24.2 0.0 copy-start.7
  24.2 5.0 %shard_map.96 = (bf16[512,512]{1,0:T(8,128)(2,1)S(1)}, f32[16,2,512]{2,1,0:T(2,128)S(1)}, f32[512,3072]{1,0:T(8,128)S(1)}, f32[512,1024]{1,0:T(8,128)S(1)}) custom-call(bf16[512,512]{1,0:T(8,128)(2,1)} %bitcast.2.a_ref, bf16[512,3072]{1,0:T(8,128)(2,1)S(1)} %shard_map.95.f_ref, f32[2,1024]{1,0:T(2,128)S(1)} %copy-done.9, f32[3,1024]{1,0:T(4,128)S(1)} %copy-done.8, ...), custom_call_target="tpu_custom_call" | custom-call | flops 3221225472 | bytes 11534336 | tf_op jit(solution)/shard_map/pallas_call | solution.py:197
  29.3 0.0 copy-start
  29.3 2.6 %copy-done = f32[512,3072]{1,0:T(8,128)} copy-done((f32[512,3072]{1,0:T(8,128)}, f32[512,3072]{1,0:T(8,128)S(1)}, u32[]{:S(2)}) %copy-start) | copy-done | bytes 6291480
  31.9 0.0 copy-start.3
  31.9 1.4 %copy-done.3 = f32[512,1024]{1,0:T(8,128)} copy-done((f32[512,1024]{1,0:T(8,128)}, f32[512,1024]{1,0:T(8,128)S(1)}, u32[]{:S(2)}) %copy-start.3) | copy-done | bytes 2097176
  33.3 0.0 copy-start.5
  33.3 0.8 %copy-done.5 = bf16[512,512]{1,0:T(8,128)(2,1)} copy-done((bf16[512,512]{1,0:T(8,128)(2,1)}, bf16[512,512]{1,0:T(8,128)(2,1)S(1)}, u32[]{:S(2)}) %copy-start.5) | copy-done | bytes 524312
  34.1 10.8 %all_to_all.15.stat_ref = f32[16,2,512]{2,1,0:T(2,128)S(1)} all-to-all(f32[16,2,512]{2,1,0:T(2,128)S(1)} %get-tuple-element.10), channel_id=1, replica_groups=mesh['case'=2,'elem'=16] {'elem'}, dimensions={0} | all-to-all | bytes 131072 | tf_op jit(solution)/shard_map/all_to_all | solution.py:216
  44.9 3.6 %all-to-all-start.2 = ((bf16[16,32,512]{2,1,0:T(8,128)(2,1)}), bf16[16,32,512]{2,1,0:T(8,128)(2,1)S(1)}, u32[]{:S(2)}, u32[]{:S(2)}) async-start(bf16[16,32,512]{2,1,0:T(8,128)(2,1)} %bitcast.9), calls=%async_computation.2 | async-start | bytes 1048576 | tf_op jit(solution)/shard_map/all_to_all | solution.py:217
  48.5 0.0 copy-done.7
  48.5 0.0 copy-start.1
  48.5 2.8 %copy-done.1 = f32[512,3072]{1,0:T(8,128)S(1)} copy-done((f32[512,3072]{1,0:T(8,128)S(1)}, f32[512,3072]{1,0:T(8,128)}, u32[]{:S(2)}) %copy-start.1) | copy-done | bytes 6291480
  51.3 0.0 copy-start.4
  51.3 1.6 %copy-done.4 = f32[512,1024]{1,0:T(8,128)S(1)} copy-done((f32[512,1024]{1,0:T(8,128)S(1)}, f32[512,1024]{1,0:T(8,128)}, u32[]{:S(2)}) %copy-start.4) | copy-done | bytes 2097176
  52.9 1.3 %shard_map.97 = (f32[6,1024]{1,0:T(8,128)S(1)}, f32[32,128]{1,0:T(8,128)S(1)}) custom-call(s32[1]{0:T(128)} %bitcast.me_ref, f32[1,512]{1,0:T(1,128)S(1)} %bitcast.11, f32[512,3072]{1,0:T(8,128)S(1)} %copy-done.1, f32[512,1024]{1,0:T(8,128)S(1)} %copy-done.4, f32[16,2,512]{2,1,0:T(2,128)S(1)} %all_to_all.15.stat_ref), custom_call_target="tpu_custom_call" | custom-call | flops 7340032 | bytes 8388608 | tf_op jit(solution)/shard_map/pallas_call | solution.py:220
  54.3 1.6 %collective-permute-start = (f32[6,1024]{1,0:T(8,128)S(1)}, f32[6,1024]{1,0:T(8,128)S(1)}, u32[]{:S(2)}, u32[]{:S(2)}) collective-permute-start(f32[6,1024]{1,0:T(8,128)S(1)} %get-tuple-element.13), channel_id=1, source_target_pairs={{0,16},{16,0},{1,17},{17,1},{2,18},{18,2},{3,19},{19,3},{4,20},{20... | collective-permute-start | bytes 73736 | tf_op jit(solution)/shard_map/ppermute | solution.py:231
  55.8 2.4 %collective-permute-done = f32[6,1024]{1,0:T(8,128)S(1)} collective-permute-done((f32[6,1024]{1,0:T(8,128)S(1)}, f32[6,1024]{1,0:T(8,128)S(1)}, u32[]{:S(2)}, u32[]{:S(2)}) %collective-permute-start) | collective-permute-done | bytes 24608 | tf_op jit(solution)/shard_map/ppermute | solution.py:231
  58.2 0.6 add.3
  58.9 4.1 %all-to-all-done.2.part_ref = bf16[16,32,512]{2,1,0:T(8,128)(2,1)S(1)} async-done(((bf16[16,32,512]{2,1,0:T(8,128)(2,1)}), bf16[16,32,512]{2,1,0:T(8,128)(2,1)S(1)}, u32[]{:S(2)}, u32[]{:S(2)}) %all-to-all-start.2) | async-done | bytes 524320 | tf_op jit(solution)/shard_map/all_to_all | solution.py:217
  62.9 0.8 %shard_map.98 = f32[32,512]{1,0:T(8,128)} custom-call(f32[32,128]{1,0:T(8,128)S(1)} %get-tuple-element.11.gain_ref, bf16[16,32,512]{2,1,0:T(8,128)(2,1)S(1)} %all-to-all-done.2.part_ref), custom_call_target="tpu_custom_call" | custom-call | flops 524288 | bytes 524288 | tf_op jit(solution)/shard_map/pallas_call | solution.py:234
Async XLA Ops:
  2.2 22.0 %all-to-all-start = ((bf16[16,32,512]{2,1,0:T(8,128)(2,1)}), bf16[16,32,512]{2,1,0:T(8,128)(2,1)}, u32[]{:S(2)}, u32[]{:S(2)}) async-start(bf16[16,32,512]{2,1,0:T(8,128)(2,1)} %broadcast_in_dim.2), calls=%async_computation | async-start | bytes 1048576 | tf_op jit(solution)/shard_map/all_to_all | solution.py:187
  9.7 1.9 %copy-start.2 = (bf16[512,3,1024]{2,0,1:T(8,128)(2,1)S(1)}, bf16[512,3,1024]{2,0,1:T(8,128)(2,1)}, u32[]{:S(2)}) copy-start(bf16[512,3,1024]{2,0,1:T(8,128)(2,1)} %param.9) | copy-start | bytes 9437188
  11.6 0.8 %copy-start.6 = (s32[512,3,8]{0,2,1:T(8,128)S(1)}, s32[512,3,8]{0,2,1:T(8,128)}, u32[]{:S(2)}) copy-start(s32[512,3,8]{0,2,1:T(8,128)} %param.10) | copy-start | bytes 147460
  12.4 11.8 %copy-start.8 = (f32[3,1024]{1,0:T(4,128)S(1)}, f32[3,1024]{1,0:T(4,128)}, u32[]{:S(2)}) copy-start(f32[3,1024]{1,0:T(4,128)} %quad_ref.1) | copy-start | bytes 36868
  12.4 11.8 %copy-start.9 = (f32[2,1024]{1,0:T(2,128)S(1)}, f32[2,1024]{1,0:T(2,128)}, u32[]{:S(2)}) copy-start(f32[2,1024]{1,0:T(2,128)} %lin_ref.1) | copy-start | bytes 24580
  12.4 11.8 %copy-start.10 = (f32[1024]{0:T(1024)S(1)}, f32[1024]{0:T(1024)}, u32[]{:S(2)}) copy-start(f32[1024]{0:T(1024)} %param.13) | copy-start | bytes 12292
  12.4 11.8 %copy-start.11 = (s32[1024]{0:T(1024)S(1)}, s32[1024]{0:T(1024)}, u32[]{:S(2)}) copy-start(s32[1024]{0:T(1024)} %param.14) | copy-start | bytes 12292
  24.2 24.3 %copy-start.7 = (f32[512]{0:T(512)S(1)}, f32[512]{0:T(512)}, u32[]{:S(2)}) copy-start(f32[512]{0:T(512)} %param.15) | copy-start | bytes 6148
  29.3 2.7 %copy-start = (f32[512,3072]{1,0:T(8,128)}, f32[512,3072]{1,0:T(8,128)S(1)}, u32[]{:S(2)}) copy-start(f32[512,3072]{1,0:T(8,128)S(1)} %get-tuple-element.8.s_ref) | copy-start | bytes 18874372
  31.9 1.4 %copy-start.3 = (f32[512,1024]{1,0:T(8,128)}, f32[512,1024]{1,0:T(8,128)S(1)}, u32[]{:S(2)}) copy-start(f32[512,1024]{1,0:T(8,128)S(1)} %get-tuple-element.9.w_ref) | copy-start | bytes 6291460
  33.3 0.8 %copy-start.5 = (bf16[512,512]{1,0:T(8,128)(2,1)}, bf16[512,512]{1,0:T(8,128)(2,1)S(1)}, u32[]{:S(2)}) copy-start(bf16[512,512]{1,0:T(8,128)(2,1)S(1)} %get-tuple-element.12) | copy-start | bytes 1572868
  44.9 18.0 %all-to-all-start.2 = ((bf16[16,32,512]{2,1,0:T(8,128)(2,1)}), bf16[16,32,512]{2,1,0:T(8,128)(2,1)S(1)}, u32[]{:S(2)}, u32[]{:S(2)}) async-start(bf16[16,32,512]{2,1,0:T(8,128)(2,1)} %bitcast.9), calls=%async_computation.2 | async-start | bytes 1048576 | tf_op jit(solution)/shard_map/all_to_all | solution.py:217
  48.5 2.8 %copy-start.1 = (f32[512,3072]{1,0:T(8,128)S(1)}, f32[512,3072]{1,0:T(8,128)}, u32[]{:S(2)}) copy-start(f32[512,3072]{1,0:T(8,128)} %copy-done) | copy-start | bytes 18874372
  51.3 1.6 %copy-start.4 = (f32[512,1024]{1,0:T(8,128)S(1)}, f32[512,1024]{1,0:T(8,128)}, u32[]{:S(2)}) copy-start(f32[512,1024]{1,0:T(8,128)} %copy-done.3) | copy-start | bytes 6291460
  54.3 4.0 %collective-permute-start = (f32[6,1024]{1,0:T(8,128)S(1)}, f32[6,1024]{1,0:T(8,128)S(1)}, u32[]{:S(2)}, u32[]{:S(2)}) collective-permute-start(f32[6,1024]{1,0:T(8,128)S(1)} %get-tuple-element.13), channel_id=1, source_target_pairs={{0,16},{16,0},{1,17},{17,1},{2,18},{18,2},{3,19},{19,3},{4,20},{20... | collective-permute-start | bytes 73736 | tf_op jit(solution)/shard_map/ppermute | solution.py:231

commit v3 on v2

--- a/solution.py
+++ b/solution.py
@@ -11,7 +11,7 @@
 VMEM = pltpu.VMEM
 
 
-def vmem_call(kernel, out_shape, scratch_shapes=(), flops=0, nbytes=0, exps=0, n_in=0, smem=(), limit=40):
+def vmem_call(kernel, out_shape, scratch_shapes=(), flops=0, nbytes=0, exps=0, n_in=0, smem=(), limit=16):
     return pl.pallas_call(
         kernel,
         out_shape=out_shape,
@@ -38,7 +38,8 @@
     return jnp.transpose(jnp.broadcast_to(row[:, at : at + 128], (128, 128)))
 
 
-def prep_kernel(mant_ref, exp_ref, out_ref):
+def prep_kernel(mant_ref, exp_ref, cot_ref, out_ref, cot_out_ref):
+    cot_out_ref[...] = cot_ref[...]
     comps, units, width = mant_ref.shape
     blocks = exp_ref.shape[1]
     span = width // blocks
@@ -54,16 +55,18 @@
             out_ref[:, at : at + span] = value
 
 
-def main_kernel(n, a_ref, f_ref, lin_ref, quad_ref, cross_ref, ply_ref, part_ref, stat_ref, s_ref, w_ref, idx, d, acc):
-    cases = a_ref.shape[0]
+def main_kernel(mine_ref, other_ref, f_ref, lin_ref, quad_ref, cross_ref, ply_ref, keep_ref, send_ref, stat_ref, s_ref, w_ref, idx, d, acc):
+    half = mine_ref.shape[0]
+    cases = 2 * half
     width = lin_ref.shape[1]
     tile = 32
     peak = jnp.full((cases, 128), -jnp.inf, jnp.float32)
     for jb in range(width // JB):
         cols = slice(jb * JB, (jb + 1) * JB)
         base = jb * 3 * JB
+        a = jnp.concatenate([mine_ref[...], other_ref[...]], axis=0)
         s_ref[:, base : base + 3 * JB] = jnp.dot(
-            a_ref[...], f_ref[:, base : base + 3 * JB], preferred_element_type=jnp.float32
+            a, f_ref[:, base : base + 3 * JB], preferred_element_type=jnp.float32
         )
         f1, f2 = lin_ref[0:1, cols], lin_ref[1:2, cols]
         f11, f22, f66 = quad_ref[0:1, cols], quad_ref[1:2, cols], quad_ref[2:3, cols]
@@ -118,34 +121,71 @@
         elif jb < width // JB - 1:
             acc[...] += part
         else:
-            part_ref[...] = (acc[...] + part).astype(jnp.bfloat16)
+            keep_ref[...] = acc[0:half] + part[0:half]
+            send_ref[...] = (acc[half:] + part[half:]).astype(jnp.bfloat16)
     total = jnp.sum(total, axis=1, keepdims=True)
-    both = jnp.concatenate([to_lanes(peak, cases), to_lanes(total, cases)], axis=0)
-    for s in range(n):
-        stat_ref[s] = both
-
-
-def coef_kernel(n, me_ref, cot_ref, s_ref, w_ref, stat_ref, coef_ref, gain_ref, peaks, totals, turned):
+    stat_ref[0:1, :] = to_lanes(peak, cases)
+    stat_ref[1:2, :] = to_lanes(total, cases)
+
+
+def swap_halves(x):
+    half = x.shape[1] // 2
+    return jnp.concatenate([x[:, half:], x[:, :half]], axis=1)
+
+
+def merge_kernel(chips, keep_ref, got_ref, stat_ref, twin_ref, out_ref):
+    half, units = keep_ref.shape
+    rows = half // chips
+    cases = 2 * half
+    p1, p2 = stat_ref[0:1, :], swap_halves(twin_ref[0:1, :])
+    t1, t2 = stat_ref[1:2, :], swap_halves(twin_ref[1:2, :])
+    peak = jnp.maximum(p1, p2)
+    env = peak + jnp.log(t1 * jnp.exp(p1 - peak) + t2 * jnp.exp(p2 - peak))
+    lines = jnp.concatenate([env[:, at : at + 128] for at in range(0, cases, 128)], axis=0)
+    high = lines.astype(jnp.bfloat16).astype(jnp.float32)
+    middle = (lines - high).astype(jnp.bfloat16).astype(jnp.float32)
+    low = lines - high - middle
+    rest = jnp.zeros((16 - 3 * (cases // 128), 128), jnp.float32)
+    tail = jnp.concatenate([high, middle, low, rest], axis=0).astype(jnp.bfloat16)
+    g1, g2 = jnp.exp(p1 - env), jnp.exp(p2 - env)
+    step = min(128, half)
+    for at in range(0, half, step):
+        up, down = to_rows(g1, at), to_rows(g2, at)
+        for s in range(at // rows, (at + step) // rows):
+            r = slice(s * rows, (s + 1) * rows)
+            q = slice(s * rows - at, (s + 1) * rows - at)
+            blocks = [
+                keep_ref[r, c : c + 128] * up[q] + got_ref[r, c : c + 128].astype(jnp.float32) * down[q]
+                for c in range(0, units, 128)
+            ]
+            value = jnp.concatenate(blocks, axis=0).astype(jnp.bfloat16)
+            size = value.shape[0]
+            out_ref[s, 0:size, :] = value
+            out_ref[s, size : size + 16, :] = tail
+
+
+def coef_kernel(me_ref, cot_ref, s_ref, w_ref, stat_ref, part_ref, coef_ref, gain_ref, turned):
+    chips, size = part_ref.shape[0], part_ref.shape[1] - 16
     cases = cot_ref.shape[1]
     width = w_ref.shape[1]
-    rows = cases // n
-    for p in range(n):
-        peaks[p : p + 1, :] = stat_ref[p, 0:1, :]
-        totals[p : p + 1, :] = stat_ref[p, 1:2, :]
-    peak_all = peaks[...]
-    peak = jnp.max(peak_all, axis=0, keepdims=True)
-    total = jnp.sum(totals[...] * jnp.exp(peak_all - peak), axis=0, keepdims=True)
-    envelope = peak + jnp.log(total)
-    gain = cot_ref[...] * jnp.exp(peak_all - envelope)
-    peaks[...] = gain
-    for at in range(0, cases, 128):
-        square = gain[:, at : at + 128]
-        if n < 128:
-            square = jnp.concatenate([square, jnp.zeros((128 - n, 128), jnp.float32)], axis=0)
-        turned[at : at + 128, :] = jnp.transpose(square)
-    me = me_ref[0]
-    gain_ref[...] = turned[pl.ds(pl.multiple_of(me * rows, rows), rows), :]
-    mine = peaks[pl.ds(me, 1), :]
+    rows = cases // (2 * chips)
+    groups = cases // 128
+    envs = []
+    for p in range(chips):
+        lines = part_ref[p, size : size + 16, :].astype(jnp.float32)
+        lines = lines[0:groups] + lines[groups : 2 * groups] + lines[2 * groups : 3 * groups]
+        envs.append(jnp.concatenate([lines[g : g + 1] for g in range(groups)], axis=1))
+    env_all = jnp.concatenate(envs, axis=0)
+    top = jnp.max(env_all, axis=0, keepdims=True)
+    env = top + jnp.log(jnp.sum(jnp.exp(env_all - top), axis=0, keepdims=True))
+    cot = cot_ref[...]
+    gain = cot * jnp.exp(env_all - env)
+    pad = jnp.zeros((128 - chips, 128), jnp.float32)
+    for at in range(0, cases // 2, 128):
+        turned[at : at + 128, :] = jnp.transpose(jnp.concatenate([gain[:, at : at + 128], pad], axis=0))
+    chip = me_ref[0] >> 1
+    gain_ref[...] = turned[pl.ds(pl.multiple_of(chip * rows, rows), rows), :]
+    mine = cot * jnp.exp(stat_ref[0:1, :] - env)
     scales = [to_rows(mine, at) for at in range(0, cases, 128)]
     for jb in range(width // JB):
         base = jb * 3 * JB
@@ -168,37 +208,53 @@
                 coef_ref[i : i + 1, jb * JB + c : jb * JB + c + 128] = line
 
 
-def combine_kernel(n, gain_ref, part_ref, out_ref):
-    rows = out_ref.shape[0]
-    value = part_ref[0].astype(jnp.float32) * gain_ref[:, 0:1]
-    for p in range(1, n):
-        value = value + part_ref[p].astype(jnp.float32) * gain_ref[:, p : p + 1]
-    out_ref[...] = value
+def combine_kernel(gain_ref, part_ref, out_ref):
+    rows, units = out_ref.shape
+    chips = part_ref.shape[0]
+    value = jnp.zeros((rows * units // 128, 128), jnp.float32)
+    for p in range(chips):
+        gain = jnp.broadcast_to(gain_ref[:, p : p + 1], (rows, 128))
+        gain = jnp.concatenate([gain] * (units // 128), axis=0)
+        value = value + part_ref[p, 0 : rows * units // 128, :].astype(jnp.float32) * gain
+    for c in range(units // 128):
+        out_ref[:, c * 128 : (c + 1) * 128] = value[c * rows : (c + 1) * rows]
 
 
 def per_device(n, n_case, load_coef, mantissa, scale_exp, lin_coef, quad_coef, cross_coef, ply_count, cotangent):
     units, comps, width = mantissa.shape
     rows = load_coef.shape[0]
     cases = rows * n
+    half, chips = cases // 2, n // 2
     f32, bf16 = jnp.float32, jnp.bfloat16
     shape = jax.ShapeDtypeStruct
-
-    copies = jnp.broadcast_to(load_coef[None], (n, rows, units))
-    gathered = lax.all_to_all(copies, "elem", 0, 0).reshape(cases, units)
-
-    fields = vmem_call(
+    groups = [list(range(c, n, 2)) for c in range(2)]
+    me = lax.axis_index("elem").astype(jnp.int32)
+
+    def twin(x):
+        return lax.ppermute(x, "elem", [(i, i ^ 1) for i in range(n)])
+
+    copies = jnp.broadcast_to(load_coef[None], (chips, rows, units))
+    mine = lax.all_to_all(copies, "elem", 0, 0, axis_index_groups=groups).reshape(half, units)
+    other = twin(mine)
+    cot = cotangent.reshape(chips, 2, rows)
+    cot = jnp.concatenate(
+        [lax.dynamic_index_in_dim(cot, (me & 1) ^ c, 1, keepdims=False).reshape(1, half) for c in range(2)], axis=1
+    )
+
+    fields, cot = vmem_call(
         prep_kernel,
-        shape((units, comps * width), bf16),
+        [shape((units, comps * width), bf16), shape((1, cases), f32)],
         flops=units * comps * width,
         nbytes=4 * units * comps * width,
-        n_in=2,
-    )(jnp.transpose(mantissa, (1, 0, 2)), jnp.transpose(scale_exp, (1, 2, 0)))
-
-    part, stat, stress, weight = vmem_call(
-        functools.partial(main_kernel, n),
+        n_in=3,
+    )(jnp.transpose(mantissa, (1, 0, 2)), jnp.transpose(scale_exp, (1, 2, 0)), cot)
+
+    keep, send, stat, stress, weight = vmem_call(
+        main_kernel,
         [
-            shape((cases, units), bf16),
-            shape((n, 2, cases), f32),
+            shape((half, units), f32),
+            shape((half, units), bf16),
+            shape((2, cases), f32),
             shape((cases, comps * width), f32),
             shape((cases, width), f32),
         ],
@@ -210,29 +266,35 @@
         flops=4 * cases * units * comps * width,
         nbytes=2 * units * comps * width + 4 * cases * 4 * width,
         exps=cases * width,
-        n_in=6,
-    )(gathered, fields, lin_coef, quad_coef, cross_coef.reshape(1, width), ply_count.reshape(1, width))
-
-    stats = lax.all_to_all(stat, "elem", 0, 0)
-    parts = lax.all_to_all(part.reshape(n, rows, units), "elem", 0, 0)
-
-    me = lax.axis_index("elem").astype(jnp.int32).reshape(1)
+        n_in=7,
+        limit=24,
+    )(mine, other, fields, lin_coef, quad_coef, cross_coef.reshape(1, width), ply_count.reshape(1, width))
+
+    chunks = vmem_call(
+        functools.partial(merge_kernel, chips),
+        shape((chips, rows * units // 128 + 16, 128), bf16),
+        flops=4 * half * units,
+        nbytes=8 * half * units,
+        n_in=4,
+    )(keep, twin(send), stat, twin(stat))
+    parts = lax.all_to_all(chunks, "elem", 0, 0, axis_index_groups=groups)
+
     coef, gain = vmem_call(
-        functools.partial(coef_kernel, n),
+        coef_kernel,
         [shape((6, width), f32), shape((rows, 128), f32)],
-        scratch_shapes=[VMEM((n, cases), f32), VMEM((n, cases), f32), VMEM((cases, 128), f32)],
+        scratch_shapes=[VMEM((half, 128), f32)],
         flops=14 * cases * width,
         nbytes=16 * cases * width,
-        n_in=5,
+        n_in=6,
         smem=(0,),
-    )(me, cotangent.reshape(1, cases), stress, weight, stats)
+    )(me.reshape(1), cot, stress, weight, stat, parts)
     bit = 1
     while bit < n_case:
         coef = coef + lax.ppermute(coef, "case", [(i, i ^ bit) for i in range(n_case)])
         bit *= 2
 
     load_grad = vmem_call(
-        functools.partial(combine_kernel, n),
+        combine_kernel,
         shape((rows, units), f32),
         flops=2 * n * rows * units,
         nbytes=2 * n * rows * units,

time: 64.4 us -> 49.1 us (0.76)
  blocking collectives: 10.8 us -> 30.3 us
  waiting for transfers between devices: 17.3 us -> 2.77 us
  starting transfers between devices: 12.6 us -> 2.21 us
  local copies, waits for them, and re-layouts: 13.5 us -> 4.46 us
    all_to_all x1 -> x2, blocking collectives: 10.8 us -> 30.3 us  [the longest x1 16 us: per_device(): lax.all_to_all(copies, 'elem', 0, 0, axis_index_groups=groups)]
    all_to_all x2 -> x0, waiting for transfers between devices: 14.8 us -> none  [the longest x1 10.8 us: per_device(): gathered = lax.all_to_all(copies, 'elem', 0, 0).reshape(cases, units)]
    all_to_all x2 -> x0, starting transfers between devices: 11 us -> none  [the longest x1 7.44 us: per_device(): gathered = lax.all_to_all(copies, 'elem', 0, 0).reshape(cases, units)]
    unnamed x24 -> x12, local copies, waits for them, and re-layouts: 11.9 us -> 2.71 us
    ppermute x0 -> x3, waiting for transfers between devices: none -> 1.09 us  [twin(): return lax.ppermute(x, 'elem', [(i, i ^ 1) for i in range(n)])]
    reshape x0 -> x3, local copies, waits for them, and re-layouts: none -> 0.92 us  [the longest x1 0.76 us: per_device(): cot = cotangent.reshape(chips, 2, rows)]
    broadcast_in_dim x1, local copies, waits for them, and re-layouts: 1.61 us -> 0.8 us  [per_device(): copies = jnp.broadcast_to(load_coef[None], (chips, rows, units))]
    ppermute x1, waiting for transfers between devices: 2.42 us -> 1.67 us  [per_device(): lax.ppermute(coef, 'case', [(i, i ^ bit) for i in range(n_case)])]
  transfers between devices with their start and end apart: 3 -> 4, of which waited for: 3 -> 2; matrix products, arithmetic and copies ran while one was open for 1% -> 2% of each run, Pallas kernels for 4% -> 4%
where the time goes in v3:
time: 49.1 us; the launch traced here: 48.7 us
  blocking collectives  30.3 us (62%)
  Pallas kernels  7.65 us (16%)
  local copies, waits for them, and re-layouts  4.46 us (9%)
  waiting for transfers between devices  2.77 us (6%)
  starting transfers between devices  2.21 us (5%)
  between operations  0.75 us (2%)
  other arithmetic  0.63 us (1%)
    all_to_all x1, blocking collectives, per_device(): lax.all_to_all(copies, 'elem', 0, 0, axis_index_groups=groups)  16 us
    all_to_all x1, blocking collectives, per_device(): parts = lax.all_to_all(chunks, 'elem', 0, 0, axis_index_groups=groups)  14.3 us
    pallas_call x1, Pallas kernels, per_device(): vmem_call(main_kernel, [shape((half, units), f32), shape((half, units), b...  4.34 us
    unnamed x12, local copies, waits for them, and re-layouts  2.71 us
    ppermute x1, waiting for transfers between devices, per_device(): lax.ppermute(coef, 'case', [(i, i ^ bit) for i in range(n_case)])  1.67 us
    ppermute x1, starting transfers between devices, per_device(): lax.ppermute(coef, 'case', [(i, i ^ bit) for i in range(n_case)])  1.56 us
    pallas_call x1, Pallas kernels, per_device(): vmem_call(coef_kernel, [shape((6, width), f32), shape((rows, 128), f32)],...  1.33 us
    ppermute x3, waiting for transfers between devices, twin(): return lax.ppermute(x, 'elem', [(i, i ^ 1) for i in range(n)])  1.09 us
  transfers between devices with their start and end apart: 4, of which 2 were waited for; matrix products, arithmetic and copies ran while one was open for 2% of the time, Pallas kernels for 4%

profile of v3, /device:TPU:0, one launch (start us, length us, event | category | flops | bytes accessed | tf_op | source)
XLA Modules:
  0.0 48.7 jit_solution(17725026974047730038)
XLA Ops:
  0.6 0.0 copy-start.5
  0.6 0.0 copy-start.4
  0.7 0.0 copy-start.2
  0.7 0.0 copy-start.3
  0.7 0.8 %broadcast_in_dim.2 = bf16[8,32,512]{2,1,0:T(8,128)(2,1)S(1)} broadcast(bf16[32,512]{1,0:T(8,128)(2,1)} %param.8), dimensions={1,2} | broadcast | bytes 294912 | tf_op jit(solution)/shard_map/broadcast_in_dim | solution.py:236
  1.5 16.0 %all_to_all.10 = bf16[8,32,512]{2,1,0:T(8,128)(2,1)S(1)} all-to-all(bf16[8,32,512]{2,1,0:T(8,128)(2,1)S(1)} %broadcast_in_dim.2), channel_id=1, replica_groups={{0,2,4,6,8,10,12,14},{1,3,5,7,9,11,13,15},{16,18,20,22,24,26,28,30},{17..., dimensions={0} | all-to-all | bytes 524288 | tf_op jit(solution)/shard_map/all_to_all | solution.py:237
  17.5 0.0 collective-permute-start
  17.5 0.8 %reshape.29 = f32[8,2,32]{2,1,0:T(2,128)S(1)} reshape(f32[512]{0:T(512)} %param.15) | data formatting | bytes 4096 | tf_op jit(solution)/shard_map/reshape | solution.py:239
  18.3 0.1 reshape.30
  18.4 0.1 reshape.31
  18.4 0.0 copy-start
  18.4 1.9 %copy-done = bf16[512,3,1024]{2,0,1:T(8,128)(2,1)S(1)} copy-done((bf16[512,3,1024]{2,0,1:T(8,128)(2,1)S(1)}, bf16[512,3,1024]{2,0,1:T(8,128)(2,1)}, u32[]{:S(2)}) %copy-start) | copy-done | bytes 3145752
  20.3 0.0 copy-start.1
  20.3 0.8 %copy-done.1 = s32[512,3,8]{0,2,1:T(8,128)S(1)} copy-done((s32[512,3,8]{0,2,1:T(8,128)S(1)}, s32[512,3,8]{0,2,1:T(8,128)}, u32[]{:S(2)}) %copy-start.1) | copy-done | bytes 49176
  21.1 1.1 %shard_map.95 = (bf16[512,3072]{1,0:T(8,128)(2,1)S(1)}, f32[1,512]{1,0:T(1,128)S(1)}) custom-call(bf16[3,512,1024]{2,1,0:T(8,128)(2,1)S(1)} %bitcast.6, s32[3,8,512]{2,1,0:T(8,128)S(1)} %bitcast.9, f32[1,512]{1,0:T(1,128)S(1)} %pad_maximum_fusion.cot_ref), custom_call_target="tpu_custom_call" | custom-call | flops 1572864 | bytes 6291456 | tf_op jit(solution)/shard_map/pallas_call | solution.py:244
  22.2 0.0 collective-permute-done.other_ref
  22.2 0.0 copy-done.5
  22.2 0.0 copy-done.4
  22.2 0.0 copy-done.2
  22.2 0.0 copy-done.3
  22.2 4.3 %shard_map.96 = (f32[256,512]{1,0:T(8,128)S(1)}, bf16[256,512]{1,0:T(8,128)(2,1)S(1)}, f32[2,512]{1,0:T(2,128)S(1)}, f32[512,3072]{1,0:T(8,128)S(1)}, f32[512,1024]{1,0:T(8,128)S(1)}) custom-call(bf16[256,512]{1,0:T(8,128)(2,1)S(1)} %bitcast.8, bf16[256,512]{1,0:T(8,128)(2,1)S(1)} %collective-permute-done.other_ref, ...), custom_call_target="tpu_custom_call" | custom-call | flops 3221225472 | bytes 11534336 | tf_op jit(solution)/shard_map/pallas_call | solution.py:252
  26.6 0.6 %collective-permute-start.1 = (bf16[256,512]{1,0:T(8,128)(2,1)S(1)}, bf16[256,512]{1,0:T(8,128)(2,1)S(1)}, u32[]{:S(2)}, u32[]{:S(2)}) collective-permute-start(bf16[256,512]{1,0:T(8,128)(2,1)S(1)} %get-tuple-element.17), channel_id=1, source_target_pairs={{0,1},{1,0},{2,3},{3,2},{4,5},{5,4},{6,7},{7,6},{8,9},{9,8},{10,11... | collective-permute-start | bytes 786440 | tf_op jit(solution)/shard_map/ppermute | solution.py:234
  27.2 0.1 collective-permute-start.2
  27.2 1.1 %collective-permute-done.2.twin_ref = f32[2,512]{1,0:T(2,128)S(1)} collective-permute-done((f32[2,512]{1,0:T(2,128)S(1)}, f32[2,512]{1,0:T(2,128)S(1)}, u32[]{:S(2)}, u32[]{:S(2)}) %collective-permute-start.2) | collective-permute-done | bytes 4128 | tf_op jit(solution)/shard_map/ppermute | solution.py:234
  28.3 0.0 collective-permute-done.1.got_ref
  28.3 0.2 shard_map.97
  28.5 14.3 %all_to_all.11.part_ref = bf16[8,144,128]{2,1,0:T(8,128)(2,1)S(1)} all-to-all(bf16[8,144,128]{2,1,0:T(8,128)(2,1)S(1)} %shard_map.97), channel_id=1, replica_groups={{0,2,4,6,8,10,12,14},{1,3,5,7,9,11,13,15},{16,18,20,22,24,26,28,30},{17..., dimensions={0} | all-to-all | bytes 589824 | tf_op jit(solution)/shard_map/all_to_all | solution.py:280
  42.8 1.3 %shard_map.98 = (f32[6,1024]{1,0:T(8,128)S(1)}, f32[32,128]{1,0:T(8,128)S(1)}) custom-call(s32[1]{0:T(128)} %bitcast.me_ref, f32[1,512]{1,0:T(1,128)S(1)} %get-tuple-element.11.cot_ref, f32[512,3072]{1,0:T(8,128)S(1)} %get-tuple-element.13.s_ref, f32[512,1024]{1,0:T(8,128)S(1)} %get-tuple-element.14.w_ref, f32[2,512]{1,0:T(2,128)S(1)} %get-tuple-element.15.stat_ref, ...), custom_call_target="tpu_custom_call" | custom-call | flops 7340032 | bytes 8388608 | tf_op jit(solution)/shard_map/pallas_call | solution.py:282
  44.1 1.6 %collective-permute-start.3 = (f32[6,1024]{1,0:T(8,128)S(1)}, f32[6,1024]{1,0:T(8,128)S(1)}, u32[]{:S(2)}, u32[]{:S(2)}) collective-permute-start(f32[6,1024]{1,0:T(8,128)S(1)} %get-tuple-element.19), channel_id=1, source_target_pairs={{0,16},{16,0},{1,17},{17,1},{2,18},{18,2},{3,19},{19,3},{4,20},{20... | collective-permute-start | bytes 73736 | tf_op jit(solution)/shard_map/ppermute | solution.py:293
  45.7 0.7 %shard_map.99 = f32[32,512]{1,0:T(8,128)} custom-call(f32[32,128]{1,0:T(8,128)S(1)} %get-tuple-element.18.gain_ref, bf16[8,144,128]{2,1,0:T(8,128)(2,1)S(1)} %all_to_all.11.part_ref), custom_call_target="tpu_custom_call" | custom-call | flops 524288 | bytes 524288 | tf_op jit(solution)/shard_map/pallas_call | solution.py:296
  46.4 1.7 %collective-permute-done.3 = f32[6,1024]{1,0:T(8,128)S(1)} collective-permute-done((f32[6,1024]{1,0:T(8,128)S(1)}, f32[6,1024]{1,0:T(8,128)S(1)}, u32[]{:S(2)}, u32[]{:S(2)}) %collective-permute-start.3) | collective-permute-done | bytes 24608 | tf_op jit(solution)/shard_map/ppermute | solution.py:293
  48.1 0.6 %add.12 = f32[6,1024]{1,0:T(8,128)} add(f32[6,1024]{1,0:T(8,128)S(1)} %get-tuple-element.19, f32[6,1024]{1,0:T(8,128)S(1)} %collective-permute-done.3) | non-fusion elementwise | flops 6144 | bytes 73728 | tf_op jit(solution)/shard_map/add | solution.py:293
  (2 shorter events, 0.0 us)
Async XLA Ops:
  0.6 21.6 %copy-start.5 = (s32[1024]{0:T(1024)S(1)}, s32[1024]{0:T(1024)}, u32[]{:S(2)}) copy-start(s32[1024]{0:T(1024)} %param.14) | copy-start | bytes 12292
  0.6 21.6 %copy-start.4 = (f32[1024]{0:T(1024)S(1)}, f32[1024]{0:T(1024)}, u32[]{:S(2)}) copy-start(f32[1024]{0:T(1024)} %param.13) | copy-start | bytes 12292
  0.7 21.6 %copy-start.2 = (f32[3,1024]{1,0:T(4,128)S(1)}, f32[3,1024]{1,0:T(4,128)}, u32[]{:S(2)}) copy-start(f32[3,1024]{1,0:T(4,128)} %quad_ref.1) | copy-start | bytes 36868
  0.7 21.6 %copy-start.3 = (f32[2,1024]{1,0:T(2,128)S(1)}, f32[2,1024]{1,0:T(2,128)}, u32[]{:S(2)}) copy-start(f32[2,1024]{1,0:T(2,128)} %lin_ref.1) | copy-start | bytes 24580
  17.5 4.7 %collective-permute-start = (bf16[256,512]{1,0:T(8,128)(2,1)S(1)}, bf16[256,512]{1,0:T(8,128)(2,1)S(1)}, u32[]{:S(2)}, u32[]{:S(2)}) collective-permute-start(bf16[256,512]{1,0:T(8,128)(2,1)S(1)} %bitcast.7), channel_id=1, source_target_pairs={{0,1},{1,0},{2,3},{3,2},{4,5},{5,4},{6,7},{7,6},{8,9},{9,8},{10,11... | collective-permute-start | bytes 786440 | tf_op jit(solution)/shard_map/ppermute | solution.py:234
  18.4 1.9 %copy-start = (bf16[512,3,1024]{2,0,1:T(8,128)(2,1)S(1)}, bf16[512,3,1024]{2,0,1:T(8,128)(2,1)}, u32[]{:S(2)}) copy-start(bf16[512,3,1024]{2,0,1:T(8,128)(2,1)} %param.9) | copy-start | bytes 9437188
  20.3 0.8 %copy-start.1 = (s32[512,3,8]{0,2,1:T(8,128)S(1)}, s32[512,3,8]{0,2,1:T(8,128)}, u32[]{:S(2)}) copy-start(s32[512,3,8]{0,2,1:T(8,128)} %param.10) | copy-start | bytes 147460
  26.6 1.7 %collective-permute-start.1 = (bf16[256,512]{1,0:T(8,128)(2,1)S(1)}, bf16[256,512]{1,0:T(8,128)(2,1)S(1)}, u32[]{:S(2)}, u32[]{:S(2)}) collective-permute-start(bf16[256,512]{1,0:T(8,128)(2,1)S(1)} %get-tuple-element.17), channel_id=1, source_target_pairs={{0,1},{1,0},{2,3},{3,2},{4,5},{5,4},{6,7},{7,6},{8,9},{9,8},{10,11... | collective-permute-start | bytes 786440 | tf_op jit(solution)/shard_map/ppermute | solution.py:234
  27.2 1.2 %collective-permute-start.2 = (f32[2,512]{1,0:T(2,128)S(1)}, f32[2,512]{1,0:T(2,128)S(1)}, u32[]{:S(2)}, u32[]{:S(2)}) collective-permute-start(f32[2,512]{1,0:T(2,128)S(1)} %get-tuple-element.15.stat_ref), channel_id=1, source_target_pairs={{0,1},{1,0},{2,3},{3,2},{4,5},{5,4},{6,7},{7,6},{8,9},{9,8},{10,11... | collective-permute-start | bytes 12296 | tf_op jit(solution)/shard_map/ppermute | solution.py:234
  44.1 4.0 %collective-permute-start.3 = (f32[6,1024]{1,0:T(8,128)S(1)}, f32[6,1024]{1,0:T(8,128)S(1)}, u32[]{:S(2)}, u32[]{:S(2)}) collective-permute-start(f32[6,1024]{1,0:T(8,128)S(1)} %get-tuple-element.19), channel_id=1, source_target_pairs={{0,16},{16,0},{1,17},{17,1},{2,18},{18,2},{3,19},{19,3},{4,20},{20... | collective-permute-start | bytes 73736 | tf_op jit(solution)/shard_map/ppermute | solution.py:293

commit v4 on v3

--- a/solution.py
+++ b/solution.py
@@ -11,13 +11,14 @@
 VMEM = pltpu.VMEM
 
 
-def vmem_call(kernel, out_shape, scratch_shapes=(), flops=0, nbytes=0, exps=0, n_in=0, smem=(), limit=16):
+def vmem_call(kernel, out_shape, scratch_shapes=(), flops=0, nbytes=0, exps=0, n_in=0, smem=(), hbm=(), limit=16):
+    def place(i):
+        return pltpu.SMEM if i in smem else pltpu.HBM if i in hbm else VMEM
+
     return pl.pallas_call(
         kernel,
         out_shape=out_shape,
-        in_specs=[
-            pl.BlockSpec(memory_space=pltpu.SMEM if i in smem else VMEM) for i in range(n_in)
-        ],
+        in_specs=[pl.BlockSpec(memory_space=place(i)) for i in range(n_in)],
         out_specs=jax.tree.map(lambda _: pl.BlockSpec(memory_space=VMEM), out_shape),
         scratch_shapes=list(scratch_shapes),
         cost_estimate=pl.CostEstimate(flops=flops, bytes_accessed=nbytes, transcendentals=exps),
@@ -38,35 +39,75 @@
     return jnp.transpose(jnp.broadcast_to(row[:, at : at + 128], (128, 128)))
 
 
-def prep_kernel(mant_ref, exp_ref, cot_ref, out_ref, cot_out_ref):
-    cot_out_ref[...] = cot_ref[...]
-    comps, units, width = mant_ref.shape
+def swap_lanes(x, which, width, n):
+    lane = lax.broadcasted_iota(jnp.int32, x.shape, 1)
+    bit = 1
+    while bit < n:
+        step = bit * width
+        ahead = jnp.concatenate([x[:, step:], x[:, :step]], axis=1)
+        behind = jnp.concatenate([x[:, -step:], x[:, :-step]], axis=1)
+        other = jnp.where((lane & step) != 0, behind, ahead)
+        x = jnp.where((which & bit) != 0, other, x)
+        bit *= 2
+    return x
+
+
+def swap_halves(x):
+    half = x.shape[1] // 2
+    return jnp.concatenate([x[:, half:], x[:, :half]], axis=1)
+
+
+def pair_kernel(core_ref, own_ref, twin_ref, out_ref):
+    own, twin = own_ref[...].astype(jnp.float32), twin_ref[...].astype(jnp.float32)
+
+    @pl.when(core_ref[0] == 0)
+    def _():
+        out_ref[...] = jnp.concatenate([own, twin], axis=0).astype(jnp.bfloat16)
+
+    @pl.when(core_ref[0] != 0)
+    def _():
+        out_ref[...] = jnp.concatenate([twin, own], axis=0).astype(jnp.bfloat16)
+
+
+def prep_kernel(chip_ref, mant_hbm, exp_ref, cot_ref, out_ref, cot_out_ref, mant, sems):
+    comps, units, width = mant.shape
     blocks = exp_ref.shape[1]
     span = width // blocks
+    copies = [pltpu.make_async_copy(mant_hbm.at[k], mant.at[k], sems.at[k]) for k in range(comps)]
+    for copy in copies:
+        copy.start()
+    chips = cot_ref.shape[0]
+    order = list(range(0, chips, 2)) + list(range(1, chips, 2))
+    cot_out_ref[...] = jnp.concatenate([cot_ref[pl.ds(chip_ref[0] ^ p, 1), :] for p in order], axis=1)
     factor = jnp.exp2(exp_ref[...].astype(jnp.float32)).reshape(comps * blocks, units)
     pad = jnp.zeros((128 - comps * blocks, units), jnp.float32)
     columns = jnp.transpose(jnp.concatenate([factor, pad], axis=0))
     for k in range(comps):
+        copies[k].wait()
         for b in range(blocks):
             gain = jnp.broadcast_to(columns[:, k * blocks + b : k * blocks + b + 1], (units, span))
-            value = mant_ref[k, :, b * span : (b + 1) * span] * gain.astype(jnp.bfloat16)
+            value = mant[k, :, b * span : (b + 1) * span] * gain.astype(jnp.bfloat16)
             first = b * span
             at = (first // JB) * (comps * JB) + k * JB + first % JB
             out_ref[:, at : at + span] = value
 
 
-def main_kernel(mine_ref, other_ref, f_ref, lin_ref, quad_ref, cross_ref, ply_ref, keep_ref, send_ref, stat_ref, s_ref, w_ref, idx, d, acc):
-    half = mine_ref.shape[0]
+def main_kernel(f_ref, lin_ref, quad_ref, cross_ref, ply_ref, *refs):
+    keep_ref, send_ref, stat_ref, s_ref, w_ref, a_ref, idx, d, acc = refs[-9:]
+    half = keep_ref.shape[0]
     cases = 2 * half
+    at = 0
+    for ref in refs[:-9]:
+        a_ref[at : at + ref.shape[0], :] = ref[...]
+        at += ref.shape[0]
     width = lin_ref.shape[1]
     tile = 32
     peak = jnp.full((cases, 128), -jnp.inf, jnp.float32)
     for jb in range(width // JB):
         cols = slice(jb * JB, (jb + 1) * JB)
         base = jb * 3 * JB
-        a = jnp.concatenate([mine_ref[...], other_ref[...]], axis=0)
         s_ref[:, base : base + 3 * JB] = jnp.dot(
-            a, f_ref[:, base : base + 3 * JB], preferred_element_type=jnp.float32
+            a_ref[...], f_ref[:, base : base + 3 * JB], preferred_element_type=jnp.float32
         )
         f1, f2 = lin_ref[0:1, cols], lin_ref[1:2, cols]
         f11, f22, f66 = quad_ref[0:1, cols], quad_ref[1:2, cols], quad_ref[2:3, cols]
@@ -128,14 +169,9 @@
     stat_ref[1:2, :] = to_lanes(total, cases)
 
 
-def swap_halves(x):
-    half = x.shape[1] // 2
-    return jnp.concatenate([x[:, half:], x[:, :half]], axis=1)
-
-
-def merge_kernel(chips, keep_ref, got_ref, stat_ref, twin_ref, out_ref):
+def merge_kernel(keep_ref, got_ref, stat_ref, twin_ref, *out_refs):
     half, units = keep_ref.shape
-    rows = half // chips
+    rows = half // len(out_refs)
     cases = 2 * half
     p1, p2 = stat_ref[0:1, :], swap_halves(twin_ref[0:1, :])
     t1, t2 = stat_ref[1:2, :], swap_halves(twin_ref[1:2, :])
@@ -151,41 +187,45 @@
     step = min(128, half)
     for at in range(0, half, step):
         up, down = to_rows(g1, at), to_rows(g2, at)
-        for s in range(at // rows, (at + step) // rows):
-            r = slice(s * rows, (s + 1) * rows)
-            q = slice(s * rows - at, (s + 1) * rows - at)
+        for j in range(at // rows, (at + step) // rows):
+            r = slice(j * rows, (j + 1) * rows)
+            q = slice(j * rows - at, (j + 1) * rows - at)
             blocks = [
                 keep_ref[r, c : c + 128] * up[q] + got_ref[r, c : c + 128].astype(jnp.float32) * down[q]
                 for c in range(0, units, 128)
             ]
             value = jnp.concatenate(blocks, axis=0).astype(jnp.bfloat16)
             size = value.shape[0]
-            out_ref[s, 0:size, :] = value
-            out_ref[s, size : size + 16, :] = tail
-
-
-def coef_kernel(me_ref, cot_ref, s_ref, w_ref, stat_ref, part_ref, coef_ref, gain_ref, turned):
-    chips, size = part_ref.shape[0], part_ref.shape[1] - 16
+            out_refs[j][0:size, :] = value
+            out_refs[j][size : size + 16, :] = tail
+
+
+def coef_kernel(core_ref, cot_ref, s_ref, w_ref, stat_ref, *refs):
+    coef_ref, gain_ref = refs[-2:]
+    part_refs = refs[:-2]
+    count = len(part_refs) // 2
+    size = part_refs[0].shape[0] - 16
     cases = cot_ref.shape[1]
     width = w_ref.shape[1]
-    rows = cases // (2 * chips)
     groups = cases // 128
+    rows = cases // (2 * count)
     envs = []
-    for p in range(chips):
-        lines = part_ref[p, size : size + 16, :].astype(jnp.float32)
+    for ref in part_refs:
+        lines = ref[size : size + 16, :].astype(jnp.float32)
         lines = lines[0:groups] + lines[groups : 2 * groups] + lines[2 * groups : 3 * groups]
         envs.append(jnp.concatenate([lines[g : g + 1] for g in range(groups)], axis=1))
     env_all = jnp.concatenate(envs, axis=0)
+    which = lax.broadcasted_iota(jnp.int32, env_all.shape, 0) & (count - 1)
+    env_all = swap_lanes(env_all, which, rows, count)
     top = jnp.max(env_all, axis=0, keepdims=True)
     env = top + jnp.log(jnp.sum(jnp.exp(env_all - top), axis=0, keepdims=True))
     cot = cot_ref[...]
-    gain = cot * jnp.exp(env_all - env)
-    pad = jnp.zeros((128 - chips, 128), jnp.float32)
-    for at in range(0, cases // 2, 128):
-        turned[at : at + 128, :] = jnp.transpose(jnp.concatenate([gain[:, at : at + 128], pad], axis=0))
-    chip = me_ref[0] >> 1
-    gain_ref[...] = turned[pl.ds(pl.multiple_of(chip * rows, rows), rows), :]
-    mine = cot * jnp.exp(stat_ref[0:1, :] - env)
+    gain = cot[:, 0:128] * jnp.exp(env_all[:, 0:128] - env[:, 0:128])
+    pad = jnp.zeros((128 - 2 * count, 128), jnp.float32)
+    gain_ref[...] = jnp.transpose(jnp.concatenate([gain, pad], axis=0))[0:rows]
+    both = jnp.concatenate([cot, env], axis=0)
+    both = jnp.where(core_ref[0] == 0, both, swap_halves(both))
+    mine = both[0:1] * jnp.exp(stat_ref[0:1, :] - both[1:2])
     scales = [to_rows(mine, at) for at in range(0, cases, 128)]
     for jb in range(width // JB):
         base = jb * 3 * JB
@@ -208,16 +248,18 @@
                 coef_ref[i : i + 1, jb * JB + c : jb * JB + c + 128] = line
 
 
-def combine_kernel(gain_ref, part_ref, out_ref):
+def combine_kernel(core_ref, gain_ref, *refs):
+    part_refs, out_ref, total = refs[:-2], refs[-2], refs[-1]
     rows, units = out_ref.shape
-    chips = part_ref.shape[0]
-    value = jnp.zeros((rows * units // 128, 128), jnp.float32)
-    for p in range(chips):
-        gain = jnp.broadcast_to(gain_ref[:, p : p + 1], (rows, 128))
+    value = jnp.zeros(total.shape, jnp.float32)
+    for p, ref in enumerate(part_refs):
+        gain = jnp.broadcast_to(gain_ref[:, p : p + 1], (2 * rows, 128))
         gain = jnp.concatenate([gain] * (units // 128), axis=0)
-        value = value + part_ref[p, 0 : rows * units // 128, :].astype(jnp.float32) * gain
+        value = value + ref[0 : total.shape[0], :].astype(jnp.float32) * gain
+    total[...] = value
     for c in range(units // 128):
-        out_ref[:, c * 128 : (c + 1) * 128] = value[c * rows : (c + 1) * rows]
+        at = pl.multiple_of((2 * c + core_ref[0]) * rows, rows)
+        out_ref[:, c * 128 : (c + 1) * 128] = total[pl.ds(at, rows), :]
 
 
 def per_device(n, n_case, load_coef, mantissa, scale_exp, lin_coef, quad_coef, cross_coef, ply_count, cotangent):
@@ -225,29 +267,40 @@
     rows = load_coef.shape[0]
     cases = rows * n
     half, chips = cases // 2, n // 2
+    count = chips // 2
     f32, bf16 = jnp.float32, jnp.bfloat16
     shape = jax.ShapeDtypeStruct
-    groups = [list(range(c, n, 2)) for c in range(2)]
     me = lax.axis_index("elem").astype(jnp.int32)
+    core, chip = (me & 1).reshape(1), (me >> 1).reshape(1)
 
     def twin(x):
         return lax.ppermute(x, "elem", [(i, i ^ 1) for i in range(n)])
 
-    copies = jnp.broadcast_to(load_coef[None], (chips, rows, units))
-    mine = lax.all_to_all(copies, "elem", 0, 0, axis_index_groups=groups).reshape(half, units)
-    other = twin(mine)
-    cot = cotangent.reshape(chips, 2, rows)
-    cot = jnp.concatenate(
-        [lax.dynamic_index_in_dim(cot, (me & 1) ^ c, 1, keepdims=False).reshape(1, half) for c in range(2)], axis=1
-    )
-
+    def reach(x, j):
+        return lax.ppermute(x, "elem", [(i, ((i >> 1) ^ (2 * j + (i & 1))) * 2 + (i & 1)) for i in range(n)])
+
+    block = vmem_call(
+        pair_kernel, shape((2 * rows, units), bf16), nbytes=8 * rows * units, n_in=3, smem=(0,)
+    )(core, load_coef, twin(load_coef))
+    mine = [reach(block, j) for j in range(count)]
     fields, cot = vmem_call(
         prep_kernel,
         [shape((units, comps * width), bf16), shape((1, cases), f32)],
+        scratch_shapes=[VMEM((comps, units, width), bf16), pltpu.SemaphoreType.DMA((comps,))],
         flops=units * comps * width,
         nbytes=4 * units * comps * width,
-        n_in=3,
-    )(jnp.transpose(mantissa, (1, 0, 2)), jnp.transpose(scale_exp, (1, 2, 0)), cot)
+        n_in=4,
+        smem=(0,),
+        hbm=(1,),
+    )(
+        chip,
+        pltpu.with_memory_space_constraint(jnp.transpose(mantissa, (1, 0, 2)), pltpu.HBM),
+        jnp.transpose(scale_exp, (1, 2, 0)),
+        cotangent.reshape(chips, 2 * rows),
+    )
+
+    mine[0], fields = lax.optimization_barrier((mine[0], fields))
+    other = [twin(x) for x in mine]
 
     keep, send, stat, stress, weight = vmem_call(
         main_kernel,
@@ -259,6 +312,7 @@
             shape((cases, width), f32),
         ],
         scratch_shapes=[
+            VMEM((cases, units), bf16),
             VMEM((cases, width), f32),
             VMEM((cases, comps * width), bf16),
             VMEM((cases, units), f32),
@@ -266,28 +320,28 @@
         flops=4 * cases * units * comps * width,
         nbytes=2 * units * comps * width + 4 * cases * 4 * width,
         exps=cases * width,
-        n_in=7,
+        n_in=5 + 2 * count,
         limit=24,
-    )(mine, other, fields, lin_coef, quad_coef, cross_coef.reshape(1, width), ply_count.reshape(1, width))
+    )(fields, lin_coef, quad_coef, cross_coef.reshape(1, width), ply_count.reshape(1, width), *mine, *other)
 
     chunks = vmem_call(
-        functools.partial(merge_kernel, chips),
-        shape((chips, rows * units // 128 + 16, 128), bf16),
+        merge_kernel,
+        [shape((2 * rows * units // 128 + 16, 128), bf16)] * count,
         flops=4 * half * units,
         nbytes=8 * half * units,
         n_in=4,
     )(keep, twin(send), stat, twin(stat))
-    parts = lax.all_to_all(chunks, "elem", 0, 0, axis_index_groups=groups)
+    parts = [reach(x, j) for j, x in enumerate(chunks)]
+    parts = parts + [twin(x) for x in parts]
 
     coef, gain = vmem_call(
         coef_kernel,
-        [shape((6, width), f32), shape((rows, 128), f32)],
-        scratch_shapes=[VMEM((half, 128), f32)],
+        [shape((6, width), f32), shape((2 * rows, 128), f32)],
         flops=14 * cases * width,
         nbytes=16 * cases * width,
-        n_in=6,
+        n_in=5 + chips,
         smem=(0,),
-    )(me.reshape(1), cot, stress, weight, stat, parts)
+    )(core, cot, stress, weight, stat, *parts)
     bit = 1
     while bit < n_case:
         coef = coef + lax.ppermute(coef, "case", [(i, i ^ bit) for i in range(n_case)])
@@ -296,10 +350,12 @@
     load_grad = vmem_call(
         combine_kernel,
         shape((rows, units), f32),
+        scratch_shapes=[VMEM((2 * rows * units // 128, 128), f32)],
         flops=2 * n * rows * units,
         nbytes=2 * n * rows * units,
-        n_in=2,
-    )(gain, parts)
+        n_in=2 + chips,
+        smem=(0,),
+    )(core, gain, *parts)
     return (load_grad, coef)
 
 

time: 49.1 us -> 45.1 us (0.919)
  blocking collectives: 30.3 us -> 0 us
  starting transfers between devices: 2.21 us -> 26 us
  waiting for transfers between devices: 2.77 us -> 6.08 us
  local copies, waits for them, and re-layouts: 4.46 us -> 2.33 us
  Pallas kernels: 7.65 us -> 9 us
    all_to_all x2 -> x0, blocking collectives: 30.3 us -> none  [the longest x1 16 us: per_device(): lax.all_to_all(copies, 'elem', 0, 0, axis_index_groups=groups)]
    ppermute x3 -> x11, starting transfers between devices: 0.65 us -> 12.9 us  [twin(): return lax.ppermute(x, 'elem', [(i, i ^ 1) for i in range(n)])]
    ppermute x0 -> x8, starting transfers between devices: none -> 11.6 us  [reach(): lax.ppermute(x, 'elem', [(i, (i >> 1 ^ 2 * j + (i & 1)) * 2 + (i & 1)) fo...]
    ppermute x3 -> x11, waiting for transfers between devices: 1.09 us -> 4.17 us  [twin(): return lax.ppermute(x, 'elem', [(i, i ^ 1) for i in range(n)])]
    pallas_call x1, Pallas kernels: 1.06 us -> 2.44 us  [per_device(): vmem_call(prep_kernel, [shape((units, comps * width), bf16), shape((1, ca...]
    unnamed x12, local copies, waits for them, and re-layouts: 2.71 us -> 1.57 us
    broadcast_in_dim x1 -> x0, local copies, waits for them, and re-layouts: 0.8 us -> none  [per_device(): copies = jnp.broadcast_to(load_coef[None], (chips, rows, units))]
    pallas_call x3 -> x4, Pallas kernels: 2.26 us -> 2.25 us  [the longest x1 1.24 us: per_device(): vmem_call(coef_kernel, [shape((6, width), f32), shape((2 * rows, 128), f3...]
  transfers between devices with their start and end apart: 4 -> 20, of which waited for: 2 -> 9; matrix products, arithmetic and copies ran while one was open for 2% -> 2% of each run, Pallas kernels for 4% -> 7%
where the time goes in v4:
time: 45.1 us; the launch traced here: 44.8 us
  starting transfers between devices  26 us (58%)
  Pallas kernels  9 us (20%)
  waiting for transfers between devices  6.08 us (13%)
  local copies, waits for them, and re-layouts  2.33 us (5%)
  between operations  0.75 us (2%)
  other arithmetic  0.62 us (1%)
    ppermute x11, starting transfers between devices, twin(): return lax.ppermute(x, 'elem', [(i, i ^ 1) for i in range(n)])  12.9 us
    ppermute x8, starting transfers between devices, reach(): lax.ppermute(x, 'elem', [(i, (i >> 1 ^ 2 * j + (i & 1)) * 2 + (i & 1)) fo...  11.6 us
    pallas_call x1, Pallas kernels, per_device(): vmem_call(main_kernel, [shape((half, units), f32), shape((half, units), b...  4.31 us
    ppermute x11, waiting for transfers between devices, twin(): return lax.ppermute(x, 'elem', [(i, i ^ 1) for i in range(n)])  4.17 us
    pallas_call x1, Pallas kernels, per_device(): vmem_call(prep_kernel, [shape((units, comps * width), bf16), shape((1, ca...  2.44 us
    ppermute x1, waiting for transfers between devices, per_device(): lax.ppermute(coef, 'case', [(i, i ^ bit) for i in range(n_case)])  1.61 us
    unnamed x12, local copies, waits for them, and re-layouts  1.57 us
    ppermute x1, starting transfers between devices, per_device(): lax.ppermute(coef, 'case', [(i, i ^ bit) for i in range(n_case)])  1.56 us
  transfers between devices with their start and end apart: 20, of which 9 were waited for; matrix products, arithmetic and copies ran while one was open for 2% of the time, Pallas kernels for 7%

profile of v4, /device:TPU:0, one launch (start us, length us, event | category | flops | bytes accessed | tf_op | source)
XLA Modules:
  0.0 44.8 jit_solution(12737774104241606923)
XLA Ops:
  0.6 0.0 copy-start.3
  0.6 0.5 %collective-permute-start = (bf16[32,512]{1,0:T(8,128)(2,1)}, bf16[32,512]{1,0:T(8,128)(2,1)S(1)}, u32[]{:S(2)}, u32[]{:S(2)}) collective-permute-start(bf16[32,512]{1,0:T(8,128)(2,1)} %own_ref.1), channel_id=1, source_target_pairs={{0,1},{1,0},{2,3},{3,2},{4,5},{5,4},{6,7},{7,6},{8,9},{9,8},{10,11... | collective-permute-start | bytes 98312 | tf_op jit(solution)/shard_map/ppermute | solution.py:277
  1.2 1.1 %collective-permute-done.twin_ref = bf16[32,512]{1,0:T(8,128)(2,1)S(1)} collective-permute-done((bf16[32,512]{1,0:T(8,128)(2,1)}, bf16[32,512]{1,0:T(8,128)(2,1)S(1)}, u32[]{:S(2)}, u32[]{:S(2)}) %collective-permute-start) | collective-permute-done | bytes 32800 | tf_op jit(solution)/shard_map/ppermute | solution.py:277
  2.2 0.0 copy-start.1
  2.2 0.8 %copy-done.1 = bf16[32,512]{1,0:T(8,128)(2,1)S(1)} copy-done((bf16[32,512]{1,0:T(8,128)(2,1)S(1)}, bf16[32,512]{1,0:T(8,128)(2,1)}, u32[]{:S(2)}) %copy-start.1) | copy-done | bytes 32792
  3.0 0.0 copy-start.2
  3.0 0.0 copy-start.4
  3.0 0.0 copy-start.5
  3.0 0.8 %collective-permute-start.1 = (bf16[64,512]{1,0:T(8,128)(2,1)S(1)}, bf16[64,512]{1,0:T(8,128)(2,1)S(1)}, u32[]{:S(2)}, u32[]{:S(2)}) collective-permute-start(bf16[64,512]{1,0:T(8,128)(2,1)S(1)} %shard_map.96), channel_id=1, source_target_pairs={{0,0},{1,3},{2,2},{3,1},{4,4},{5,7},{6,6},{7,5},{8,8},{9,11},{10,1... | collective-permute-start | bytes 196616 | tf_op jit(solution)/shard_map/ppermute | solution.py:280
  3.8 5.0 %collective-permute-start.4 = (bf16[64,512]{1,0:T(8,128)(2,1)S(1)}, bf16[64,512]{1,0:T(8,128)(2,1)S(1)}, u32[]{:S(2)}, u32[]{:S(2)}) collective-permute-start(bf16[64,512]{1,0:T(8,128)(2,1)S(1)} %shard_map.96), channel_id=1, source_target_pairs={{0,12},{1,15},{2,14},{3,13},{4,8},{5,11},{6,10},{7,9},{8,4},{9,7},... | collective-permute-start | bytes 196616 | tf_op jit(solution)/shard_map/ppermute | solution.py:280
  8.8 0.0 collective-permute-start.3
  8.8 0.6 %collective-permute-start.2 = (bf16[64,512]{1,0:T(8,128)(2,1)S(1)}, bf16[64,512]{1,0:T(8,128)(2,1)S(1)}, u32[]{:S(2)}, u32[]{:S(2)}) collective-permute-start(bf16[64,512]{1,0:T(8,128)(2,1)S(1)} %shard_map.96), channel_id=1, source_target_pairs={{0,4},{1,7},{2,6},{3,5},{4,0},{5,3},{6,2},{7,1},{8,12},{9,15},{10,... | collective-permute-start | bytes 196616 | tf_op jit(solution)/shard_map/ppermute | solution.py:280
  9.5 0.8 %reshape.21.cot_ref = f32[8,64]{1,0:T(8,128)S(1)} reshape(f32[512]{0:T(512)} %param.15) | data formatting | bytes 4096 | tf_op jit(solution)/shard_map/reshape | solution.py:299
  10.2 0.0 copy-start
  10.2 0.8 %copy-done = s32[512,3,8]{0,2,1:T(8,128)S(1)} copy-done((s32[512,3,8]{0,2,1:T(8,128)S(1)}, s32[512,3,8]{0,2,1:T(8,128)}, u32[]{:S(2)}) %copy-start) | copy-done | bytes 49176
  11.0 2.4 %shard_map.95 = (bf16[512,3072]{1,0:T(8,128)(2,1)S(1)}, f32[1,512]{1,0:T(1,128)S(1)}) custom-call(s32[1]{0:T(128)} %bitcast.1.chip_ref, bf16[3,512,1024]{2,1,0:T(8,128)(2,1)} %bitcast.9, s32[3,8,512]{2,1,0:T(8,128)S(1)} %bitcast.6, f32[8,64]{1,0:T(8,128)S(1)} %reshape.21.cot_ref), custom_call_target="tpu_custom_call" | custom-call | flops 1572864 | bytes 6291456 | tf_op jit(solution)/shard_map/pallas_call | solution.py:286
  13.5 0.0 collective-permute-done.1.refs_0_
  13.5 0.0 collective-permute-done.4.refs_3_
  13.5 3.0 %collective-permute-start.8 = (bf16[64,512]{1,0:T(8,128)(2,1)S(1)}, bf16[64,512]{1,0:T(8,128)(2,1)S(1)}, u32[]{:S(2)}, u32[]{:S(2)}) collective-permute-start(bf16[64,512]{1,0:T(8,128)(2,1)S(1)} %collective-permute-done.4.refs_3_), channel_id=1, source_target_pairs={{0,1},{1,0},{2,3},{3,2},{4,5},{5,4},{6,7},{7,6},{8,9},{9,8},{10,11... | collective-permute-start | bytes 196616 | tf_op jit(solution)/shard_map/ppermute | solution.py:277
  16.5 0.0 collective-permute-done.3.refs_2_
  16.5 0.1 collective-permute-start.7
  16.6 0.0 collective-permute-done.2.refs_1_
  16.6 0.4 collective-permute-start.6
  17.1 0.1 collective-permute-start.5
  17.1 0.3 collective-permute-done.8.refs_7_
  17.4 0.4 collective-permute-done.7.refs_6_
  17.8 0.2 collective-permute-done.6.refs_5_
  18.0 0.4 collective-permute-done.5.refs_4_
  18.3 0.0 copy-done.3
  18.3 0.0 copy-done.2
  18.3 0.0 copy-done.4
  18.3 0.0 copy-done.5
  18.3 4.3 %shard_map.97 = (f32[256,512]{1,0:T(8,128)S(1)}, bf16[256,512]{1,0:T(8,128)(2,1)S(1)}, f32[2,512]{1,0:T(2,128)S(1)}, f32[512,3072]{1,0:T(8,128)S(1)}, f32[512,1024]{1,0:T(8,128)S(1)}) custom-call(bf16[512,3072]{1,0:T(8,128)(2,1)S(1)} %get-tuple-element.19.f_ref, f32[2,1024]{1,0:T(2,128)S(1)} %copy-done.3, f32[3,1024]{1,0:T(4,128)S(1)} %copy-done.2, ...), custom_call_target="tpu_custom_call" | custom-call | flops 3221225472 | bytes 11534336 | tf_op jit(solution)/shard_map/pallas_call | solution.py:305
  22.7 0.2 collective-permute-start.9
  22.9 0.4 collective-permute-start.10
  23.2 1.0 %collective-permute-done.10.twin_ref = f32[2,512]{1,0:T(2,128)S(1)} collective-permute-done((f32[2,512]{1,0:T(2,128)S(1)}, f32[2,512]{1,0:T(2,128)S(1)}, u32[]{:S(2)}, u32[]{:S(2)}) %collective-permute-start.10) | collective-permute-done | bytes 4128 | tf_op jit(solution)/shard_map/ppermute | solution.py:277
  24.3 0.0 collective-permute-done.9.got_ref
  24.3 0.2 shard_map.98
  24.5 0.7 %collective-permute-start.11 = (bf16[272,128]{1,0:T(8,128)(2,1)S(1)}, bf16[272,128]{1,0:T(8,128)(2,1)S(1)}, u32[]{:S(2)}, u32[]{:S(2)}) collective-permute-start(bf16[272,128]{1,0:T(8,128)(2,1)S(1)} %get-tuple-element.26), channel_id=1, source_target_pairs={{0,0},{1,3},{2,2},{3,1},{4,4},{5,7},{6,6},{7,5},{8,8},{9,11},{10,1... | collective-permute-start | bytes 208904 | tf_op jit(solution)/shard_map/ppermute | solution.py:280
  25.1 1.5 %collective-permute-start.12 = (bf16[272,128]{1,0:T(8,128)(2,1)S(1)}, bf16[272,128]{1,0:T(8,128)(2,1)S(1)}, u32[]{:S(2)}, u32[]{:S(2)}) collective-permute-start(bf16[272,128]{1,0:T(8,128)(2,1)S(1)} %get-tuple-element.27), channel_id=1, source_target_pairs={{0,4},{1,7},{2,6},{3,5},{4,0},{5,3},{6,2},{7,1},{8,12},{9,15},{10,... | collective-permute-start | bytes 208904 | tf_op jit(solution)/shard_map/ppermute | solution.py:280
  26.6 2.6 %collective-permute-start.13 = (bf16[272,128]{1,0:T(8,128)(2,1)S(1)}, bf16[272,128]{1,0:T(8,128)(2,1)S(1)}, u32[]{:S(2)}, u32[]{:S(2)}) collective-permute-start(bf16[272,128]{1,0:T(8,128)(2,1)S(1)} %get-tuple-element.28), channel_id=1, source_target_pairs={{0,8},{1,11},{2,10},{3,9},{4,12},{5,15},{6,14},{7,13},{8,0},{9,3},... | collective-permute-start | bytes 208904 | tf_op jit(solution)/shard_map/ppermute | solution.py:280
  29.2 0.4 collective-permute-start.14
  29.6 0.0 collective-permute-done.11.refs_0_
  29.6 2.6 %collective-permute-start.15 = (bf16[272,128]{1,0:T(8,128)(2,1)S(1)}, bf16[272,128]{1,0:T(8,128)(2,1)S(1)}, u32[]{:S(2)}, u32[]{:S(2)}) collective-permute-start(bf16[272,128]{1,0:T(8,128)(2,1)S(1)} %collective-permute-done.11.refs_0_), channel_id=1, source_target_pairs={{0,1},{1,0},{2,3},{3,2},{4,5},{5,4},{6,7},{7,6},{8,9},{9,8},{10,11... | collective-permute-start | bytes 208904 | tf_op jit(solution)/shard_map/ppermute | solution.py:277
  32.2 0.0 collective-permute-done.12.refs_1_
  32.2 0.1 collective-permute-start.16
  32.3 0.3 collective-permute-done.13.refs_2_
  32.6 2.8 %collective-permute-start.17 = (bf16[272,128]{1,0:T(8,128)(2,1)S(1)}, bf16[272,128]{1,0:T(8,128)(2,1)S(1)}, u32[]{:S(2)}, u32[]{:S(2)}) collective-permute-start(bf16[272,128]{1,0:T(8,128)(2,1)S(1)} %collective-permute-done.13.refs_2_), channel_id=1, source_target_pairs={{0,1},{1,0},{2,3},{3,2},{4,5},{5,4},{6,7},{7,6},{8,9},{9,8},{10,11... | collective-permute-start | bytes 208904 | tf_op jit(solution)/shard_map/ppermute | solution.py:277
  35.4 0.0 collective-permute-done.14.refs_3_
  35.4 2.6 %collective-permute-start.18 = (bf16[272,128]{1,0:T(8,128)(2,1)S(1)}, bf16[272,128]{1,0:T(8,128)(2,1)S(1)}, u32[]{:S(2)}, u32[]{:S(2)}) collective-permute-start(bf16[272,128]{1,0:T(8,128)(2,1)S(1)} %collective-permute-done.14.refs_3_), channel_id=1, source_target_pairs={{0,1},{1,0},{2,3},{3,2},{4,5},{5,4},{6,7},{7,6},{8,9},{9,8},{10,11... | collective-permute-start | bytes 208904 | tf_op jit(solution)/shard_map/ppermute | solution.py:277
  38.0 0.0 collective-permute-done.15.refs_4_
  38.0 0.0 collective-permute-done.16.refs_5_
  38.0 0.0 collective-permute-done.17.refs_6_
  38.0 0.9 %collective-permute-done.18.refs_7_ = bf16[272,128]{1,0:T(8,128)(2,1)S(1)} collective-permute-done((bf16[272,128]{1,0:T(8,128)(2,1)S(1)}, bf16[272,128]{1,0:T(8,128)(2,1)S(1)}, u32[]{:S(2)}, u32[]{:S(2)}) %collective-permute-start.18) | collective-permute-done | bytes 69664 | tf_op jit(solution)/shard_map/ppermute | solution.py:277
  38.9 1.2 %shard_map.99 = (f32[6,1024]{1,0:T(8,128)S(1)}, f32[64,128]{1,0:T(8,128)S(1)}) custom-call(s32[1]{0:T(128)} %bitcast.core_ref, f32[1,512]{1,0:T(1,128)S(1)} %get-tuple-element.17.cot_ref, f32[512,3072]{1,0:T(8,128)S(1)} %get-tuple-element.21.s_ref, f32[512,1024]{1,0:T(8,128)S(1)} %get-tuple-element.22.w_ref, f32[2,512]{1,0:T(2,128)S(1)} %get-tuple-element.23.stat_ref, ...), custom_call_target="tpu_custom_call" | custom-call | flops 7340032 | bytes 8388608 | tf_op jit(solution)/shard_map/pallas_call | solution.py:337
  40.2 1.6 %collective-permute-start.19 = (f32[6,1024]{1,0:T(8,128)S(1)}, f32[6,1024]{1,0:T(8,128)S(1)}, u32[]{:S(2)}, u32[]{:S(2)}) collective-permute-start(f32[6,1024]{1,0:T(8,128)S(1)} %get-tuple-element.31), channel_id=1, source_target_pairs={{0,16},{16,0},{1,17},{17,1},{2,18},{18,2},{3,19},{19,3},{4,20},{20... | collective-permute-start | bytes 73736 | tf_op jit(solution)/shard_map/ppermute | solution.py:347
  41.7 0.8 %shard_map.100 = f32[32,512]{1,0:T(8,128)} custom-call(s32[1]{0:T(128)} %bitcast.core_ref, f32[64,128]{1,0:T(8,128)S(1)} %get-tuple-element.30.gain_ref, bf16[272,128]{1,0:T(8,128)(2,1)S(1)} %collective-permute-done.11.refs_0_, bf16[272,128]{1,0:T(8,128)(2,1)S(1)} %collective-permute-done.12.refs_1_, bf16[272,128]{1,0:T(8,128)(2,1)S(1)} %collective-permute-done.13.refs_2_, ...), custom_call_target="tpu_custom_call" | custom-call | flops 524288 | bytes 524288 | tf_op jit(solution)/shard_map/pallas_call | solution.py:350
  42.5 1.6 %collective-permute-done.19 = f32[6,1024]{1,0:T(8,128)S(1)} collective-permute-done((f32[6,1024]{1,0:T(8,128)S(1)}, f32[6,1024]{1,0:T(8,128)S(1)}, u32[]{:S(2)}, u32[]{:S(2)}) %collective-permute-start.19) | collective-permute-done | bytes 24608 | tf_op jit(solution)/shard_map/ppermute | solution.py:347
  44.1 0.6 %add.3 = f32[6,1024]{1,0:T(8,128)} add(f32[6,1024]{1,0:T(8,128)S(1)} %get-tuple-element.31, f32[6,1024]{1,0:T(8,128)S(1)} %collective-permute-done.19) | non-fusion elementwise | flops 6144 | bytes 73728 | tf_op jit(solution)/shard_map/add | solution.py:347
  (1 shorter events, 0.0 us)
Async XLA Ops:
  0.6 17.7 %copy-start.3 = (f32[2,1024]{1,0:T(2,128)S(1)}, f32[2,1024]{1,0:T(2,128)}, u32[]{:S(2)}) copy-start(f32[2,1024]{1,0:T(2,128)} %lin_ref.1) | copy-start | bytes 24580
  0.6 1.6 %collective-permute-start = (bf16[32,512]{1,0:T(8,128)(2,1)}, bf16[32,512]{1,0:T(8,128)(2,1)S(1)}, u32[]{:S(2)}, u32[]{:S(2)}) collective-permute-start(bf16[32,512]{1,0:T(8,128)(2,1)} %own_ref.1), channel_id=1, source_target_pairs={{0,1},{1,0},{2,3},{3,2},{4,5},{5,4},{6,7},{7,6},{8,9},{9,8},{10,11... | collective-permute-start | bytes 98312 | tf_op jit(solution)/shard_map/ppermute | solution.py:277
  2.2 0.8 %copy-start.1 = (bf16[32,512]{1,0:T(8,128)(2,1)S(1)}, bf16[32,512]{1,0:T(8,128)(2,1)}, u32[]{:S(2)}) copy-start(bf16[32,512]{1,0:T(8,128)(2,1)} %own_ref.1) | copy-start | bytes 98308
  3.0 15.3 %copy-start.2 = (f32[3,1024]{1,0:T(4,128)S(1)}, f32[3,1024]{1,0:T(4,128)}, u32[]{:S(2)}) copy-start(f32[3,1024]{1,0:T(4,128)} %quad_ref.1) | copy-start | bytes 36868
  3.0 15.3 %copy-start.4 = (f32[1024]{0:T(1024)S(1)}, f32[1024]{0:T(1024)}, u32[]{:S(2)}) copy-start(f32[1024]{0:T(1024)} %param.13) | copy-start | bytes 12292
  3.0 15.3 %copy-start.5 = (s32[1024]{0:T(1024)S(1)}, s32[1024]{0:T(1024)}, u32[]{:S(2)}) copy-start(s32[1024]{0:T(1024)} %param.14) | copy-start | bytes 12292
  3.0 10.5 %collective-permute-start.1 = (bf16[64,512]{1,0:T(8,128)(2,1)S(1)}, bf16[64,512]{1,0:T(8,128)(2,1)S(1)}, u32[]{:S(2)}, u32[]{:S(2)}) collective-permute-start(bf16[64,512]{1,0:T(8,128)(2,1)S(1)} %shard_map.96), channel_id=1, source_target_pairs={{0,0},{1,3},{2,2},{3,1},{4,4},{5,7},{6,6},{7,5},{8,8},{9,11},{10,1... | collective-permute-start | bytes 196616 | tf_op jit(solution)/shard_map/ppermute | solution.py:280
  3.8 9.7 %collective-permute-start.4 = (bf16[64,512]{1,0:T(8,128)(2,1)S(1)}, bf16[64,512]{1,0:T(8,128)(2,1)S(1)}, u32[]{:S(2)}, u32[]{:S(2)}) collective-permute-start(bf16[64,512]{1,0:T(8,128)(2,1)S(1)} %shard_map.96), channel_id=1, source_target_pairs={{0,12},{1,15},{2,14},{3,13},{4,8},{5,11},{6,10},{7,9},{8,4},{9,7},... | collective-permute-start | bytes 196616 | tf_op jit(solution)/shard_map/ppermute | solution.py:280
  8.8 7.7 %collective-permute-start.3 = (bf16[64,512]{1,0:T(8,128)(2,1)S(1)}, bf16[64,512]{1,0:T(8,128)(2,1)S(1)}, u32[]{:S(2)}, u32[]{:S(2)}) collective-permute-start(bf16[64,512]{1,0:T(8,128)(2,1)S(1)} %shard_map.96), channel_id=1, source_target_pairs={{0,8},{1,11},{2,10},{3,9},{4,12},{5,15},{6,14},{7,13},{8,0},{9,3},... | collective-permute-start | bytes 196616 | tf_op jit(solution)/shard_map/ppermute | solution.py:280
  8.8 7.8 %collective-permute-start.2 = (bf16[64,512]{1,0:T(8,128)(2,1)S(1)}, bf16[64,512]{1,0:T(8,128)(2,1)S(1)}, u32[]{:S(2)}, u32[]{:S(2)}) collective-permute-start(bf16[64,512]{1,0:T(8,128)(2,1)S(1)} %shard_map.96), channel_id=1, source_target_pairs={{0,4},{1,7},{2,6},{3,5},{4,0},{5,3},{6,2},{7,1},{8,12},{9,15},{10,... | collective-permute-start | bytes 196616 | tf_op jit(solution)/shard_map/ppermute | solution.py:280
  10.2 0.8 %copy-start = (s32[512,3,8]{0,2,1:T(8,128)S(1)}, s32[512,3,8]{0,2,1:T(8,128)}, u32[]{:S(2)}) copy-start(s32[512,3,8]{0,2,1:T(8,128)} %param.10) | copy-start | bytes 147460
  13.5 4.0 %collective-permute-start.8 = (bf16[64,512]{1,0:T(8,128)(2,1)S(1)}, bf16[64,512]{1,0:T(8,128)(2,1)S(1)}, u32[]{:S(2)}, u32[]{:S(2)}) collective-permute-start(bf16[64,512]{1,0:T(8,128)(2,1)S(1)} %collective-permute-done.4.refs_3_), channel_id=1, source_target_pairs={{0,1},{1,0},{2,3},{3,2},{4,5},{5,4},{6,7},{7,6},{8,9},{9,8},{10,11... | collective-permute-start | bytes 196616 | tf_op jit(solution)/shard_map/ppermute | solution.py:277
  16.5 1.3 %collective-permute-start.7 = (bf16[64,512]{1,0:T(8,128)(2,1)S(1)}, bf16[64,512]{1,0:T(8,128)(2,1)S(1)}, u32[]{:S(2)}, u32[]{:S(2)}) collective-permute-start(bf16[64,512]{1,0:T(8,128)(2,1)S(1)} %collective-permute-done.3.refs_2_), channel_id=1, source_target_pairs={{0,1},{1,0},{2,3},{3,2},{4,5},{5,4},{6,7},{7,6},{8,9},{9,8},{10,11... | collective-permute-start | bytes 196616 | tf_op jit(solution)/shard_map/ppermute | solution.py:277
  16.6 1.3 %collective-permute-start.6 = (bf16[64,512]{1,0:T(8,128)(2,1)S(1)}, bf16[64,512]{1,0:T(8,128)(2,1)S(1)}, u32[]{:S(2)}, u32[]{:S(2)}) collective-permute-start(bf16[64,512]{1,0:T(8,128)(2,1)S(1)} %collective-permute-done.2.refs_1_), channel_id=1, source_target_pairs={{0,1},{1,0},{2,3},{3,2},{4,5},{5,4},{6,7},{7,6},{8,9},{9,8},{10,11... | collective-permute-start | bytes 196616 | tf_op jit(solution)/shard_map/ppermute | solution.py:277
  17.1 1.3 %collective-permute-start.5 = (bf16[64,512]{1,0:T(8,128)(2,1)S(1)}, bf16[64,512]{1,0:T(8,128)(2,1)S(1)}, u32[]{:S(2)}, u32[]{:S(2)}) collective-permute-start(bf16[64,512]{1,0:T(8,128)(2,1)S(1)} %collective-permute-done.1.refs_0_), channel_id=1, source_target_pairs={{0,1},{1,0},{2,3},{3,2},{4,5},{5,4},{6,7},{7,6},{8,9},{9,8},{10,11... | collective-permute-start | bytes 196616 | tf_op jit(solution)/shard_map/ppermute | solution.py:277
  22.7 1.6 %collective-permute-start.9 = (bf16[256,512]{1,0:T(8,128)(2,1)S(1)}, bf16[256,512]{1,0:T(8,128)(2,1)S(1)}, u32[]{:S(2)}, u32[]{:S(2)}) collective-permute-start(bf16[256,512]{1,0:T(8,128)(2,1)S(1)} %get-tuple-element.25), channel_id=1, source_target_pairs={{0,1},{1,0},{2,3},{3,2},{4,5},{5,4},{6,7},{7,6},{8,9},{9,8},{10,11... | collective-permute-start | bytes 786440 | tf_op jit(solution)/shard_map/ppermute | solution.py:277
  22.9 1.4 %collective-permute-start.10 = (f32[2,512]{1,0:T(2,128)S(1)}, f32[2,512]{1,0:T(2,128)S(1)}, u32[]{:S(2)}, u32[]{:S(2)}) collective-permute-start(f32[2,512]{1,0:T(2,128)S(1)} %get-tuple-element.23.stat_ref), channel_id=1, source_target_pairs={{0,1},{1,0},{2,3},{3,2},{4,5},{5,4},{6,7},{7,6},{8,9},{9,8},{10,11... | collective-permute-start | bytes 12296 | tf_op jit(solution)/shard_map/ppermute | solution.py:277
  24.5 5.1 %collective-permute-start.11 = (bf16[272,128]{1,0:T(8,128)(2,1)S(1)}, bf16[272,128]{1,0:T(8,128)(2,1)S(1)}, u32[]{:S(2)}, u32[]{:S(2)}) collective-permute-start(bf16[272,128]{1,0:T(8,128)(2,1)S(1)} %get-tuple-element.26), channel_id=1, source_target_pairs={{0,0},{1,3},{2,2},{3,1},{4,4},{5,7},{6,6},{7,5},{8,8},{9,11},{10,1... | collective-permute-start | bytes 208904 | tf_op jit(solution)/shard_map/ppermute | solution.py:280
  25.1 7.1 %collective-permute-start.12 = (bf16[272,128]{1,0:T(8,128)(2,1)S(1)}, bf16[272,128]{1,0:T(8,128)(2,1)S(1)}, u32[]{:S(2)}, u32[]{:S(2)}) collective-permute-start(bf16[272,128]{1,0:T(8,128)(2,1)S(1)} %get-tuple-element.27), channel_id=1, source_target_pairs={{0,4},{1,7},{2,6},{3,5},{4,0},{5,3},{6,2},{7,1},{8,12},{9,15},{10,... | collective-permute-start | bytes 208904 | tf_op jit(solution)/shard_map/ppermute | solution.py:280
  26.6 6.0 %collective-permute-start.13 = (bf16[272,128]{1,0:T(8,128)(2,1)S(1)}, bf16[272,128]{1,0:T(8,128)(2,1)S(1)}, u32[]{:S(2)}, u32[]{:S(2)}) collective-permute-start(bf16[272,128]{1,0:T(8,128)(2,1)S(1)} %get-tuple-element.28), channel_id=1, source_target_pairs={{0,8},{1,11},{2,10},{3,9},{4,12},{5,15},{6,14},{7,13},{8,0},{9,3},... | collective-permute-start | bytes 208904 | tf_op jit(solution)/shard_map/ppermute | solution.py:280
  29.2 6.2 %collective-permute-start.14 = (bf16[272,128]{1,0:T(8,128)(2,1)S(1)}, bf16[272,128]{1,0:T(8,128)(2,1)S(1)}, u32[]{:S(2)}, u32[]{:S(2)}) collective-permute-start(bf16[272,128]{1,0:T(8,128)(2,1)S(1)} %get-tuple-element.29), channel_id=1, source_target_pairs={{0,12},{1,15},{2,14},{3,13},{4,8},{5,11},{6,10},{7,9},{8,4},{9,7},... | collective-permute-start | bytes 208904 | tf_op jit(solution)/shard_map/ppermute | solution.py:280
  29.6 8.4 %collective-permute-start.15 = (bf16[272,128]{1,0:T(8,128)(2,1)S(1)}, bf16[272,128]{1,0:T(8,128)(2,1)S(1)}, u32[]{:S(2)}, u32[]{:S(2)}) collective-permute-start(bf16[272,128]{1,0:T(8,128)(2,1)S(1)} %collective-permute-done.11.refs_0_), channel_id=1, source_target_pairs={{0,1},{1,0},{2,3},{3,2},{4,5},{5,4},{6,7},{7,6},{8,9},{9,8},{10,11... | collective-permute-start | bytes 208904 | tf_op jit(solution)/shard_map/ppermute | solution.py:277
  32.2 5.8 %collective-permute-start.16 = (bf16[272,128]{1,0:T(8,128)(2,1)S(1)}, bf16[272,128]{1,0:T(8,128)(2,1)S(1)}, u32[]{:S(2)}, u32[]{:S(2)}) collective-permute-start(bf16[272,128]{1,0:T(8,128)(2,1)S(1)} %collective-permute-done.12.refs_1_), channel_id=1, source_target_pairs={{0,1},{1,0},{2,3},{3,2},{4,5},{5,4},{6,7},{7,6},{8,9},{9,8},{10,11... | collective-permute-start | bytes 208904 | tf_op jit(solution)/shard_map/ppermute | solution.py:277
  32.6 5.4 %collective-permute-start.17 = (bf16[272,128]{1,0:T(8,128)(2,1)S(1)}, bf16[272,128]{1,0:T(8,128)(2,1)S(1)}, u32[]{:S(2)}, u32[]{:S(2)}) collective-permute-start(bf16[272,128]{1,0:T(8,128)(2,1)S(1)} %collective-permute-done.13.refs_2_), channel_id=1, source_target_pairs={{0,1},{1,0},{2,3},{3,2},{4,5},{5,4},{6,7},{7,6},{8,9},{9,8},{10,11... | collective-permute-start | bytes 208904 | tf_op jit(solution)/shard_map/ppermute | solution.py:277
  35.4 3.5 %collective-permute-start.18 = (bf16[272,128]{1,0:T(8,128)(2,1)S(1)}, bf16[272,128]{1,0:T(8,128)(2,1)S(1)}, u32[]{:S(2)}, u32[]{:S(2)}) collective-permute-start(bf16[272,128]{1,0:T(8,128)(2,1)S(1)} %collective-permute-done.14.refs_3_), channel_id=1, source_target_pairs={{0,1},{1,0},{2,3},{3,2},{4,5},{5,4},{6,7},{7,6},{8,9},{9,8},{10,11... | collective-permute-start | bytes 208904 | tf_op jit(solution)/shard_map/ppermute | solution.py:277
  40.2 4.0 %collective-permute-start.19 = (f32[6,1024]{1,0:T(8,128)S(1)}, f32[6,1024]{1,0:T(8,128)S(1)}, u32[]{:S(2)}, u32[]{:S(2)}) collective-permute-start(f32[6,1024]{1,0:T(8,128)S(1)} %get-tuple-element.31), channel_id=1, source_target_pairs={{0,16},{16,0},{1,17},{17,1},{2,18},{18,2},{3,19},{19,3},{4,20},{20... | collective-permute-start | bytes 73736 | tf_op jit(solution)/shard_map/ppermute | solution.py:347

commit v5 on v2

v5 whole, which is shorter than its diff:
```python
import functools

import jax
import jax.numpy as jnp
from jax import lax
from jax.experimental import pallas as pl
from jax.experimental.pallas import tpu as pltpu
from jax.sharding import PartitionSpec as P

JB = 256
VMEM = pltpu.VMEM


def vmem_call(kernel, out_shape, scratch_shapes=(), flops=0, nbytes=0, exps=0, n_in=0, smem=(), hbm=(), limit=16):
    def place(i):
        return pltpu.SMEM if i in smem else pltpu.HBM if i in hbm else VMEM

    return pl.pallas_call(
        kernel,
        out_shape=out_shape,
        in_specs=[pl.BlockSpec(memory_space=place(i)) for i in range(n_in)],
        out_specs=jax.tree.map(lambda _: pl.BlockSpec(memory_space=VMEM), out_shape),
        scratch_shapes=list(scratch_shapes),
        cost_estimate=pl.CostEstimate(flops=flops, bytes_accessed=nbytes, transcendentals=exps),
        compiler_params=pltpu.CompilerParams(vmem_limit_bytes=limit << 20),
    )


def to_lanes(column, rows):
    step = min(rows, 128)
    parts = []
    for at in range(0, rows, step):
        square = jnp.broadcast_to(column[at : at + step], (step, 128))
        parts.append(jnp.transpose(square)[0:1, :])
    return jnp.concatenate(parts, axis=1)


def to_rows(row, at):
    return jnp.transpose(jnp.broadcast_to(row[:, at : at + 128], (128, 128)))


def swap_lanes(x, which, width, n):
    lane = lax.broadcasted_iota(jnp.int32, x.shape, 1)
    bit = 1
    while bit < n:
        step = bit * width
        ahead = jnp.concatenate([x[:, step:], x[:, :step]], axis=1)
        behind = jnp.concatenate([x[:, -step:], x[:, :-step]], axis=1)
        other = jnp.where((lane & step) != 0, behind, ahead)
        x = jnp.where((which & bit) != 0, other, x)
        bit *= 2
    return x


def swap_halves(x):
    half = x.shape[1] // 2
    return jnp.concatenate([x[:, half:], x[:, :half]], axis=1)


def block_kernel(*refs):
    out_ref = refs[-1]
    values = [ref[...].astype(jnp.float32) for ref in refs[:-1]]
    out_ref[...] = jnp.concatenate(values, axis=0).astype(jnp.bfloat16)


def prep_kernel(n, me_ref, mant_hbm, exp_hbm, cot_ref, out_ref, cot_out_ref, mant, expo, sems):
    comps, units, width = mant.shape
    blocks = expo.shape[1]
    span = width // blocks
    copies = [pltpu.make_async_copy(exp_hbm, expo, sems.at[comps])]
    copies += [pltpu.make_async_copy(mant_hbm.at[k], mant.at[k], sems.at[k]) for k in range(comps)]
    for copy in copies:
        copy.start()
    cases = cot_ref.shape[1]
    rows = cases // n
    nz = n // 4
    order = [z * 4 + y * 2 + c for c in range(2) for y in range(2) for z in range(nz)]
    cot = jnp.concatenate([cot_ref[:, e * rows : (e + 1) * rows] for e in order], axis=1)
    code = (me_ref[0] & 1) * (2 * nz) + ((me_ref[0] >> 1) & 1) * nz + (me_ref[0] >> 2)
    cot = jnp.broadcast_to(cot, (8, cases))
    cot_out_ref[...] = swap_lanes(cot, jnp.full((8, cases), code, jnp.int32), rows, n)[0:1]
    copies[0].wait()
    factor = jnp.exp2(expo[...].astype(jnp.float32)).reshape(comps * blocks, units)
    pad = jnp.zeros((128 - comps * blocks, units), jnp.float32)
    columns = jnp.transpose(jnp.concatenate([factor, pad], axis=0))
    for k in range(comps):
        copies[1 + k].wait()
        for b in range(blocks):
            gain = jnp.broadcast_to(columns[:, k * blocks + b : k * blocks + b + 1], (units, span))
            value = mant[k, :, b * span : (b + 1) * span] * gain.astype(jnp.bfloat16)
            first = b * span
            at = (first // JB) * (comps * JB) + k * JB + first % JB
            out_ref[:, at : at + span] = value


def main_kernel(n_rows, n_stat, f_ref, lin_ref, quad_ref, cross_ref, ply_ref, *refs):
    row_refs, stat_refs = refs[:n_rows], refs[n_rows : n_rows + n_stat]
    term_refs = refs[n_rows + n_stat : 2 * n_rows + n_stat]
    stat_ref, s_ref, w_ref, a_ref, idx, d, acc = refs[2 * n_rows + n_stat :]
    cases = a_ref.shape[0]
    width = w_ref.shape[1]
    at = 0
    for ref in row_refs:
        a_ref[at : at + ref.shape[0], :] = ref[...]
        at += ref.shape[0]
    tile = 32
    peak = jnp.full((cases, 128), -jnp.inf, jnp.float32)
    for jb in range(width // JB):
        cols = slice(jb * JB, (jb + 1) * JB)
        base = jb * 3 * JB
        s_ref[:, base : base + 3 * JB] = jnp.dot(
            a_ref[...], f_ref[:, base : base + 3 * JB], preferred_element_type=jnp.float32
        )
        f1, f2 = lin_ref[0:1, cols], lin_ref[1:2, cols]
        f11, f22, f66 = quad_ref[0:1, cols], quad_ref[1:2, cols], quad_ref[2:3, cols]
        f12 = 2.0 * cross_ref[0:1, cols]
        tops = []
        for at in range(0, cases, tile):
            r = slice(at, at + tile)
            s1 = s_ref[r, base : base + JB]
            s2 = s_ref[r, base + JB : base + 2 * JB]
            t = s_ref[r, base + 2 * JB : base + 3 * JB]
            index = s1 * (f1 + f11 * s1 + f12 * s2) + s2 * (f2 + f22 * s2) + f66 * (t * t)
            idx[r, cols] = index
            top = index[:, 0:128]
            for c in range(128, JB, 128):
                top = jnp.maximum(top, index[:, c : c + 128])
            tops.append(top)
        peak = jnp.maximum(peak, jnp.concatenate(tops, axis=0))
    peak = jnp.max(peak, axis=1, keepdims=True)

    total = jnp.zeros((cases, 128), jnp.float32)
    for jb in range(width // JB):
        cols = slice(jb * JB, (jb + 1) * JB)
        base = jb * 3 * JB
        f1, f2 = lin_ref[0:1, cols], lin_ref[1:2, cols]
        q11, q22, q66 = 2.0 * quad_ref[0:1, cols], 2.0 * quad_ref[1:2, cols], 2.0 * quad_ref[2:3, cols]
        f12 = 2.0 * cross_ref[0:1, cols]
        plies = (ply_ref[0:1, cols] + 1).astype(jnp.float32)
        sums = []
        for at in range(0, cases, tile):
            r = slice(at, at + tile)
            s1 = s_ref[r, base : base + JB]
            s2 = s_ref[r, base + JB : base + 2 * JB]
            t = s_ref[r, base + 2 * JB : base + 3 * JB]
            w = plies * jnp.exp(idx[r, cols] - peak[r])
            w_ref[r, cols] = w
            part = w[:, 0:128]
            for c in range(128, JB, 128):
                part = part + w[:, c : c + 128]
            sums.append(part)
            d[r, base : base + JB] = (w * (f1 + q11 * s1 + f12 * s2)).astype(jnp.bfloat16)
            d[r, base + JB : base + 2 * JB] = (w * (f2 + q22 * s2 + f12 * s1)).astype(jnp.bfloat16)
            d[r, base + 2 * JB : base + 3 * JB] = (w * (q66 * t)).astype(jnp.bfloat16)
        total = total + jnp.concatenate(sums, axis=0)
        part = lax.dot_general(
            d[:, base : base + 3 * JB],
            f_ref[:, base : base + 3 * JB],
            (((1,), (1,)), ((), ())),
            preferred_element_type=jnp.float32,
        )
        if jb == 0:
            acc[...] = part
        elif jb < width // JB - 1:
            acc[...] += part
        else:
            total = jnp.sum(total, axis=1, keepdims=True)
            part = (acc[...] + part) * (1.0 / total)
            at = 0
            for ref in term_refs:
                ref[...] = part[at : at + ref.shape[0]].astype(ref.dtype)
                at += ref.shape[0]
    lines = [to_lanes(peak, cases), to_lanes(peak + jnp.log(total), cases)]
    at = 0
    for ref in stat_refs:
        at += ref.shape[1]
    if stat_refs:
        quarter = cases
        first, second = stat_refs
        stat_ref[:, 0:quarter] = first[:, 0:quarter]
        stat_ref[:, quarter : 2 * quarter] = second[...]
        stat_ref[:, 2 * quarter : 3 * quarter] = first[:, quarter : 2 * quarter]
        at = 3 * quarter
    stat_ref[0:1, at : at + cases] = lines[0]
    stat_ref[1:2, at : at + cases] = lines[1]


def join(a, b):
    top = jnp.maximum(a, b)
    return top + jnp.log(jnp.exp(a - top) + jnp.exp(b - top))


def encode(env):
    groups = env.shape[1] // 128
    lines = jnp.concatenate([env[:, g * 128 : (g + 1) * 128] for g in range(groups)], axis=0)
    high = lines.astype(jnp.bfloat16).astype(jnp.float32)
    middle = (lines - high).astype(jnp.bfloat16).astype(jnp.float32)
    rest = jnp.zeros((16 - 3 * groups, 128), jnp.float32)
    return jnp.concatenate([high, middle, lines - high - middle, rest], axis=0).astype(jnp.bfloat16)


def decode(ref, cases):
    size, groups = ref.shape[0] - 16, cases // 128
    lines = ref[size : size + 16, :].astype(jnp.float32)
    lines = lines[0:groups] + lines[groups : 2 * groups] + lines[2 * groups : 3 * groups]
    return jnp.concatenate([lines[g : g + 1] for g in range(groups)], axis=1)


def fold(x):
    return jnp.concatenate([x[:, c : c + 128] for c in range(0, x.shape[1], 128)], axis=0)


def cores_kernel(own_ref, got_ref, stat_ref, twin_ref, out_ref):
    quarter = own_ref.shape[0]
    cases = 4 * quarter
    mine, theirs = stat_ref[1:2, :], swap_halves(twin_ref[1:2, :])
    env = join(mine, theirs)
    r = slice(quarter, 2 * quarter)
    up = column(jnp.exp(mine - env)[:, r], quarter)
    down = column(jnp.exp(theirs - env)[:, r], quarter)
    value = own_ref[...] * up + got_ref[...].astype(jnp.float32) * down
    size = out_ref.shape[0] - 16
    out_ref[0:size, :] = fold(value).astype(jnp.bfloat16)
    out_ref[size : size + 16, :] = encode(env)


def column(row, rows):
    return jnp.concatenate([to_rows(row, at)[:, 0:1] for at in range(0, rows, 128)], axis=0)


def chips_kernel(own_ref, got_ref, stat_ref, twin_ref, part_ref, own_out_ref, env_ref, *out_refs):
    quarter, units = own_ref.shape
    cases = 4 * quarter
    rows = quarter // (1 + len(out_refs))
    mine, theirs = stat_ref[1:2, :], swap_halves(twin_ref[1:2, :])
    far = decode(part_ref, cases)
    far = jnp.concatenate([far[:, g * quarter : (g + 1) * quarter] for g in (1, 0, 3, 2)], axis=1)
    env = join(join(mine, theirs), far)
    env_ref[...] = env
    scale = [column(jnp.exp(x - env)[:, 0:quarter], quarter) for x in (mine, theirs, far)]
    total = own_ref[...] * scale[0] + got_ref[...].astype(jnp.float32) * scale[1]
    parts = []
    for c in range(units // 128):
        part = part_ref[c * quarter : (c + 1) * quarter, :].astype(jnp.float32)
        parts.append(total[:, c * 128 : (c + 1) * 128] + part * scale[2])
    own_out_ref[...] = jnp.concatenate([p[0:rows] for p in parts], axis=0)
    tail = encode(env)
    for m, ref in enumerate(out_refs):
        r = slice((m + 1) * rows, (m + 2) * rows)
        size = ref.shape[0] - 16
        ref[0:size, :] = jnp.concatenate([p[r] for p in parts], axis=0).astype(jnp.bfloat16)
        ref[size : size + 16, :] = tail


def coef_kernel(cot_ref, stat_ref, env_ref, s0_ref, s1_ref, s2_ref, w0_ref, w1_ref, w2_ref, *refs):
    coef_ref, gain_ref = refs[-2:]
    part_refs = refs[:-2]
    nz = 1 + len(part_refs)
    cases = cot_ref.shape[1]
    quarter = cases // 4
    rows = quarter // nz
    width = w0_ref.shape[1]
    envs = [env_ref[...]] + [decode(ref, cases) for ref in part_refs]
    pad = -nz % 8
    env_all = jnp.concatenate(envs + [envs[0]] * pad, axis=0)
    which = lax.broadcasted_iota(jnp.int32, env_all.shape, 0)
    env_all = swap_lanes(env_all, jnp.where(which < nz, which, 0), rows, nz)[0:nz]
    top = jnp.max(env_all, axis=0, keepdims=True)
    env = top + jnp.log(jnp.sum(jnp.exp(env_all - top), axis=0, keepdims=True))
    cot = cot_ref[...]
    gain = cot[:, 0:128] * jnp.exp(env_all[:, 0:128] - env[:, 0:128])
    fill = jnp.zeros((128 - nz, 128), jnp.float32)
    gain_ref[...] = jnp.transpose(jnp.concatenate([gain, fill], axis=0))[0:rows]
    scale = cot * jnp.exp(stat_ref[0:1, :] - env)
    scales = [to_rows(scale, at) for at in range(0, cases, 128)]
    sets = [
        (0, s0_ref, w0_ref, 0),
        (quarter, s1_ref, w1_ref, 0),
        (2 * quarter, s0_ref, w0_ref, quarter),
        (3 * quarter, s2_ref, w2_ref, 0),
    ]
    for jb in range(width // JB):
        base = jb * 3 * JB
        for c in range(0, JB, 128):
            sums = [jnp.zeros((8, 128), jnp.float32) for _ in range(6)]
            for here, s_ref, w_ref, there in sets:
                for at in range(0, quarter, 8):
                    r = slice(there + at, there + at + 8)
                    s1 = s_ref[r, base + c : base + c + 128]
                    s2 = s_ref[r, base + JB + c : base + JB + c + 128]
                    t = s_ref[r, base + 2 * JB + c : base + 2 * JB + c + 128]
                    place = here + at
                    gain = scales[place // 128][place % 128 : place % 128 + 8]
                    w = w_ref[r, jb * JB + c : jb * JB + c + 128] * gain
                    a, b = w * s1, w * s2
                    for i, v in enumerate((a, b, a * s1, b * s2, w * t * t, a * s2)):
                        sums[i] = sums[i] + v
            for i in range(6):
                line = jnp.sum(sums[i], axis=0, keepdims=True)
                if i == 5:
                    line = 2.0 * line
                coef_ref[i : i + 1, jb * JB + c : jb * JB + c + 128] = line


def combine_kernel(gain_ref, own_ref, *refs):
    part_refs, out_ref = refs[:-1], refs[-1]
    rows, units = out_ref.shape
    size = rows * units // 128
    for c in range(units // 128):
        r = slice(c * rows, (c + 1) * rows)
        value = own_ref[r, :] * gain_ref[:, 0:1]
        for m, ref in enumerate(part_refs):
            part = ref[0:size, :].astype(jnp.float32)[r]
            value = value + part * gain_ref[:, m + 1 : m + 2]
        out_ref[:, c * 128 : (c + 1) * 128] = value


def per_device(n, n_case, load_coef, mantissa, scale_exp, lin_coef, quad_coef, cross_coef, ply_count, cotangent):
    units, comps, width = mantissa.shape
    rows = load_coef.shape[0]
    cases = rows * n
    nz = n // 4
    quarter = rows * nz
    f32, bf16 = jnp.float32, jnp.bfloat16
    shape = jax.ShapeDtypeStruct
    me = lax.axis_index("elem").astype(jnp.int32).reshape(1)

    def along(bits, x):
        return lax.ppermute(x, "elem", [(i, i ^ bits) for i in range(n)])

    along_z = [along(4 * m, load_coef) for m in range(1, nz)]
    fields, cot = vmem_call(
        functools.partial(prep_kernel, n),
        [shape((units, comps * width), bf16), shape((1, cases), f32)],
        scratch_shapes=[
            VMEM((comps, units, width), bf16),
            VMEM((comps, scale_exp.shape[2], units), jnp.int32),
            pltpu.SemaphoreType.DMA((comps + 1,)),
        ],
        flops=units * comps * width,
        nbytes=4 * units * comps * width,
        n_in=4,
        smem=(0,),
        hbm=(1, 2),
    )(
        me,
        pltpu.with_memory_space_constraint(jnp.transpose(mantissa, (1, 0, 2)), pltpu.HBM),
        pltpu.with_memory_space_constraint(jnp.transpose(scale_exp, (1, 2, 0)), pltpu.HBM),
        cotangent.reshape(1, cases),
    )
    along_z[0], fields = lax.optimization_barrier((along_z[0], fields))
    near = vmem_call(block_kernel, shape((quarter, units), bf16), nbytes=4 * quarter * units, n_in=nz)(
        load_coef, *along_z
    )
    far = along(2, near)
    near_twin, far_twin = along(1, near), along(1, far)

    def main(blocks, dtypes, stats=()):
        count = len(blocks) * quarter
        outs = vmem_call(
            functools.partial(main_kernel, len(blocks), len(stats)),
            [shape((quarter, units), dtype) for dtype in dtypes]
            + [
                shape((2, cases if stats else count), f32),
                shape((count, comps * width), f32),
                shape((count, width), f32),
            ],
            scratch_shapes=[
                VMEM((count, units), bf16),
                VMEM((count, width), f32),
                VMEM((count, comps * width), bf16),
                VMEM((count, units), f32),
            ],
            flops=4 * count * units * comps * width,
            nbytes=2 * units * comps * width + 4 * count * 4 * width,
            exps=count * width,
            n_in=5 + len(blocks) + len(stats),
            limit=24,
        )(
            fields,
            lin_coef,
            quad_coef,
            cross_coef.reshape(1, width),
            ply_count.reshape(1, width),
            *blocks,
            *stats,
        )
        return outs

    near_own, near_send, stat0, s0, w0 = main([near, near_twin], [f32, bf16])
    near_got = along(1, near_send)
    far_own, stat1, s1, w1 = main([far], [f32])
    far_send, stat, s2, w2 = main([far_twin], [bf16], [stat0, stat1])
    far_got = along(1, far_send)
    stat_twin = along(1, stat)

    chunk = vmem_call(
        cores_kernel,
        shape((quarter * units // 128 + 16, 128), bf16),
        flops=4 * quarter * units,
        nbytes=8 * quarter * units,
        n_in=4,
    )(far_own, far_got, stat, stat_twin)
    part = along(2, chunk)
    outs = vmem_call(
        chips_kernel,
        [shape((rows * units // 128, 128), f32), shape((1, cases), f32)]
        + [shape((rows * units // 128 + 16, 128), bf16)] * (nz - 1),
        flops=6 * quarter * units,
        nbytes=10 * quarter * units,
        n_in=5,
    )(near_own, near_got, stat, stat_twin, part)
    own, env = outs[:2]
    parts = [along(4 * m, x) for m, x in enumerate(outs[2:], start=1)]

    coef, gain = vmem_call(
        coef_kernel,
        [shape((6, width), f32), shape((rows, 128), f32)],
        flops=14 * cases * width,
        nbytes=16 * cases * width,
        n_in=9 + len(parts),
    )(cot, stat, env, s0, s1, s2, w0, w1, w2, *parts)
    bit = 1
    while bit < n_case:
        coef = coef + lax.ppermute(coef, "case", [(i, i ^ bit) for i in range(n_case)])
        bit *= 2

    load_grad = vmem_call(
        combine_kernel,
        shape((rows, units), f32),
        flops=2 * nz * rows * units,
        nbytes=2 * nz * rows * units,
        n_in=2 + len(parts),
    )(gain, own, *parts)
    return (load_grad, coef)


def solution(mesh):
    n, n_case = mesh.shape["elem"], mesh.shape["case"]
    return jax.shard_map(
        functools.partial(per_device, n, n_case),
        mesh=mesh,
        in_specs=(
            P(("case", "elem"), None),
            P(None, None, "elem"),
            P(None, None, "elem"),
            P(None, "elem"),
            P(None, "elem"),
            P("elem"),
            P("elem"),
            P("case"),
        ),
        out_specs=(P(("case", "elem"), None), P(None, "elem")),
        check_vma=False,
    )
```

time: 64.4 us -> 45.6 us (0.71)
  local copies, waits for them, and re-layouts: 13.5 us -> 0.7 us
  blocking collectives: 10.8 us -> 0 us
  Pallas kernels: 8.24 us -> 11.7 us
  starting transfers between devices: 12.6 us -> 15.5 us
  waiting for transfers between devices: 17.3 us -> 16.1 us
    all_to_all x2 -> x0, waiting for transfers between devices: 14.8 us -> none  [the longest x1 10.8 us: per_device(): gathered = lax.all_to_all(copies, 'elem', 0, 0).reshape(cases, units)]
    ppermute x0 -> x13, waiting for transfers between devices: none -> 14.5 us  [along(): return lax.ppermute(x, 'elem', [(i, i ^ bits) for i in range(n)])]
    ppermute x0 -> x13, starting transfers between devices: none -> 13.9 us  [along(): return lax.ppermute(x, 'elem', [(i, i ^ bits) for i in range(n)])]
    unnamed x24 -> x12, local copies, waits for them, and re-layouts: 11.9 us -> 0.7 us
    all_to_all x2 -> x0, starting transfers between devices: 11 us -> none  [the longest x1 7.44 us: per_device(): gathered = lax.all_to_all(copies, 'elem', 0, 0).reshape(cases, units)]
    all_to_all x1 -> x0, blocking collectives: 10.8 us -> none  [per_device(): stats = lax.all_to_all(stat, 'elem', 0, 0)]
    pallas_call x4 -> x9, Pallas kernels: 8.24 us -> 11.7 us  [the longest x3 6.44 us: main(): vmem_call(functools.partial(main_kernel, len(blocks), len(stats)), [shape...]
    broadcast_in_dim x1 -> x0, local copies, waits for them, and re-layouts: 1.61 us -> none  [per_device(): copies = jnp.broadcast_to(load_coef[None], (n, rows, units))]
  transfers between devices with their start and end apart: 3 -> 14, of which waited for: 3 -> 8; matrix products, arithmetic and copies ran while one was open for 1% -> 0% of each run, Pallas kernels for 4% -> 17%
where the time goes in v5:
time: 45.6 us; the launch traced here: 45.4 us
  waiting for transfers between devices  16.1 us (35%)
  starting transfers between devices  15.5 us (34%)
  Pallas kernels  11.7 us (26%)
  between operations  0.8 us (2%)
  local copies, waits for them, and re-layouts  0.7 us (2%)
  other arithmetic  0.62 us (1%)
    ppermute x13, waiting for transfers between devices, along(): return lax.ppermute(x, 'elem', [(i, i ^ bits) for i in range(n)])  14.5 us
    ppermute x13, starting transfers between devices, along(): return lax.ppermute(x, 'elem', [(i, i ^ bits) for i in range(n)])  13.9 us
    pallas_call x3, Pallas kernels, main(): vmem_call(functools.partial(main_kernel, len(blocks), len(stats)), [shape...  6.44 us
    pallas_call x1, Pallas kernels, per_device(): vmem_call(functools.partial(prep_kernel, n), [shape((units, comps * width...  2.46 us
    ppermute x1, waiting for transfers between devices, per_device(): lax.ppermute(coef, 'case', [(i, i ^ bit) for i in range(n_case)])  1.62 us
    ppermute x1, starting transfers between devices, per_device(): lax.ppermute(coef, 'case', [(i, i ^ bit) for i in range(n_case)])  1.58 us
    pallas_call x1, Pallas kernels, per_device(): vmem_call(coef_kernel, [shape((6, width), f32), shape((rows, 128), f32)],...  1.53 us
  transfers between devices with their start and end apart: 14, of which 8 were waited for; matrix products, arithmetic and copies ran while one was open for 0% of the time, Pallas kernels for 17%

profile of v5, /device:TPU:0, one launch (start us, length us, event | category | flops | bytes accessed | tf_op | source)
XLA Modules:
  0.0 45.4 jit_solution(12421289867786342614)
XLA Ops:
  0.6 0.0 copy-start.2
  0.6 0.0 copy-start
  0.7 0.0 copy-start.1
  0.7 0.0 copy-start.4
  0.7 0.0 copy-start.3
  0.7 3.1 %collective-permute-start = (bf16[32,512]{1,0:T(8,128)(2,1)}, bf16[32,512]{1,0:T(8,128)(2,1)S(1)}, u32[]{:S(2)}, u32[]{:S(2)}) collective-permute-start(bf16[32,512]{1,0:T(8,128)(2,1)} %refs_0_.1), channel_id=1, source_target_pairs={{0,4},{1,5},{2,6},{3,7},{4,0},{5,1},{6,2},{7,3},{8,12},{9,13},{10,... | collective-permute-start | bytes 98312 | tf_op jit(solution)/shard_map/ppermute | solution.py:329
  3.8 2.6 %collective-permute-start.1 = (bf16[32,512]{1,0:T(8,128)(2,1)}, bf16[32,512]{1,0:T(8,128)(2,1)S(1)}, u32[]{:S(2)}, u32[]{:S(2)}) collective-permute-start(bf16[32,512]{1,0:T(8,128)(2,1)} %refs_0_.1), channel_id=1, source_target_pairs={{0,8},{1,9},{2,10},{3,11},{4,12},{5,13},{6,14},{7,15},{8,0},{9,1},... | collective-permute-start | bytes 98312 | tf_op jit(solution)/shard_map/ppermute | solution.py:329
  6.4 0.0 collective-permute-start.2
  6.4 0.0 copy-start.5
  6.4 0.7 %copy-done.5 = f32[512]{0:T(512)S(1)} copy-done((f32[512]{0:T(512)S(1)}, f32[512]{0:T(512)}, u32[]{:S(2)}) %copy-start.5) | copy-done | bytes 2072
  7.0 2.5 %shard_map.95 = (bf16[512,3072]{1,0:T(8,128)(2,1)S(1)}, f32[1,512]{1,0:T(1,128)S(1)}) custom-call(s32[1]{0:T(128)} %bitcast.me_ref, bf16[3,512,1024]{2,1,0:T(8,128)(2,1)} %bitcast.13, s32[3,8,512]{2,1,0:T(8,128)} %bitcast.14, f32[1,512]{1,0:T(1,128)S(1)} %bitcast.12), custom_call_target="tpu_custom_call" | custom-call | flops 1572864 | bytes 6291456 | tf_op jit(solution)/shard_map/pallas_call | solution.py:332
  9.5 0.0 collective-permute-done.refs_1_
  9.5 0.0 collective-permute-done.1.refs_2_
  9.5 2.7 %collective-permute-done.2.refs_3_ = bf16[32,512]{1,0:T(8,128)(2,1)S(1)} collective-permute-done((bf16[32,512]{1,0:T(8,128)(2,1)}, bf16[32,512]{1,0:T(8,128)(2,1)S(1)}, u32[]{:S(2)}, u32[]{:S(2)}) %collective-permute-start.2) | collective-permute-done | bytes 32800 | tf_op jit(solution)/shard_map/ppermute | solution.py:329
  12.3 0.0 copy-done.2
  12.3 1.6 %collective-permute-start.3 = (bf16[128,512]{1,0:T(8,128)(2,1)S(1)}, bf16[128,512]{1,0:T(8,128)(2,1)S(1)}, u32[]{:S(2)}, u32[]{:S(2)}) collective-permute-start(bf16[128,512]{1,0:T(8,128)(2,1)S(1)} %shard_map.96.refs_0_), channel_id=1, source_target_pairs={{0,2},{1,3},{2,0},{3,1},{4,6},{5,7},{6,4},{7,5},{8,10},{9,11},{10,... | collective-permute-start | bytes 393224 | tf_op jit(solution)/shard_map/ppermute | solution.py:329
  13.9 0.0 collective-permute-start.5
  13.9 3.4 %collective-permute-done.3.refs_0_ = bf16[128,512]{1,0:T(8,128)(2,1)S(1)} collective-permute-done((bf16[128,512]{1,0:T(8,128)(2,1)S(1)}, bf16[128,512]{1,0:T(8,128)(2,1)S(1)}, u32[]{:S(2)}, u32[]{:S(2)}) %collective-permute-start.3) | collective-permute-done | bytes 131104 | tf_op jit(solution)/shard_map/ppermute | solution.py:329
  17.3 0.0 collective-permute-start.4
  17.3 0.0 copy-done
  17.3 0.0 copy-done.1
  17.3 0.0 copy-done.4
  17.4 0.0 copy-done.3
  17.4 2.0 %shard_map.98 = (f32[128,512]{1,0:T(8,128)S(1)}, f32[2,128]{1,0:T(2,128)S(1)}, f32[128,3072]{1,0:T(8,128)S(1)}, f32[128,1024]{1,0:T(8,128)S(1)}) custom-call(bf16[512,3072]{1,0:T(8,128)(2,1)S(1)} %get-tuple-element.28.f_ref, f32[2,1024]{1,0:T(2,128)S(1)} %copy-done.1, f32[3,1024]{1,0:T(4,128)S(1)} %copy-done, f32[1,1024]{1,0:T(1,128)S(1)} %bitcast.6, ...), custom_call_target="tpu_custom_call" | custom-call | flops 805306368 | bytes 5242880 | tf_op jit(solution)/shard_map/pallas_call | solution.py:360
  19.4 0.0 collective-permute-done.5.refs_1_
  19.4 2.4 %shard_map.97 = (f32[128,512]{1,0:T(8,128)S(1)}, bf16[128,512]{1,0:T(8,128)(2,1)S(1)}, f32[2,256]{1,0:T(2,128)S(1)}, f32[256,3072]{1,0:T(8,128)S(1)}, f32[256,1024]{1,0:T(8,128)S(1)}) custom-call(bf16[512,3072]{1,0:T(8,128)(2,1)S(1)} %get-tuple-element.28.f_ref, f32[2,1024]{1,0:T(2,128)S(1)} %copy-done.1, f32[3,1024]{1,0:T(4,128)S(1)} %copy-done, ...), custom_call_target="tpu_custom_call" | custom-call | flops 1610612736 | bytes 7340032 | tf_op jit(solution)/shard_map/pallas_call | solution.py:360
  21.9 0.0 collective-permute-done.4.refs_0_
  21.9 2.0 %shard_map.99 = (bf16[128,512]{1,0:T(8,128)(2,1)S(1)}, f32[2,512]{1,0:T(2,128)S(1)}, f32[128,3072]{1,0:T(8,128)S(1)}, f32[128,1024]{1,0:T(8,128)S(1)}) custom-call(bf16[512,3072]{1,0:T(8,128)(2,1)S(1)} %get-tuple-element.28.f_ref, f32[2,1024]{1,0:T(2,128)S(1)} %copy-done.1, f32[3,1024]{1,0:T(4,128)S(1)} %copy-done, f32[1,1024]{1,0:T(1,128)S(1)} %bitcast.8, ...), custom_call_target="tpu_custom_call" | custom-call | flops 805306368 | bytes 5242880 | tf_op jit(solution)/shard_map/pallas_call | solution.py:360
  23.8 0.5 %collective-permute-start.8 = (bf16[128,512]{1,0:T(8,128)(2,1)S(1)}, bf16[128,512]{1,0:T(8,128)(2,1)S(1)}, u32[]{:S(2)}, u32[]{:S(2)}) collective-permute-start(bf16[128,512]{1,0:T(8,128)(2,1)S(1)} %get-tuple-element.36), channel_id=1, source_target_pairs={{0,1},{1,0},{2,3},{3,2},{4,5},{5,4},{6,7},{7,6},{8,9},{9,8},{10,11... | collective-permute-start | bytes 393224 | tf_op jit(solution)/shard_map/ppermute | solution.py:329
  24.4 0.1 collective-permute-start.7
  24.5 1.1 %collective-permute-done.7.twin_ref = f32[2,512]{1,0:T(2,128)S(1)} collective-permute-done((f32[2,512]{1,0:T(2,128)S(1)}, f32[2,512]{1,0:T(2,128)S(1)}, u32[]{:S(2)}, u32[]{:S(2)}) %collective-permute-start.7) | collective-permute-done | bytes 4128 | tf_op jit(solution)/shard_map/ppermute | solution.py:329
  25.6 0.0 collective-permute-done.8.got_ref
  25.6 0.2 shard_map.100
  25.8 1.6 %collective-permute-start.9 = (bf16[528,128]{1,0:T(8,128)(2,1)S(1)}, bf16[528,128]{1,0:T(8,128)(2,1)S(1)}, u32[]{:S(2)}, u32[]{:S(2)}) collective-permute-start(bf16[528,128]{1,0:T(8,128)(2,1)S(1)} %shard_map.100), channel_id=1, source_target_pairs={{0,2},{1,3},{2,0},{3,1},{4,6},{5,7},{6,4},{7,5},{8,10},{9,11},{10,... | collective-permute-start | bytes 405512 | tf_op jit(solution)/shard_map/ppermute | solution.py:329
  27.4 0.0 collective-permute-start.6
  27.4 1.3 %collective-permute-done.6.got_ref = bf16[128,512]{1,0:T(8,128)(2,1)S(1)} collective-permute-done((bf16[128,512]{1,0:T(8,128)(2,1)S(1)}, bf16[128,512]{1,0:T(8,128)(2,1)S(1)}, u32[]{:S(2)}, u32[]{:S(2)}) %collective-permute-start.6) | collective-permute-done | bytes 131104 | tf_op jit(solution)/shard_map/ppermute | solution.py:329
  28.7 2.8 %collective-permute-done.9.part_ref = bf16[528,128]{1,0:T(8,128)(2,1)S(1)} collective-permute-done((bf16[528,128]{1,0:T(8,128)(2,1)S(1)}, bf16[528,128]{1,0:T(8,128)(2,1)S(1)}, u32[]{:S(2)}, u32[]{:S(2)}) %collective-permute-start.9) | collective-permute-done | bytes 135200 | tf_op jit(solution)/shard_map/ppermute | solution.py:329
  31.5 0.3 shard_map.101
  31.8 0.1 collective-permute-start.10
  31.9 1.6 %collective-permute-start.11 = (bf16[144,128]{1,0:T(8,128)(2,1)S(1)}, bf16[144,128]{1,0:T(8,128)(2,1)S(1)}, u32[]{:S(2)}, u32[]{:S(2)}) collective-permute-start(bf16[144,128]{1,0:T(8,128)(2,1)S(1)} %get-tuple-element.45), channel_id=1, source_target_pairs={{0,8},{1,9},{2,10},{3,11},{4,12},{5,13},{6,14},{7,15},{8,0},{9,1},... | collective-permute-start | bytes 110600 | tf_op jit(solution)/shard_map/ppermute | solution.py:329
  33.6 2.7 %collective-permute-start.12 = (bf16[144,128]{1,0:T(8,128)(2,1)S(1)}, bf16[144,128]{1,0:T(8,128)(2,1)S(1)}, u32[]{:S(2)}, u32[]{:S(2)}) collective-permute-start(bf16[144,128]{1,0:T(8,128)(2,1)S(1)} %get-tuple-element.46), channel_id=1, source_target_pairs={{0,12},{1,13},{2,14},{3,15},{4,8},{5,9},{6,10},{7,11},{8,4},{9,5},... | collective-permute-start | bytes 110600 | tf_op jit(solution)/shard_map/ppermute | solution.py:329
  36.3 0.0 collective-permute-done.10.refs_0_
  36.3 0.6 %collective-permute-done.11.refs_1_ = bf16[144,128]{1,0:T(8,128)(2,1)S(1)} collective-permute-done((bf16[144,128]{1,0:T(8,128)(2,1)S(1)}, bf16[144,128]{1,0:T(8,128)(2,1)S(1)}, u32[]{:S(2)}, u32[]{:S(2)}) %collective-permute-start.11) | collective-permute-done | bytes 36896 | tf_op jit(solution)/shard_map/ppermute | solution.py:329
  36.8 2.5 %collective-permute-done.12.refs_2_ = bf16[144,128]{1,0:T(8,128)(2,1)S(1)} collective-permute-done((bf16[144,128]{1,0:T(8,128)(2,1)S(1)}, bf16[144,128]{1,0:T(8,128)(2,1)S(1)}, u32[]{:S(2)}, u32[]{:S(2)}) %collective-permute-start.12) | collective-permute-done | bytes 36896 | tf_op jit(solution)/shard_map/ppermute | solution.py:329
  39.3 1.5 %shard_map.102 = (f32[6,1024]{1,0:T(8,128)S(1)}, f32[32,128]{1,0:T(8,128)S(1)}) custom-call(f32[1,512]{1,0:T(1,128)S(1)} %get-tuple-element.26.cot_ref, f32[2,512]{1,0:T(2,128)S(1)} %get-tuple-element.32.stat_ref, f32[1,512]{1,0:T(1,128)S(1)} %get-tuple-element.37.env_ref, f32[256,3072]{1,0:T(8,128)S(1)} %get-tuple-element.38.s0_ref, ...), custom_call_target="tpu_custom_call" | custom-call | flops 7340032 | bytes 8388608 | tf_op jit(solution)/shard_map/pallas_call | solution.py:416
  40.8 1.6 %collective-permute-start.13 = (f32[6,1024]{1,0:T(8,128)S(1)}, f32[6,1024]{1,0:T(8,128)S(1)}, u32[]{:S(2)}, u32[]{:S(2)}) collective-permute-start(f32[6,1024]{1,0:T(8,128)S(1)} %get-tuple-element.49), channel_id=1, source_target_pairs={{0,16},{16,0},{1,17},{17,1},{2,18},{18,2},{3,19},{19,3},{4,20},{20... | collective-permute-start | bytes 73736 | tf_op jit(solution)/shard_map/ppermute | solution.py:425
  42.4 0.8 %shard_map.103 = f32[32,512]{1,0:T(8,128)} custom-call(f32[32,128]{1,0:T(8,128)S(1)} %get-tuple-element.47.gain_ref, f32[128,128]{1,0:T(8,128)S(1)} %get-tuple-element.48.own_ref, bf16[144,128]{1,0:T(8,128)(2,1)S(1)} %collective-permute-done.10.refs_0_, bf16[144,128]{1,0:T(8,128)(2,1)S(1)} %collective-permute-done.11.refs_1_, ...), custom_call_target="tpu_custom_call" | custom-call | flops 131072 | bytes 131072 | tf_op jit(solution)/shard_map/pallas_call | solution.py:428
  43.2 1.6 %collective-permute-done.13 = f32[6,1024]{1,0:T(8,128)S(1)} collective-permute-done((f32[6,1024]{1,0:T(8,128)S(1)}, f32[6,1024]{1,0:T(8,128)S(1)}, u32[]{:S(2)}, u32[]{:S(2)}) %collective-permute-start.13) | collective-permute-done | bytes 24608 | tf_op jit(solution)/shard_map/ppermute | solution.py:425
  44.8 0.6 %add.3 = f32[6,1024]{1,0:T(8,128)} add(f32[6,1024]{1,0:T(8,128)S(1)} %get-tuple-element.49, f32[6,1024]{1,0:T(8,128)S(1)} %collective-permute-done.13) | non-fusion elementwise | flops 6144 | bytes 73728 | tf_op jit(solution)/shard_map/add | solution.py:425
  (1 shorter events, 0.0 us)
Async XLA Ops:
  0.6 11.7 %copy-start.2 = (bf16[32,512]{1,0:T(8,128)(2,1)S(1)}, bf16[32,512]{1,0:T(8,128)(2,1)}, u32[]{:S(2)}) copy-start(bf16[32,512]{1,0:T(8,128)(2,1)} %refs_0_.1) | copy-start | bytes 98308
  0.6 16.7 %copy-start = (f32[3,1024]{1,0:T(4,128)S(1)}, f32[3,1024]{1,0:T(4,128)}, u32[]{:S(2)}) copy-start(f32[3,1024]{1,0:T(4,128)} %quad_ref.5) | copy-start | bytes 36868
  0.7 16.7 %copy-start.1 = (f32[2,1024]{1,0:T(2,128)S(1)}, f32[2,1024]{1,0:T(2,128)}, u32[]{:S(2)}) copy-start(f32[2,1024]{1,0:T(2,128)} %lin_ref.5) | copy-start | bytes 24580
  0.7 16.7 %copy-start.4 = (s32[1024]{0:T(1024)S(1)}, s32[1024]{0:T(1024)}, u32[]{:S(2)}) copy-start(s32[1024]{0:T(1024)} %param.14) | copy-start | bytes 12292
  0.7 16.7 %copy-start.3 = (f32[1024]{0:T(1024)S(1)}, f32[1024]{0:T(1024)}, u32[]{:S(2)}) copy-start(f32[1024]{0:T(1024)} %param.13) | copy-start | bytes 12292
  0.7 8.8 %collective-permute-start = (bf16[32,512]{1,0:T(8,128)(2,1)}, bf16[32,512]{1,0:T(8,128)(2,1)S(1)}, u32[]{:S(2)}, u32[]{:S(2)}) collective-permute-start(bf16[32,512]{1,0:T(8,128)(2,1)} %refs_0_.1), channel_id=1, source_target_pairs={{0,4},{1,5},{2,6},{3,7},{4,0},{5,1},{6,2},{7,3},{8,12},{9,13},{10,... | collective-permute-start | bytes 98312 | tf_op jit(solution)/shard_map/ppermute | solution.py:329
  3.8 5.8 %collective-permute-start.1 = (bf16[32,512]{1,0:T(8,128)(2,1)}, bf16[32,512]{1,0:T(8,128)(2,1)S(1)}, u32[]{:S(2)}, u32[]{:S(2)}) collective-permute-start(bf16[32,512]{1,0:T(8,128)(2,1)} %refs_0_.1), channel_id=1, source_target_pairs={{0,8},{1,9},{2,10},{3,11},{4,12},{5,13},{6,14},{7,15},{8,0},{9,1},... | collective-permute-start | bytes 98312 | tf_op jit(solution)/shard_map/ppermute | solution.py:329
  6.4 5.9 %collective-permute-start.2 = (bf16[32,512]{1,0:T(8,128)(2,1)}, bf16[32,512]{1,0:T(8,128)(2,1)S(1)}, u32[]{:S(2)}, u32[]{:S(2)}) collective-permute-start(bf16[32,512]{1,0:T(8,128)(2,1)} %refs_0_.1), channel_id=1, source_target_pairs={{0,12},{1,13},{2,14},{3,15},{4,8},{5,9},{6,10},{7,11},{8,4},{9,5},... | collective-permute-start | bytes 98312 | tf_op jit(solution)/shard_map/ppermute | solution.py:329
  6.4 0.7 %copy-start.5 = (f32[512]{0:T(512)S(1)}, f32[512]{0:T(512)}, u32[]{:S(2)}) copy-start(f32[512]{0:T(512)} %param.15) | copy-start | bytes 6148
  12.3 5.0 %collective-permute-start.3 = (bf16[128,512]{1,0:T(8,128)(2,1)S(1)}, bf16[128,512]{1,0:T(8,128)(2,1)S(1)}, u32[]{:S(2)}, u32[]{:S(2)}) collective-permute-start(bf16[128,512]{1,0:T(8,128)(2,1)S(1)} %shard_map.96.refs_0_), channel_id=1, source_target_pairs={{0,2},{1,3},{2,0},{3,1},{4,6},{5,7},{6,4},{7,5},{8,10},{9,11},{10,... | collective-permute-start | bytes 393224 | tf_op jit(solution)/shard_map/ppermute | solution.py:329
  13.9 5.5 %collective-permute-start.5 = (bf16[128,512]{1,0:T(8,128)(2,1)S(1)}, bf16[128,512]{1,0:T(8,128)(2,1)S(1)}, u32[]{:S(2)}, u32[]{:S(2)}) collective-permute-start(bf16[128,512]{1,0:T(8,128)(2,1)S(1)} %shard_map.96.refs_0_), channel_id=1, source_target_pairs={{0,1},{1,0},{2,3},{3,2},{4,5},{5,4},{6,7},{7,6},{8,9},{9,8},{10,11... | collective-permute-start | bytes 393224 | tf_op jit(solution)/shard_map/ppermute | solution.py:329
  17.3 4.5 %collective-permute-start.4 = (bf16[128,512]{1,0:T(8,128)(2,1)S(1)}, bf16[128,512]{1,0:T(8,128)(2,1)S(1)}, u32[]{:S(2)}, u32[]{:S(2)}) collective-permute-start(bf16[128,512]{1,0:T(8,128)(2,1)S(1)} %collective-permute-done.3.refs_0_), channel_id=1, source_target_pairs={{0,1},{1,0},{2,3},{3,2},{4,5},{5,4},{6,7},{7,6},{8,9},{9,8},{10,11... | collective-permute-start | bytes 393224 | tf_op jit(solution)/shard_map/ppermute | solution.py:329
  23.8 1.7 %collective-permute-start.8 = (bf16[128,512]{1,0:T(8,128)(2,1)S(1)}, bf16[128,512]{1,0:T(8,128)(2,1)S(1)}, u32[]{:S(2)}, u32[]{:S(2)}) collective-permute-start(bf16[128,512]{1,0:T(8,128)(2,1)S(1)} %get-tuple-element.36), channel_id=1, source_target_pairs={{0,1},{1,0},{2,3},{3,2},{4,5},{5,4},{6,7},{7,6},{8,9},{9,8},{10,11... | collective-permute-start | bytes 393224 | tf_op jit(solution)/shard_map/ppermute | solution.py:329
  24.4 1.2 %collective-permute-start.7 = (f32[2,512]{1,0:T(2,128)S(1)}, f32[2,512]{1,0:T(2,128)S(1)}, u32[]{:S(2)}, u32[]{:S(2)}) collective-permute-start(f32[2,512]{1,0:T(2,128)S(1)} %get-tuple-element.32.stat_ref), channel_id=1, source_target_pairs={{0,1},{1,0},{2,3},{3,2},{4,5},{5,4},{6,7},{7,6},{8,9},{9,8},{10,11... | collective-permute-start | bytes 12296 | tf_op jit(solution)/shard_map/ppermute | solution.py:329
  25.8 5.7 %collective-permute-start.9 = (bf16[528,128]{1,0:T(8,128)(2,1)S(1)}, bf16[528,128]{1,0:T(8,128)(2,1)S(1)}, u32[]{:S(2)}, u32[]{:S(2)}) collective-permute-start(bf16[528,128]{1,0:T(8,128)(2,1)S(1)} %shard_map.100), channel_id=1, source_target_pairs={{0,2},{1,3},{2,0},{3,1},{4,6},{5,7},{6,4},{7,5},{8,10},{9,11},{10,... | collective-permute-start | bytes 405512 | tf_op jit(solution)/shard_map/ppermute | solution.py:329
  27.4 1.3 %collective-permute-start.6 = (bf16[128,512]{1,0:T(8,128)(2,1)S(1)}, bf16[128,512]{1,0:T(8,128)(2,1)S(1)}, u32[]{:S(2)}, u32[]{:S(2)}) collective-permute-start(bf16[128,512]{1,0:T(8,128)(2,1)S(1)} %get-tuple-element.34), channel_id=1, source_target_pairs={{0,1},{1,0},{2,3},{3,2},{4,5},{5,4},{6,7},{7,6},{8,9},{9,8},{10,11... | collective-permute-start | bytes 393224 | tf_op jit(solution)/shard_map/ppermute | solution.py:329
  31.8 4.5 %collective-permute-start.10 = (bf16[144,128]{1,0:T(8,128)(2,1)S(1)}, bf16[144,128]{1,0:T(8,128)(2,1)S(1)}, u32[]{:S(2)}, u32[]{:S(2)}) collective-permute-start(bf16[144,128]{1,0:T(8,128)(2,1)S(1)} %get-tuple-element.44), channel_id=1, source_target_pairs={{0,4},{1,5},{2,6},{3,7},{4,0},{5,1},{6,2},{7,3},{8,12},{9,13},{10,... | collective-permute-start | bytes 110600 | tf_op jit(solution)/shard_map/ppermute | solution.py:329
  31.9 4.9 %collective-permute-start.11 = (bf16[144,128]{1,0:T(8,128)(2,1)S(1)}, bf16[144,128]{1,0:T(8,128)(2,1)S(1)}, u32[]{:S(2)}, u32[]{:S(2)}) collective-permute-start(bf16[144,128]{1,0:T(8,128)(2,1)S(1)} %get-tuple-element.45), channel_id=1, source_target_pairs={{0,8},{1,9},{2,10},{3,11},{4,12},{5,13},{6,14},{7,15},{8,0},{9,1},... | collective-permute-start | bytes 110600 | tf_op jit(solution)/shard_map/ppermute | solution.py:329
  33.6 5.8 %collective-permute-start.12 = (bf16[144,128]{1,0:T(8,128)(2,1)S(1)}, bf16[144,128]{1,0:T(8,128)(2,1)S(1)}, u32[]{:S(2)}, u32[]{:S(2)}) collective-permute-start(bf16[144,128]{1,0:T(8,128)(2,1)S(1)} %get-tuple-element.46), channel_id=1, source_target_pairs={{0,12},{1,13},{2,14},{3,15},{4,8},{5,9},{6,10},{7,11},{8,4},{9,5},... | collective-permute-start | bytes 110600 | tf_op jit(solution)/shard_map/ppermute | solution.py:329
  40.8 4.0 %collective-permute-start.13 = (f32[6,1024]{1,0:T(8,128)S(1)}, f32[6,1024]{1,0:T(8,128)S(1)}, u32[]{:S(2)}, u32[]{:S(2)}) collective-permute-start(f32[6,1024]{1,0:T(8,128)S(1)} %get-tuple-element.49), channel_id=1, source_target_pairs={{0,16},{16,0},{1,17},{17,1},{2,18},{18,2},{3,19},{19,3},{4,20},{20... | collective-permute-start | bytes 73736 | tf_op jit(solution)/shard_map/ppermute | solution.py:425

commit v6 on v5

--- a/solution.py
+++ b/solution.py
@@ -63,7 +63,7 @@
     out_ref[...] = jnp.concatenate(values, axis=0).astype(jnp.bfloat16)
 
 
-def prep_kernel(n, me_ref, mant_hbm, exp_hbm, cot_ref, out_ref, cot_out_ref, mant, expo, sems):
+def prep_kernel(n, me_ref, mant_hbm, exp_hbm, cot_ref, out_ref, turned_ref, cot_out_ref, mant, expo, sems):
     comps, units, width = mant.shape
     blocks = expo.shape[1]
     span = width // blocks
@@ -91,9 +91,10 @@
             first = b * span
             at = (first // JB) * (comps * JB) + k * JB + first % JB
             out_ref[:, at : at + span] = value
-
-
-def main_kernel(n_rows, n_stat, f_ref, lin_ref, quad_ref, cross_ref, ply_ref, *refs):
+            turned_ref[at : at + span, :] = jnp.transpose(value)
+
+
+def main_kernel(n_rows, n_stat, f_ref, turned_ref, lin_ref, quad_ref, cross_ref, ply_ref, *refs):
     row_refs, stat_refs = refs[:n_rows], refs[n_rows : n_rows + n_stat]
     term_refs = refs[n_rows + n_stat : 2 * n_rows + n_stat]
     stat_ref, s_ref, w_ref, a_ref, idx, d, acc = refs[2 * n_rows + n_stat :]
@@ -153,10 +154,9 @@
             d[r, base + JB : base + 2 * JB] = (w * (f2 + q22 * s2 + f12 * s1)).astype(jnp.bfloat16)
             d[r, base + 2 * JB : base + 3 * JB] = (w * (q66 * t)).astype(jnp.bfloat16)
         total = total + jnp.concatenate(sums, axis=0)
-        part = lax.dot_general(
+        part = jnp.dot(
             d[:, base : base + 3 * JB],
-            f_ref[:, base : base + 3 * JB],
-            (((1,), (1,)), ((), ())),
+            turned_ref[base : base + 3 * JB, :],
             preferred_element_type=jnp.float32,
         )
         if jb == 0:
@@ -171,18 +171,17 @@
                 ref[...] = part[at : at + ref.shape[0]].astype(ref.dtype)
                 at += ref.shape[0]
     lines = [to_lanes(peak, cases), to_lanes(peak + jnp.log(total), cases)]
-    at = 0
-    for ref in stat_refs:
-        at += ref.shape[1]
+    half = cases // 2
     if stat_refs:
-        quarter = cases
-        first, second = stat_refs
-        stat_ref[:, 0:quarter] = first[:, 0:quarter]
-        stat_ref[:, quarter : 2 * quarter] = second[...]
-        stat_ref[:, 2 * quarter : 3 * quarter] = first[:, quarter : 2 * quarter]
-        at = 3 * quarter
-    stat_ref[0:1, at : at + cases] = lines[0]
-    stat_ref[1:2, at : at + cases] = lines[1]
+        near = stat_refs[0]
+        stat_ref[:, 0:half] = near[:, 0:half]
+        stat_ref[:, 2 * half : 3 * half] = near[:, half:]
+        places = [(half, 0), (3 * half, half)]
+    else:
+        places = [(0, 0), (half, half)]
+    for here, there in places:
+        for i in range(2):
+            stat_ref[i : i + 1, here : here + half] = lines[i][:, there : there + half]
 
 
 def join(a, b):
@@ -218,7 +217,7 @@
     r = slice(quarter, 2 * quarter)
     up = column(jnp.exp(mine - env)[:, r], quarter)
     down = column(jnp.exp(theirs - env)[:, r], quarter)
-    value = own_ref[...] * up + got_ref[...].astype(jnp.float32) * down
+    value = own_ref[...] * up + got_ref[...] * down
     size = out_ref.shape[0] - 16
     out_ref[0:size, :] = fold(value).astype(jnp.bfloat16)
     out_ref[size : size + 16, :] = encode(env)
@@ -238,7 +237,7 @@
     env = join(join(mine, theirs), far)
     env_ref[...] = env
     scale = [column(jnp.exp(x - env)[:, 0:quarter], quarter) for x in (mine, theirs, far)]
-    total = own_ref[...] * scale[0] + got_ref[...].astype(jnp.float32) * scale[1]
+    total = own_ref[...] * scale[0] + got_ref[...] * scale[1]
     parts = []
     for c in range(units // 128):
         part = part_ref[c * quarter : (c + 1) * quarter, :].astype(jnp.float32)
@@ -252,7 +251,7 @@
         ref[size : size + 16, :] = tail
 
 
-def coef_kernel(cot_ref, stat_ref, env_ref, s0_ref, s1_ref, s2_ref, w0_ref, w1_ref, w2_ref, *refs):
+def coef_kernel(cot_ref, stat_ref, env_ref, s0_ref, s1_ref, w0_ref, w1_ref, *refs):
     coef_ref, gain_ref = refs[-2:]
     part_refs = refs[:-2]
     nz = 1 + len(part_refs)
@@ -277,7 +276,7 @@
         (0, s0_ref, w0_ref, 0),
         (quarter, s1_ref, w1_ref, 0),
         (2 * quarter, s0_ref, w0_ref, quarter),
-        (3 * quarter, s2_ref, w2_ref, 0),
+        (3 * quarter, s1_ref, w1_ref, quarter),
     ]
     for jb in range(width // JB):
         base = jb * 3 * JB
@@ -329,9 +328,9 @@
         return lax.ppermute(x, "elem", [(i, i ^ bits) for i in range(n)])
 
     along_z = [along(4 * m, load_coef) for m in range(1, nz)]
-    fields, cot = vmem_call(
+    fields, turned, cot = vmem_call(
         functools.partial(prep_kernel, n),
-        [shape((units, comps * width), bf16), shape((1, cases), f32)],
+        [shape((units, comps * width), bf16), shape((comps * width, units), bf16), shape((1, cases), f32)],
         scratch_shapes=[
             VMEM((comps, units, width), bf16),
             VMEM((comps, scale_exp.shape[2], units), jnp.int32),
@@ -353,7 +352,7 @@
         load_coef, *along_z
     )
     far = along(2, near)
-    near_twin, far_twin = along(1, near), along(1, far)
+    near_twin = along(1, near)
 
     def main(blocks, dtypes, stats=()):
         count = len(blocks) * quarter
@@ -374,10 +373,11 @@
             flops=4 * count * units * comps * width,
             nbytes=2 * units * comps * width + 4 * count * 4 * width,
             exps=count * width,
-            n_in=5 + len(blocks) + len(stats),
+            n_in=6 + len(blocks) + len(stats),
             limit=24,
         )(
             fields,
+            turned,
             lin_coef,
             quad_coef,
             cross_coef.reshape(1, width),
@@ -387,12 +387,11 @@
         )
         return outs
 
-    near_own, near_send, stat0, s0, w0 = main([near, near_twin], [f32, bf16])
+    near_own, near_send, near_stat, s0, w0 = main([near, near_twin], [f32, f32])
+    far, near_send = lax.optimization_barrier((far, near_send))
     near_got = along(1, near_send)
-    far_own, stat1, s1, w1 = main([far], [f32])
-    far_send, stat, s2, w2 = main([far_twin], [bf16], [stat0, stat1])
-    far_got = along(1, far_send)
-    stat_twin = along(1, stat)
+    far_own, far_send, stat, s1, w1 = main([far, along(1, far)], [f32, f32], [near_stat])
+    far_got, stat_twin = along(1, far_send), along(1, stat)
 
     chunk = vmem_call(
         cores_kernel,
@@ -418,8 +417,8 @@
         [shape((6, width), f32), shape((rows, 128), f32)],
         flops=14 * cases * width,
         nbytes=16 * cases * width,
-        n_in=9 + len(parts),
-    )(cot, stat, env, s0, s1, s2, w0, w1, w2, *parts)
+        n_in=7 + len(parts),
+    )(cot, stat, env, s0, s1, w0, w1, *parts)
     bit = 1
     while bit < n_case:
         coef = coef + lax.ppermute(coef, "case", [(i, i ^ bit) for i in range(n_case)])

time: 45.6 us -> 45.7 us (level)
    pallas_call x3 -> x2, Pallas kernels: 6.44 us -> 4.6 us  [main(): vmem_call(functools.partial(main_kernel, len(blocks), len(stats)), [shape...]
    pallas_call x1, Pallas kernels: 2.46 us -> 4.26 us  [per_device(): vmem_call(functools.partial(prep_kernel, n), [shape((units, comps * width...]
where the time goes in v6:
time: 45.7 us; the launch traced here: 45.5 us
  waiting for transfers between devices  16.1 us (35%)
  starting transfers between devices  15.6 us (34%)
  Pallas kernels  11.6 us (25%)
  between operations  0.78 us (2%)
  local copies, waits for them, and re-layouts  0.7 us (2%)
  other arithmetic  0.62 us (1%)
    ppermute x13, waiting for transfers between devices, along(): return lax.ppermute(x, 'elem', [(i, i ^ bits) for i in range(n)])  14.5 us
    ppermute x13, starting transfers between devices, along(): return lax.ppermute(x, 'elem', [(i, i ^ bits) for i in range(n)])  14.1 us
    pallas_call x2, Pallas kernels, main(): vmem_call(functools.partial(main_kernel, len(blocks), len(stats)), [shape...  4.6 us
    pallas_call x1, Pallas kernels, per_device(): vmem_call(functools.partial(prep_kernel, n), [shape((units, comps * width...  4.26 us
    ppermute x1, waiting for transfers between devices, per_device(): lax.ppermute(coef, 'case', [(i, i ^ bit) for i in range(n_case)])  1.64 us
    ppermute x1, starting transfers between devices, per_device(): lax.ppermute(coef, 'case', [(i, i ^ bit) for i in range(n_case)])  1.55 us
    pallas_call x1, Pallas kernels, per_device(): vmem_call(coef_kernel, [shape((6, width), f32), shape((rows, 128), f32)],...  1.47 us
  transfers between devices with their start and end apart: 14, of which 8 were waited for; matrix products, arithmetic and copies ran while one was open for 0% of the time, Pallas kernels for 17%

profile of v6, /device:TPU:0, one launch (start us, length us, event | category | flops | bytes accessed | tf_op | source)
XLA Modules:
  0.0 45.5 jit_solution(7392757106150976887)
XLA Ops:
  0.6 0.0 copy-start.2
  0.6 0.0 copy-start
  0.7 0.0 copy-start.1
  0.7 0.0 copy-start.4
  0.7 0.0 copy-start.3
  0.7 3.1 %collective-permute-start = (bf16[32,512]{1,0:T(8,128)(2,1)}, bf16[32,512]{1,0:T(8,128)(2,1)S(1)}, u32[]{:S(2)}, u32[]{:S(2)}) collective-permute-start(bf16[32,512]{1,0:T(8,128)(2,1)} %refs_0_.1), channel_id=1, source_target_pairs={{0,4},{1,5},{2,6},{3,7},{4,0},{5,1},{6,2},{7,3},{8,12},{9,13},{10,... | collective-permute-start | bytes 98312 | tf_op jit(solution)/shard_map/ppermute | solution.py:328
  3.8 2.6 %collective-permute-start.1 = (bf16[32,512]{1,0:T(8,128)(2,1)}, bf16[32,512]{1,0:T(8,128)(2,1)S(1)}, u32[]{:S(2)}, u32[]{:S(2)}) collective-permute-start(bf16[32,512]{1,0:T(8,128)(2,1)} %refs_0_.1), channel_id=1, source_target_pairs={{0,8},{1,9},{2,10},{3,11},{4,12},{5,13},{6,14},{7,15},{8,0},{9,1},... | collective-permute-start | bytes 98312 | tf_op jit(solution)/shard_map/ppermute | solution.py:328
  6.4 0.0 collective-permute-start.2
  6.4 0.0 copy-start.5
  6.4 0.7 %copy-done.5 = f32[512]{0:T(512)S(1)} copy-done((f32[512]{0:T(512)S(1)}, f32[512]{0:T(512)}, u32[]{:S(2)}) %copy-start.5) | copy-done | bytes 2072
  7.0 4.3 %shard_map.95 = (bf16[512,3072]{1,0:T(8,128)(2,1)S(1)}, bf16[3072,512]{1,0:T(8,128)(2,1)S(1)}, f32[1,512]{1,0:T(1,128)S(1)}) custom-call(s32[1]{0:T(128)} %bitcast.me_ref, bf16[3,512,1024]{2,1,0:T(8,128)(2,1)} %bitcast.11, s32[3,8,512]{2,1,0:T(8,128)} %bitcast.12, f32[1,512]{1,0:T(1,128)S(1)} %bitcast.10), custom_call_target="tpu_custom_call" | custom-call | flops 1572864 | bytes 6291456 | tf_op jit(solution)/shard_map/pallas_call | solution.py:331
  11.3 0.0 collective-permute-done.refs_1_
  11.3 0.0 collective-permute-done.1.refs_2_
  11.3 0.9 %collective-permute-done.2.refs_3_ = bf16[32,512]{1,0:T(8,128)(2,1)S(1)} collective-permute-done((bf16[32,512]{1,0:T(8,128)(2,1)}, bf16[32,512]{1,0:T(8,128)(2,1)S(1)}, u32[]{:S(2)}, u32[]{:S(2)}) %collective-permute-start.2) | collective-permute-done | bytes 32800 | tf_op jit(solution)/shard_map/ppermute | solution.py:328
  12.3 0.0 copy-done.2
  12.3 0.1 collective-permute-start.4
  12.4 1.6 %collective-permute-start.3 = (bf16[128,512]{1,0:T(8,128)(2,1)S(1)}, bf16[128,512]{1,0:T(8,128)(2,1)S(1)}, u32[]{:S(2)}, u32[]{:S(2)}) collective-permute-start(bf16[128,512]{1,0:T(8,128)(2,1)S(1)} %shard_map.96.refs_0_), channel_id=1, source_target_pairs={{0,2},{1,3},{2,0},{3,1},{4,6},{5,7},{6,4},{7,5},{8,10},{9,11},{10,... | collective-permute-start | bytes 393224 | tf_op jit(solution)/shard_map/ppermute | solution.py:328
  14.0 0.0 collective-permute-done.4.refs_1_
  14.0 0.0 copy-done
  14.0 0.0 copy-done.1
  14.0 0.0 copy-done.4
  14.0 0.0 copy-done.3
  14.0 2.3 %shard_map.97 = (f32[128,512]{1,0:T(8,128)S(1)}, f32[128,512]{1,0:T(8,128)S(1)}, f32[2,256]{1,0:T(2,128)S(1)}, f32[256,3072]{1,0:T(8,128)S(1)}, f32[256,1024]{1,0:T(8,128)S(1)}) custom-call(bf16[512,3072]{1,0:T(8,128)(2,1)S(1)} %get-tuple-element.28.f_ref, bf16[3072,512]{1,0:T(8,128)(2,1)S(1)} %get-tuple-element.29.turned_ref, f32[2,1024]{1,0:T(2,128)S(1)} %copy-done.1, ...), custom_call_target="tpu_custom_call" | custom-call | flops 1610612736 | bytes 7340032 | tf_op jit(solution)/shard_map/pallas_call | solution.py:359
  16.3 2.0 %collective-permute-done.3.refs_0_ = bf16[128,512]{1,0:T(8,128)(2,1)S(1)} collective-permute-done((bf16[128,512]{1,0:T(8,128)(2,1)S(1)}, bf16[128,512]{1,0:T(8,128)(2,1)S(1)}, u32[]{:S(2)}, u32[]{:S(2)}) %collective-permute-start.3) | collective-permute-done | bytes 131104 | tf_op jit(solution)/shard_map/ppermute | solution.py:328
  18.3 0.0 collective-permute-start.5
  18.3 1.3 %collective-permute-done.5.refs_1_ = bf16[128,512]{1,0:T(8,128)(2,1)S(1)} collective-permute-done((bf16[128,512]{1,0:T(8,128)(2,1)S(1)}, bf16[128,512]{1,0:T(8,128)(2,1)S(1)}, u32[]{:S(2)}, u32[]{:S(2)}) %collective-permute-start.5) | collective-permute-done | bytes 131104 | tf_op jit(solution)/shard_map/ppermute | solution.py:328
  19.6 2.3 %shard_map.98 = (f32[128,512]{1,0:T(8,128)S(1)}, f32[128,512]{1,0:T(8,128)S(1)}, f32[2,512]{1,0:T(2,128)S(1)}, f32[256,3072]{1,0:T(8,128)S(1)}, f32[256,1024]{1,0:T(8,128)S(1)}) custom-call(bf16[512,3072]{1,0:T(8,128)(2,1)S(1)} %get-tuple-element.28.f_ref, bf16[3072,512]{1,0:T(8,128)(2,1)S(1)} %get-tuple-element.29.turned_ref, f32[2,1024]{1,0:T(2,128)S(1)} %copy-done.1, ...), custom_call_target="tpu_custom_call" | custom-call | flops 1610612736 | bytes 7340032 | tf_op jit(solution)/shard_map/pallas_call | solution.py:359
  21.9 0.2 collective-permute-start.8
  22.1 0.4 collective-permute-start.6
  22.5 0.1 collective-permute-start.7
  22.6 1.3 %collective-permute-done.7.twin_ref = f32[2,512]{1,0:T(2,128)S(1)} collective-permute-done((f32[2,512]{1,0:T(2,128)S(1)}, f32[2,512]{1,0:T(2,128)S(1)}, u32[]{:S(2)}, u32[]{:S(2)}) %collective-permute-start.7) | collective-permute-done | bytes 4128 | tf_op jit(solution)/shard_map/ppermute | solution.py:328
  23.9 0.0 collective-permute-done.8.got_ref
  23.9 0.2 shard_map.99
  24.1 1.6 %collective-permute-start.9 = (bf16[528,128]{1,0:T(8,128)(2,1)S(1)}, bf16[528,128]{1,0:T(8,128)(2,1)S(1)}, u32[]{:S(2)}, u32[]{:S(2)}) collective-permute-start(bf16[528,128]{1,0:T(8,128)(2,1)S(1)} %shard_map.99), channel_id=1, source_target_pairs={{0,2},{1,3},{2,0},{3,1},{4,6},{5,7},{6,4},{7,5},{8,10},{9,11},{10,... | collective-permute-start | bytes 405512 | tf_op jit(solution)/shard_map/ppermute | solution.py:328
  25.7 0.0 collective-permute-done.6.got_ref
  25.7 4.1 %collective-permute-done.9.part_ref = bf16[528,128]{1,0:T(8,128)(2,1)S(1)} collective-permute-done((bf16[528,128]{1,0:T(8,128)(2,1)S(1)}, bf16[528,128]{1,0:T(8,128)(2,1)S(1)}, u32[]{:S(2)}, u32[]{:S(2)}) %collective-permute-start.9) | collective-permute-done | bytes 135200 | tf_op jit(solution)/shard_map/ppermute | solution.py:328
  29.8 0.3 shard_map.100
  30.1 0.1 collective-permute-start.10
  30.2 3.5 %collective-permute-start.11 = (bf16[144,128]{1,0:T(8,128)(2,1)S(1)}, bf16[144,128]{1,0:T(8,128)(2,1)S(1)}, u32[]{:S(2)}, u32[]{:S(2)}) collective-permute-start(bf16[144,128]{1,0:T(8,128)(2,1)S(1)} %get-tuple-element.45), channel_id=1, source_target_pairs={{0,8},{1,9},{2,10},{3,11},{4,12},{5,13},{6,14},{7,15},{8,0},{9,1},... | collective-permute-start | bytes 110600 | tf_op jit(solution)/shard_map/ppermute | solution.py:328
  33.7 0.9 %collective-permute-start.12 = (bf16[144,128]{1,0:T(8,128)(2,1)S(1)}, bf16[144,128]{1,0:T(8,128)(2,1)S(1)}, u32[]{:S(2)}, u32[]{:S(2)}) collective-permute-start(bf16[144,128]{1,0:T(8,128)(2,1)S(1)} %get-tuple-element.46), channel_id=1, source_target_pairs={{0,12},{1,13},{2,14},{3,15},{4,8},{5,9},{6,10},{7,11},{8,4},{9,5},... | collective-permute-start | bytes 110600 | tf_op jit(solution)/shard_map/ppermute | solution.py:328
  34.6 0.0 collective-permute-done.10.refs_0_
  34.6 1.0 %collective-permute-done.11.refs_1_ = bf16[144,128]{1,0:T(8,128)(2,1)S(1)} collective-permute-done((bf16[144,128]{1,0:T(8,128)(2,1)S(1)}, bf16[144,128]{1,0:T(8,128)(2,1)S(1)}, u32[]{:S(2)}, u32[]{:S(2)}) %collective-permute-start.11) | collective-permute-done | bytes 36896 | tf_op jit(solution)/shard_map/ppermute | solution.py:328
  35.6 3.8 %collective-permute-done.12.refs_2_ = bf16[144,128]{1,0:T(8,128)(2,1)S(1)} collective-permute-done((bf16[144,128]{1,0:T(8,128)(2,1)S(1)}, bf16[144,128]{1,0:T(8,128)(2,1)S(1)}, u32[]{:S(2)}, u32[]{:S(2)}) %collective-permute-start.12) | collective-permute-done | bytes 36896 | tf_op jit(solution)/shard_map/ppermute | solution.py:328
  39.4 1.5 %shard_map.101 = (f32[6,1024]{1,0:T(8,128)S(1)}, f32[32,128]{1,0:T(8,128)S(1)}) custom-call(f32[1,512]{1,0:T(1,128)S(1)} %get-tuple-element.26.cot_ref, f32[2,512]{1,0:T(2,128)S(1)} %get-tuple-element.34.stat_ref, f32[1,512]{1,0:T(1,128)S(1)} %get-tuple-element.39.env_ref, f32[256,3072]{1,0:T(8,128)S(1)} %get-tuple-element.40.s0_ref, ...), custom_call_target="tpu_custom_call" | custom-call | flops 7340032 | bytes 8388608 | tf_op jit(solution)/shard_map/pallas_call | solution.py:415
  40.9 1.6 %collective-permute-start.13 = (f32[6,1024]{1,0:T(8,128)S(1)}, f32[6,1024]{1,0:T(8,128)S(1)}, u32[]{:S(2)}, u32[]{:S(2)}) collective-permute-start(f32[6,1024]{1,0:T(8,128)S(1)} %get-tuple-element.49), channel_id=1, source_target_pairs={{0,16},{16,0},{1,17},{17,1},{2,18},{18,2},{3,19},{19,3},{4,20},{20... | collective-permute-start | bytes 73736 | tf_op jit(solution)/shard_map/ppermute | solution.py:424
  42.5 0.8 %shard_map.102 = f32[32,512]{1,0:T(8,128)} custom-call(f32[32,128]{1,0:T(8,128)S(1)} %get-tuple-element.47.gain_ref, f32[128,128]{1,0:T(8,128)S(1)} %get-tuple-element.48.own_ref, bf16[144,128]{1,0:T(8,128)(2,1)S(1)} %collective-permute-done.10.refs_0_, bf16[144,128]{1,0:T(8,128)(2,1)S(1)} %collective-permute-done.11.refs_1_, ...), custom_call_target="tpu_custom_call" | custom-call | flops 131072 | bytes 131072 | tf_op jit(solution)/shard_map/pallas_call | solution.py:427
  43.3 1.6 %collective-permute-done.13 = f32[6,1024]{1,0:T(8,128)S(1)} collective-permute-done((f32[6,1024]{1,0:T(8,128)S(1)}, f32[6,1024]{1,0:T(8,128)S(1)}, u32[]{:S(2)}, u32[]{:S(2)}) %collective-permute-start.13) | collective-permute-done | bytes 24608 | tf_op jit(solution)/shard_map/ppermute | solution.py:424
  44.9 0.6 %add.3 = f32[6,1024]{1,0:T(8,128)} add(f32[6,1024]{1,0:T(8,128)S(1)} %get-tuple-element.49, f32[6,1024]{1,0:T(8,128)S(1)} %collective-permute-done.13) | non-fusion elementwise | flops 6144 | bytes 73728 | tf_op jit(solution)/shard_map/add | solution.py:424
  (1 shorter events, 0.0 us)
Async XLA Ops:
  0.6 11.7 %copy-start.2 = (bf16[32,512]{1,0:T(8,128)(2,1)S(1)}, bf16[32,512]{1,0:T(8,128)(2,1)}, u32[]{:S(2)}) copy-start(bf16[32,512]{1,0:T(8,128)(2,1)} %refs_0_.1) | copy-start | bytes 98308
  0.6 13.3 %copy-start = (f32[3,1024]{1,0:T(4,128)S(1)}, f32[3,1024]{1,0:T(4,128)}, u32[]{:S(2)}) copy-start(f32[3,1024]{1,0:T(4,128)} %quad_ref.3) | copy-start | bytes 36868
  0.7 13.3 %copy-start.1 = (f32[2,1024]{1,0:T(2,128)S(1)}, f32[2,1024]{1,0:T(2,128)}, u32[]{:S(2)}) copy-start(f32[2,1024]{1,0:T(2,128)} %lin_ref.3) | copy-start | bytes 24580
  0.7 13.3 %copy-start.4 = (s32[1024]{0:T(1024)S(1)}, s32[1024]{0:T(1024)}, u32[]{:S(2)}) copy-start(s32[1024]{0:T(1024)} %param.14) | copy-start | bytes 12292
  0.7 13.3 %copy-start.3 = (f32[1024]{0:T(1024)S(1)}, f32[1024]{0:T(1024)}, u32[]{:S(2)}) copy-start(f32[1024]{0:T(1024)} %param.13) | copy-start | bytes 12292
  0.7 10.6 %collective-permute-start = (bf16[32,512]{1,0:T(8,128)(2,1)}, bf16[32,512]{1,0:T(8,128)(2,1)S(1)}, u32[]{:S(2)}, u32[]{:S(2)}) collective-permute-start(bf16[32,512]{1,0:T(8,128)(2,1)} %refs_0_.1), channel_id=1, source_target_pairs={{0,4},{1,5},{2,6},{3,7},{4,0},{5,1},{6,2},{7,3},{8,12},{9,13},{10,... | collective-permute-start | bytes 98312 | tf_op jit(solution)/shard_map/ppermute | solution.py:328
  3.8 7.6 %collective-permute-start.1 = (bf16[32,512]{1,0:T(8,128)(2,1)}, bf16[32,512]{1,0:T(8,128)(2,1)S(1)}, u32[]{:S(2)}, u32[]{:S(2)}) collective-permute-start(bf16[32,512]{1,0:T(8,128)(2,1)} %refs_0_.1), channel_id=1, source_target_pairs={{0,8},{1,9},{2,10},{3,11},{4,12},{5,13},{6,14},{7,15},{8,0},{9,1},... | collective-permute-start | bytes 98312 | tf_op jit(solution)/shard_map/ppermute | solution.py:328
  6.4 5.9 %collective-permute-start.2 = (bf16[32,512]{1,0:T(8,128)(2,1)}, bf16[32,512]{1,0:T(8,128)(2,1)S(1)}, u32[]{:S(2)}, u32[]{:S(2)}) collective-permute-start(bf16[32,512]{1,0:T(8,128)(2,1)} %refs_0_.1), channel_id=1, source_target_pairs={{0,12},{1,13},{2,14},{3,15},{4,8},{5,9},{6,10},{7,11},{8,4},{9,5},... | collective-permute-start | bytes 98312 | tf_op jit(solution)/shard_map/ppermute | solution.py:328
  6.4 0.7 %copy-start.5 = (f32[512]{0:T(512)S(1)}, f32[512]{0:T(512)}, u32[]{:S(2)}) copy-start(f32[512]{0:T(512)} %param.15) | copy-start | bytes 6148
  12.3 1.7 %collective-permute-start.4 = (bf16[128,512]{1,0:T(8,128)(2,1)S(1)}, bf16[128,512]{1,0:T(8,128)(2,1)S(1)}, u32[]{:S(2)}, u32[]{:S(2)}) collective-permute-start(bf16[128,512]{1,0:T(8,128)(2,1)S(1)} %shard_map.96.refs_0_), channel_id=1, source_target_pairs={{0,1},{1,0},{2,3},{3,2},{4,5},{5,4},{6,7},{7,6},{8,9},{9,8},{10,11... | collective-permute-start | bytes 393224 | tf_op jit(solution)/shard_map/ppermute | solution.py:328
  12.4 5.9 %collective-permute-start.3 = (bf16[128,512]{1,0:T(8,128)(2,1)S(1)}, bf16[128,512]{1,0:T(8,128)(2,1)S(1)}, u32[]{:S(2)}, u32[]{:S(2)}) collective-permute-start(bf16[128,512]{1,0:T(8,128)(2,1)S(1)} %shard_map.96.refs_0_), channel_id=1, source_target_pairs={{0,2},{1,3},{2,0},{3,1},{4,6},{5,7},{6,4},{7,5},{8,10},{9,11},{10,... | collective-permute-start | bytes 393224 | tf_op jit(solution)/shard_map/ppermute | solution.py:328
  18.3 1.3 %collective-permute-start.5 = (bf16[128,512]{1,0:T(8,128)(2,1)S(1)}, bf16[128,512]{1,0:T(8,128)(2,1)S(1)}, u32[]{:S(2)}, u32[]{:S(2)}) collective-permute-start(bf16[128,512]{1,0:T(8,128)(2,1)S(1)} %collective-permute-done.3.refs_0_), channel_id=1, source_target_pairs={{0,1},{1,0},{2,3},{3,2},{4,5},{5,4},{6,7},{7,6},{8,9},{9,8},{10,11... | collective-permute-start | bytes 393224 | tf_op jit(solution)/shard_map/ppermute | solution.py:328
  21.9 2.0 %collective-permute-start.8 = (f32[128,512]{1,0:T(8,128)S(1)}, f32[128,512]{1,0:T(8,128)S(1)}, u32[]{:S(2)}, u32[]{:S(2)}) collective-permute-start(f32[128,512]{1,0:T(8,128)S(1)} %get-tuple-element.38), channel_id=1, source_target_pairs={{0,1},{1,0},{2,3},{3,2},{4,5},{5,4},{6,7},{7,6},{8,9},{9,8},{10,11... | collective-permute-start | bytes 786440 | tf_op jit(solution)/shard_map/ppermute | solution.py:328
  22.1 3.6 %collective-permute-start.6 = (f32[128,512]{1,0:T(8,128)S(1)}, f32[128,512]{1,0:T(8,128)S(1)}, u32[]{:S(2)}, u32[]{:S(2)}) collective-permute-start(f32[128,512]{1,0:T(8,128)S(1)} %get-tuple-element.36), channel_id=1, source_target_pairs={{0,1},{1,0},{2,3},{3,2},{4,5},{5,4},{6,7},{7,6},{8,9},{9,8},{10,11... | collective-permute-start | bytes 786440 | tf_op jit(solution)/shard_map/ppermute | solution.py:328
  22.5 1.4 %collective-permute-start.7 = (f32[2,512]{1,0:T(2,128)S(1)}, f32[2,512]{1,0:T(2,128)S(1)}, u32[]{:S(2)}, u32[]{:S(2)}) collective-permute-start(f32[2,512]{1,0:T(2,128)S(1)} %get-tuple-element.34.stat_ref), channel_id=1, source_target_pairs={{0,1},{1,0},{2,3},{3,2},{4,5},{5,4},{6,7},{7,6},{8,9},{9,8},{10,11... | collective-permute-start | bytes 12296 | tf_op jit(solution)/shard_map/ppermute | solution.py:328
  24.1 5.7 %collective-permute-start.9 = (bf16[528,128]{1,0:T(8,128)(2,1)S(1)}, bf16[528,128]{1,0:T(8,128)(2,1)S(1)}, u32[]{:S(2)}, u32[]{:S(2)}) collective-permute-start(bf16[528,128]{1,0:T(8,128)(2,1)S(1)} %shard_map.99), channel_id=1, source_target_pairs={{0,2},{1,3},{2,0},{3,1},{4,6},{5,7},{6,4},{7,5},{8,10},{9,11},{10,... | collective-permute-start | bytes 405512 | tf_op jit(solution)/shard_map/ppermute | solution.py:328
  30.1 4.5 %collective-permute-start.10 = (bf16[144,128]{1,0:T(8,128)(2,1)S(1)}, bf16[144,128]{1,0:T(8,128)(2,1)S(1)}, u32[]{:S(2)}, u32[]{:S(2)}) collective-permute-start(bf16[144,128]{1,0:T(8,128)(2,1)S(1)} %get-tuple-element.44), channel_id=1, source_target_pairs={{0,4},{1,5},{2,6},{3,7},{4,0},{5,1},{6,2},{7,3},{8,12},{9,13},{10,... | collective-permute-start | bytes 110600 | tf_op jit(solution)/shard_map/ppermute | solution.py:328
  30.2 5.4 %collective-permute-start.11 = (bf16[144,128]{1,0:T(8,128)(2,1)S(1)}, bf16[144,128]{1,0:T(8,128)(2,1)S(1)}, u32[]{:S(2)}, u32[]{:S(2)}) collective-permute-start(bf16[144,128]{1,0:T(8,128)(2,1)S(1)} %get-tuple-element.45), channel_id=1, source_target_pairs={{0,8},{1,9},{2,10},{3,11},{4,12},{5,13},{6,14},{7,15},{8,0},{9,1},... | collective-permute-start | bytes 110600 | tf_op jit(solution)/shard_map/ppermute | solution.py:328
  33.7 5.8 %collective-permute-start.12 = (bf16[144,128]{1,0:T(8,128)(2,1)S(1)}, bf16[144,128]{1,0:T(8,128)(2,1)S(1)}, u32[]{:S(2)}, u32[]{:S(2)}) collective-permute-start(bf16[144,128]{1,0:T(8,128)(2,1)S(1)} %get-tuple-element.46), channel_id=1, source_target_pairs={{0,12},{1,13},{2,14},{3,15},{4,8},{5,9},{6,10},{7,11},{8,4},{9,5},... | collective-permute-start | bytes 110600 | tf_op jit(solution)/shard_map/ppermute | solution.py:328
  40.9 4.0 %collective-permute-start.13 = (f32[6,1024]{1,0:T(8,128)S(1)}, f32[6,1024]{1,0:T(8,128)S(1)}, u32[]{:S(2)}, u32[]{:S(2)}) collective-permute-start(f32[6,1024]{1,0:T(8,128)S(1)} %get-tuple-element.49), channel_id=1, source_target_pairs={{0,16},{16,0},{1,17},{17,1},{2,18},{18,2},{3,19},{19,3},{4,20},{20... | collective-permute-start | bytes 73736 | tf_op jit(solution)/shard_map/ppermute | solution.py:424

commit v7 on v6

--- a/solution.py
+++ b/solution.py
@@ -59,18 +59,22 @@
 
 def block_kernel(*refs):
     out_ref = refs[-1]
-    values = [ref[...].astype(jnp.float32) for ref in refs[:-1]]
+    values = [ref[...].astype(jnp.float32) for ref in refs[-2::-1]]
     out_ref[...] = jnp.concatenate(values, axis=0).astype(jnp.bfloat16)
 
 
-def prep_kernel(n, me_ref, mant_hbm, exp_hbm, cot_ref, out_ref, turned_ref, cot_out_ref, mant, expo, sems):
+def prep_kernel(n, me_ref, mant_hbm, exp_hbm, cot_hbm, out_ref, cot_out_ref, mant, expo, cot_ref, sems):
     comps, units, width = mant.shape
     blocks = expo.shape[1]
     span = width // blocks
-    copies = [pltpu.make_async_copy(exp_hbm, expo, sems.at[comps])]
+    copies = [
+        pltpu.make_async_copy(cot_hbm, cot_ref, sems.at[comps + 1]),
+        pltpu.make_async_copy(exp_hbm, expo, sems.at[comps]),
+    ]
     copies += [pltpu.make_async_copy(mant_hbm.at[k], mant.at[k], sems.at[k]) for k in range(comps)]
     for copy in copies:
         copy.start()
+    copies[0].wait()
     cases = cot_ref.shape[1]
     rows = cases // n
     nz = n // 4
@@ -79,25 +83,24 @@
     code = (me_ref[0] & 1) * (2 * nz) + ((me_ref[0] >> 1) & 1) * nz + (me_ref[0] >> 2)
     cot = jnp.broadcast_to(cot, (8, cases))
     cot_out_ref[...] = swap_lanes(cot, jnp.full((8, cases), code, jnp.int32), rows, n)[0:1]
-    copies[0].wait()
+    copies[1].wait()
     factor = jnp.exp2(expo[...].astype(jnp.float32)).reshape(comps * blocks, units)
     pad = jnp.zeros((128 - comps * blocks, units), jnp.float32)
     columns = jnp.transpose(jnp.concatenate([factor, pad], axis=0))
     for k in range(comps):
-        copies[1 + k].wait()
+        copies[2 + k].wait()
         for b in range(blocks):
             gain = jnp.broadcast_to(columns[:, k * blocks + b : k * blocks + b + 1], (units, span))
             value = mant[k, :, b * span : (b + 1) * span] * gain.astype(jnp.bfloat16)
             first = b * span
             at = (first // JB) * (comps * JB) + k * JB + first % JB
             out_ref[:, at : at + span] = value
-            turned_ref[at : at + span, :] = jnp.transpose(value)
-
-
-def main_kernel(n_rows, n_stat, f_ref, turned_ref, lin_ref, quad_ref, cross_ref, ply_ref, *refs):
+
+
+def main_kernel(n_rows, n_stat, f_ref, lin_ref, quad_ref, cross_ref, ply_ref, *refs):
     row_refs, stat_refs = refs[:n_rows], refs[n_rows : n_rows + n_stat]
     term_refs = refs[n_rows + n_stat : 2 * n_rows + n_stat]
-    stat_ref, s_ref, w_ref, a_ref, idx, d, acc = refs[2 * n_rows + n_stat :]
+    stat_ref, s_ref, w_ref, a_ref, idx, d, rest, acc = refs[2 * n_rows + n_stat :]
     cases = a_ref.shape[0]
     width = w_ref.shape[1]
     at = 0
@@ -150,15 +153,21 @@
             for c in range(128, JB, 128):
                 part = part + w[:, c : c + 128]
             sums.append(part)
-            d[r, base : base + JB] = (w * (f1 + q11 * s1 + f12 * s2)).astype(jnp.bfloat16)
-            d[r, base + JB : base + 2 * JB] = (w * (f2 + q22 * s2 + f12 * s1)).astype(jnp.bfloat16)
-            d[r, base + 2 * JB : base + 3 * JB] = (w * (q66 * t)).astype(jnp.bfloat16)
+            for k, slope in enumerate((f1 + q11 * s1 + f12 * s2, f2 + q22 * s2 + f12 * s1, q66 * t)):
+                value = w * slope
+                high = value.astype(jnp.bfloat16)
+                at_k = slice(base + k * JB, base + (k + 1) * JB)
+                d[r, at_k] = high
+                rest[r, at_k] = (value - high.astype(jnp.float32)).astype(jnp.bfloat16)
         total = total + jnp.concatenate(sums, axis=0)
-        part = jnp.dot(
-            d[:, base : base + 3 * JB],
-            turned_ref[base : base + 3 * JB, :],
-            preferred_element_type=jnp.float32,
-        )
+        part = 0.0
+        for term in (d, rest):
+            part = part + lax.dot_general(
+                term[:, base : base + 3 * JB],
+                f_ref[:, base : base + 3 * JB],
+                (((1,), (1,)), ((), ())),
+                preferred_element_type=jnp.float32,
+            )
         if jb == 0:
             acc[...] = part
         elif jb < width // JB - 1:
@@ -209,11 +218,12 @@
     return jnp.concatenate([x[:, c : c + 128] for c in range(0, x.shape[1], 128)], axis=0)
 
 
-def cores_kernel(own_ref, got_ref, stat_ref, twin_ref, out_ref):
+def cores_kernel(own_ref, got_ref, stat_ref, twin_ref, out_ref, env_ref):
     quarter = own_ref.shape[0]
     cases = 4 * quarter
     mine, theirs = stat_ref[1:2, :], swap_halves(twin_ref[1:2, :])
     env = join(mine, theirs)
+    env_ref[...] = env
     r = slice(quarter, 2 * quarter)
     up = column(jnp.exp(mine - env)[:, r], quarter)
     down = column(jnp.exp(theirs - env)[:, r], quarter)
@@ -227,15 +237,17 @@
     return jnp.concatenate([to_rows(row, at)[:, 0:1] for at in range(0, rows, 128)], axis=0)
 
 
-def chips_kernel(own_ref, got_ref, stat_ref, twin_ref, part_ref, own_out_ref, env_ref, *out_refs):
-    quarter, units = own_ref.shape
+def chips_kernel(nz, own_ref, got_ref, stat_ref, twin_ref, part_ref, *refs):
+    env_refs, stack_ref, own_out_ref, out_refs = refs[:nz], refs[nz], refs[nz + 1], refs[nz + 2 :]
+    quarter = own_ref.shape[0]
+    units = own_ref.shape[1]
     cases = 4 * quarter
-    rows = quarter // (1 + len(out_refs))
+    rows = quarter // nz
+    stack_ref[...] = jnp.concatenate([ref[...] for ref in env_refs], axis=0)
     mine, theirs = stat_ref[1:2, :], swap_halves(twin_ref[1:2, :])
     far = decode(part_ref, cases)
     far = jnp.concatenate([far[:, g * quarter : (g + 1) * quarter] for g in (1, 0, 3, 2)], axis=1)
     env = join(join(mine, theirs), far)
-    env_ref[...] = env
     scale = [column(jnp.exp(x - env)[:, 0:quarter], quarter) for x in (mine, theirs, far)]
     total = own_ref[...] * scale[0] + got_ref[...] * scale[1]
     parts = []
@@ -243,27 +255,20 @@
         part = part_ref[c * quarter : (c + 1) * quarter, :].astype(jnp.float32)
         parts.append(total[:, c * 128 : (c + 1) * 128] + part * scale[2])
     own_out_ref[...] = jnp.concatenate([p[0:rows] for p in parts], axis=0)
-    tail = encode(env)
     for m, ref in enumerate(out_refs):
         r = slice((m + 1) * rows, (m + 2) * rows)
-        size = ref.shape[0] - 16
-        ref[0:size, :] = jnp.concatenate([p[r] for p in parts], axis=0).astype(jnp.bfloat16)
-        ref[size : size + 16, :] = tail
-
-
-def coef_kernel(cot_ref, stat_ref, env_ref, s0_ref, s1_ref, w0_ref, w1_ref, *refs):
-    coef_ref, gain_ref = refs[-2:]
-    part_refs = refs[:-2]
-    nz = 1 + len(part_refs)
-    cases = cot_ref.shape[1]
+        ref[...] = jnp.concatenate([p[r] for p in parts], axis=0).astype(jnp.bfloat16)
+
+
+def coef_kernel(cot_ref, stat_ref, near_ref, far_ref, s0_ref, s1_ref, w0_ref, w1_ref, coef_ref, gain_ref):
+    nz, cases = near_ref.shape
     quarter = cases // 4
     rows = quarter // nz
     width = w0_ref.shape[1]
-    envs = [env_ref[...]] + [decode(ref, cases) for ref in part_refs]
-    pad = -nz % 8
-    env_all = jnp.concatenate(envs + [envs[0]] * pad, axis=0)
-    which = lax.broadcasted_iota(jnp.int32, env_all.shape, 0)
-    env_all = swap_lanes(env_all, jnp.where(which < nz, which, 0), rows, nz)[0:nz]
+    row = lax.broadcasted_iota(jnp.int32, (nz, cases), 0)
+    near = swap_lanes(near_ref[...], row, rows, 2 * nz)
+    far = swap_lanes(far_ref[...], row + nz, rows, 2 * nz)
+    env_all = join(near, far)
     top = jnp.max(env_all, axis=0, keepdims=True)
     env = top + jnp.log(jnp.sum(jnp.exp(env_all - top), axis=0, keepdims=True))
     cot = cot_ref[...]
@@ -302,14 +307,13 @@
 
 
 def combine_kernel(gain_ref, own_ref, *refs):
-    part_refs, out_ref = refs[:-1], refs[-1]
+    part_refs, out_ref = refs[-2::-1], refs[-1]
     rows, units = out_ref.shape
-    size = rows * units // 128
     for c in range(units // 128):
         r = slice(c * rows, (c + 1) * rows)
         value = own_ref[r, :] * gain_ref[:, 0:1]
         for m, ref in enumerate(part_refs):
-            part = ref[0:size, :].astype(jnp.float32)[r]
+            part = ref[...].astype(jnp.float32)[r]
             value = value + part * gain_ref[:, m + 1 : m + 2]
         out_ref[:, c * 128 : (c + 1) * 128] = value
 
@@ -327,29 +331,30 @@
     def along(bits, x):
         return lax.ppermute(x, "elem", [(i, i ^ bits) for i in range(n)])
 
-    along_z = [along(4 * m, load_coef) for m in range(1, nz)]
-    fields, turned, cot = vmem_call(
+    along_z = [along(4 * m, load_coef) for m in range(nz - 1, 0, -1)]
+    fields, cot = vmem_call(
         functools.partial(prep_kernel, n),
-        [shape((units, comps * width), bf16), shape((comps * width, units), bf16), shape((1, cases), f32)],
+        [shape((units, comps * width), bf16), shape((1, cases), f32)],
         scratch_shapes=[
             VMEM((comps, units, width), bf16),
             VMEM((comps, scale_exp.shape[2], units), jnp.int32),
-            pltpu.SemaphoreType.DMA((comps + 1,)),
+            VMEM((1, cases), f32),
+            pltpu.SemaphoreType.DMA((comps + 2,)),
         ],
         flops=units * comps * width,
         nbytes=4 * units * comps * width,
         n_in=4,
         smem=(0,),
-        hbm=(1, 2),
+        hbm=(1, 2, 3),
     )(
         me,
         pltpu.with_memory_space_constraint(jnp.transpose(mantissa, (1, 0, 2)), pltpu.HBM),
         pltpu.with_memory_space_constraint(jnp.transpose(scale_exp, (1, 2, 0)), pltpu.HBM),
-        cotangent.reshape(1, cases),
+        pltpu.with_memory_space_constraint(cotangent.reshape(1, cases), pltpu.HBM),
     )
     along_z[0], fields = lax.optimization_barrier((along_z[0], fields))
     near = vmem_call(block_kernel, shape((quarter, units), bf16), nbytes=4 * quarter * units, n_in=nz)(
-        load_coef, *along_z
+        *along_z, load_coef
     )
     far = along(2, near)
     near_twin = along(1, near)
@@ -368,16 +373,16 @@
                 VMEM((count, units), bf16),
                 VMEM((count, width), f32),
                 VMEM((count, comps * width), bf16),
+                VMEM((count, comps * width), bf16),
                 VMEM((count, units), f32),
             ],
-            flops=4 * count * units * comps * width,
+            flops=6 * count * units * comps * width,
             nbytes=2 * units * comps * width + 4 * count * 4 * width,
             exps=count * width,
-            n_in=6 + len(blocks) + len(stats),
+            n_in=5 + len(blocks) + len(stats),
             limit=24,
         )(
             fields,
-            turned,
             lin_coef,
             quad_coef,
             cross_coef.reshape(1, width),
@@ -389,36 +394,38 @@
 
     near_own, near_send, near_stat, s0, w0 = main([near, near_twin], [f32, f32])
     far, near_send = lax.optimization_barrier((far, near_send))
-    near_got = along(1, near_send)
     far_own, far_send, stat, s1, w1 = main([far, along(1, far)], [f32, f32], [near_stat])
     far_got, stat_twin = along(1, far_send), along(1, stat)
 
-    chunk = vmem_call(
+    chunk, env = vmem_call(
         cores_kernel,
-        shape((quarter * units // 128 + 16, 128), bf16),
+        [shape((quarter * units // 128 + 16, 128), bf16), shape((1, cases), f32)],
         flops=4 * quarter * units,
         nbytes=8 * quarter * units,
         n_in=4,
     )(far_own, far_got, stat, stat_twin)
-    part = along(2, chunk)
+    chunk, near_send = lax.optimization_barrier((chunk, near_send))
+    part, near_got = along(2, chunk), along(1, near_send)
+    envs = [along(4 * m, env) for m in range(nz - 1, 0, -1)]
     outs = vmem_call(
-        chips_kernel,
-        [shape((rows * units // 128, 128), f32), shape((1, cases), f32)]
-        + [shape((rows * units // 128 + 16, 128), bf16)] * (nz - 1),
+        functools.partial(chips_kernel, nz),
+        [shape((nz, cases), f32), shape((rows * units // 128, 128), f32)]
+        + [shape((rows * units // 128, 128), bf16)] * (nz - 1),
         flops=6 * quarter * units,
         nbytes=10 * quarter * units,
-        n_in=5,
-    )(near_own, near_got, stat, stat_twin, part)
-    own, env = outs[:2]
-    parts = [along(4 * m, x) for m, x in enumerate(outs[2:], start=1)]
+        n_in=5 + nz,
+    )(near_own, near_got, stat, stat_twin, part, env, *envs[::-1])
+    stack, own = outs[:2]
+    stack_far = along(2, stack)
+    parts = [along(4 * m, outs[1 + m]) for m in range(nz - 1, 0, -1)]
 
     coef, gain = vmem_call(
         coef_kernel,
         [shape((6, width), f32), shape((rows, 128), f32)],
         flops=14 * cases * width,
         nbytes=16 * cases * width,
-        n_in=7 + len(parts),
-    )(cot, stat, env, s0, s1, w0, w1, *parts)
+        n_in=8,
+    )(cot, stat, stack, stack_far, s0, s1, w0, w1)
     bit = 1
     while bit < n_case:
         coef = coef + lax.ppermute(coef, "case", [(i, i ^ bit) for i in range(n_case)])

time: 45.7 us -> 43.8 us (0.958)
  waiting for transfers between devices: 16.1 us -> 9.66 us
  starting transfers between devices: 15.6 us -> 20.6 us
  local copies, waits for them, and re-layouts: 0.7 us -> 0.02 us
    ppermute x13 -> x17, waiting for transfers between devices: 14.5 us -> 7.24 us  [along(): return lax.ppermute(x, 'elem', [(i, i ^ bits) for i in range(n)])]
    ppermute x13 -> x17, starting transfers between devices: 14.1 us -> 19.1 us  [along(): return lax.ppermute(x, 'elem', [(i, i ^ bits) for i in range(n)])]
    pallas_call x2, Pallas kernels: 4.6 us -> 6.65 us  [main(): vmem_call(functools.partial(main_kernel, len(blocks), len(stats)), [shape...]
    pallas_call x1, Pallas kernels: 4.26 us -> 2.48 us  [per_device(): vmem_call(functools.partial(prep_kernel, n), [shape((units, comps * width...]
    ppermute x1, waiting for transfers between devices: 1.64 us -> 2.43 us  [per_device(): lax.ppermute(coef, 'case', [(i, i ^ bit) for i in range(n_case)])]
    unnamed x12 -> x10, local copies, waits for them, and re-layouts: 0.7 us -> 0.02 us
  transfers between devices with their start and end apart: 14 -> 18, of which waited for: 8 -> 7; matrix products, arithmetic and copies ran while one was open for 0% -> 1% of each run, Pallas kernels for 17% -> 17%
where the time goes in v7:
time: 43.8 us; the launch traced here: 43.7 us
  starting transfers between devices  20.6 us (47%)
  Pallas kernels  12 us (27%)
  waiting for transfers between devices  9.66 us (22%)
  between operations  0.78 us (2%)
  other arithmetic  0.62 us (1%)
    ppermute x17, starting transfers between devices, along(): return lax.ppermute(x, 'elem', [(i, i ^ bits) for i in range(n)])  19.1 us
    ppermute x17, waiting for transfers between devices, along(): return lax.ppermute(x, 'elem', [(i, i ^ bits) for i in range(n)])  7.24 us
    pallas_call x2, Pallas kernels, main(): vmem_call(functools.partial(main_kernel, len(blocks), len(stats)), [shape...  6.65 us
    pallas_call x1, Pallas kernels, per_device(): vmem_call(functools.partial(prep_kernel, n), [shape((units, comps * width...  2.48 us
    ppermute x1, waiting for transfers between devices, per_device(): lax.ppermute(coef, 'case', [(i, i ^ bit) for i in range(n_case)])  2.43 us
    ppermute x1, starting transfers between devices, per_device(): lax.ppermute(coef, 'case', [(i, i ^ bit) for i in range(n_case)])  1.55 us
    pallas_call x1, Pallas kernels, per_device(): vmem_call(coef_kernel, [shape((6, width), f32), shape((rows, 128), f32)],...  1.51 us
  transfers between devices with their start and end apart: 18, of which 7 were waited for; matrix products, arithmetic and copies ran while one was open for 1% of the time, Pallas kernels for 17%

profile of v7, /device:TPU:0, one launch (start us, length us, event | category | flops | bytes accessed | tf_op | source)
XLA Modules:
  0.0 43.7 jit_solution(4855021501324673046)
XLA Ops:
  0.6 0.0 copy-start
  0.6 0.0 copy-start.1
  0.7 0.0 copy-start.2
  0.7 0.0 copy-start.4
  0.7 0.0 copy-start.3
  0.7 5.1 %collective-permute-start = (bf16[32,512]{1,0:T(8,128)(2,1)}, bf16[32,512]{1,0:T(8,128)(2,1)S(1)}, u32[]{:S(2)}, u32[]{:S(2)}) collective-permute-start(bf16[32,512]{1,0:T(8,128)(2,1)} %refs_3_.1), channel_id=1, source_target_pairs={{0,12},{1,13},{2,14},{3,15},{4,8},{5,9},{6,10},{7,11},{8,4},{9,5},... | collective-permute-start | bytes 98312 | tf_op jit(solution)/shard_map/ppermute | solution.py:332
  5.8 0.0 collective-permute-start.1
  5.8 0.6 %collective-permute-start.2 = (bf16[32,512]{1,0:T(8,128)(2,1)}, bf16[32,512]{1,0:T(8,128)(2,1)S(1)}, u32[]{:S(2)}, u32[]{:S(2)}) collective-permute-start(bf16[32,512]{1,0:T(8,128)(2,1)} %refs_3_.1), channel_id=1, source_target_pairs={{0,4},{1,5},{2,6},{3,7},{4,0},{5,1},{6,2},{7,3},{8,12},{9,13},{10,... | collective-permute-start | bytes 98312 | tf_op jit(solution)/shard_map/ppermute | solution.py:332
  6.4 2.5 %shard_map.95 = (bf16[512,3072]{1,0:T(8,128)(2,1)S(1)}, f32[1,512]{1,0:T(1,128)S(1)}) custom-call(s32[1]{0:T(128)} %bitcast.me_ref, bf16[3,512,1024]{2,1,0:T(8,128)(2,1)} %bitcast.10, s32[3,8,512]{2,1,0:T(8,128)} %bitcast.11, f32[1,512]{1,0:T(1,128)} %bitcast.12), custom_call_target="tpu_custom_call" | custom-call | flops 1572864 | bytes 6291456 | tf_op jit(solution)/shard_map/pallas_call | solution.py:335
  8.9 0.0 collective-permute-done.refs_0_
  8.9 1.9 %collective-permute-done.1.refs_1_ = bf16[32,512]{1,0:T(8,128)(2,1)S(1)} collective-permute-done((bf16[32,512]{1,0:T(8,128)(2,1)}, bf16[32,512]{1,0:T(8,128)(2,1)S(1)}, u32[]{:S(2)}, u32[]{:S(2)}) %collective-permute-start.1) | collective-permute-done | bytes 32800 | tf_op jit(solution)/shard_map/ppermute | solution.py:332
  10.8 0.0 collective-permute-done.2.refs_2_
  10.8 0.0 copy-done
  10.8 0.1 collective-permute-start.4
  10.9 1.6 %collective-permute-start.3 = (bf16[128,512]{1,0:T(8,128)(2,1)S(1)}, bf16[128,512]{1,0:T(8,128)(2,1)S(1)}, u32[]{:S(2)}, u32[]{:S(2)}) collective-permute-start(bf16[128,512]{1,0:T(8,128)(2,1)S(1)} %shard_map.96.refs_0_), channel_id=1, source_target_pairs={{0,2},{1,3},{2,0},{3,1},{4,6},{5,7},{6,4},{7,5},{8,10},{9,11},{10,... | collective-permute-start | bytes 393224 | tf_op jit(solution)/shard_map/ppermute | solution.py:332
  12.5 0.0 collective-permute-done.4.refs_1_
  12.5 0.0 copy-done.1
  12.5 0.0 copy-done.2
  12.5 0.0 copy-done.4
  12.5 0.0 copy-done.3
  12.5 3.3 %shard_map.97 = (f32[128,512]{1,0:T(8,128)S(1)}, f32[128,512]{1,0:T(8,128)S(1)}, f32[2,256]{1,0:T(2,128)S(1)}, f32[256,3072]{1,0:T(8,128)S(1)}, f32[256,1024]{1,0:T(8,128)S(1)}) custom-call(bf16[512,3072]{1,0:T(8,128)(2,1)S(1)} %get-tuple-element.31.f_ref, f32[2,1024]{1,0:T(2,128)S(1)} %copy-done.2, f32[3,1024]{1,0:T(4,128)S(1)} %copy-done.1, ...), custom_call_target="tpu_custom_call" | custom-call | flops 2415919104 | bytes 7340032 | tf_op jit(solution)/shard_map/pallas_call | solution.py:364
  15.9 1.0 %collective-permute-done.3.refs_0_ = bf16[128,512]{1,0:T(8,128)(2,1)S(1)} collective-permute-done((bf16[128,512]{1,0:T(8,128)(2,1)S(1)}, bf16[128,512]{1,0:T(8,128)(2,1)S(1)}, u32[]{:S(2)}, u32[]{:S(2)}) %collective-permute-start.3) | collective-permute-done | bytes 131104 | tf_op jit(solution)/shard_map/ppermute | solution.py:332
  16.8 0.0 collective-permute-start.5
  16.8 1.3 %collective-permute-done.5.refs_1_ = bf16[128,512]{1,0:T(8,128)(2,1)S(1)} collective-permute-done((bf16[128,512]{1,0:T(8,128)(2,1)S(1)}, bf16[128,512]{1,0:T(8,128)(2,1)S(1)}, u32[]{:S(2)}, u32[]{:S(2)}) %collective-permute-start.5) | collective-permute-done | bytes 131104 | tf_op jit(solution)/shard_map/ppermute | solution.py:332
  18.2 3.3 %shard_map.98 = (f32[128,512]{1,0:T(8,128)S(1)}, f32[128,512]{1,0:T(8,128)S(1)}, f32[2,512]{1,0:T(2,128)S(1)}, f32[256,3072]{1,0:T(8,128)S(1)}, f32[256,1024]{1,0:T(8,128)S(1)}) custom-call(bf16[512,3072]{1,0:T(8,128)(2,1)S(1)} %get-tuple-element.31.f_ref, f32[2,1024]{1,0:T(2,128)S(1)} %copy-done.2, f32[3,1024]{1,0:T(4,128)S(1)} %copy-done.1, ...), custom_call_target="tpu_custom_call" | custom-call | flops 2415919104 | bytes 7340032 | tf_op jit(solution)/shard_map/pallas_call | solution.py:364
  21.5 0.2 collective-permute-start.6
  21.7 0.4 collective-permute-start.7
  22.1 1.0 %collective-permute-done.7.twin_ref = f32[2,512]{1,0:T(2,128)S(1)} collective-permute-done((f32[2,512]{1,0:T(2,128)S(1)}, f32[2,512]{1,0:T(2,128)S(1)}, u32[]{:S(2)}, u32[]{:S(2)}) %collective-permute-start.7) | collective-permute-done | bytes 4128 | tf_op jit(solution)/shard_map/ppermute | solution.py:332
  23.1 0.0 collective-permute-done.6.got_ref
  23.1 0.2 shard_map.99
  23.4 0.2 collective-permute-start.8
  23.6 1.5 %collective-permute-start.9 = (bf16[528,128]{1,0:T(8,128)(2,1)S(1)}, bf16[528,128]{1,0:T(8,128)(2,1)S(1)}, u32[]{:S(2)}, u32[]{:S(2)}) collective-permute-start(bf16[528,128]{1,0:T(8,128)(2,1)S(1)} %get-tuple-element.43), channel_id=1, source_target_pairs={{0,2},{1,3},{2,0},{3,1},{4,6},{5,7},{6,4},{7,5},{8,10},{9,11},{10,... | collective-permute-start | bytes 405512 | tf_op jit(solution)/shard_map/ppermute | solution.py:332
  25.1 1.9 %collective-permute-start.12 = (f32[1,512]{1,0:T(1,128)S(1)}, f32[1,512]{1,0:T(1,128)S(1)}, u32[]{:S(2)}, u32[]{:S(2)}) collective-permute-start(f32[1,512]{1,0:T(1,128)S(1)} %get-tuple-element.44.refs_0_), channel_id=1, source_target_pairs={{0,12},{1,13},{2,14},{3,15},{4,8},{5,9},{6,10},{7,11},{8,4},{9,5},... | collective-permute-start | bytes 6152 | tf_op jit(solution)/shard_map/ppermute | solution.py:332
  27.0 0.1 collective-permute-start.11
  27.1 2.4 %collective-permute-start.10 = (f32[1,512]{1,0:T(1,128)S(1)}, f32[1,512]{1,0:T(1,128)S(1)}, u32[]{:S(2)}, u32[]{:S(2)}) collective-permute-start(f32[1,512]{1,0:T(1,128)S(1)} %get-tuple-element.44.refs_0_), channel_id=1, source_target_pairs={{0,4},{1,5},{2,6},{3,7},{4,0},{5,1},{6,2},{7,3},{8,12},{9,13},{10,... | collective-permute-start | bytes 6152 | tf_op jit(solution)/shard_map/ppermute | solution.py:332
  29.5 1.0 %collective-permute-done.12.refs_3_ = f32[1,512]{1,0:T(1,128)S(1)} collective-permute-done((f32[1,512]{1,0:T(1,128)S(1)}, f32[1,512]{1,0:T(1,128)S(1)}, u32[]{:S(2)}, u32[]{:S(2)}) %collective-permute-start.12) | collective-permute-done | bytes 2080 | tf_op jit(solution)/shard_map/ppermute | solution.py:332
  30.5 1.0 %collective-permute-done.11.refs_2_ = f32[1,512]{1,0:T(1,128)S(1)} collective-permute-done((f32[1,512]{1,0:T(1,128)S(1)}, f32[1,512]{1,0:T(1,128)S(1)}, u32[]{:S(2)}, u32[]{:S(2)}) %collective-permute-start.11) | collective-permute-done | bytes 2080 | tf_op jit(solution)/shard_map/ppermute | solution.py:332
  31.5 0.0 collective-permute-done.10.refs_1_
  31.5 0.0 collective-permute-done.9.part_ref
  31.5 0.0 collective-permute-done.8.got_ref
  31.5 0.3 shard_map.100
  31.8 0.6 %collective-permute-start.13 = (f32[4,512]{1,0:T(4,128)S(1)}, f32[4,512]{1,0:T(4,128)S(1)}, u32[]{:S(2)}, u32[]{:S(2)}) collective-permute-start(f32[4,512]{1,0:T(4,128)S(1)} %get-tuple-element.45.near_ref), channel_id=1, source_target_pairs={{0,2},{1,3},{2,0},{3,1},{4,6},{5,7},{6,4},{7,5},{8,10},{9,11},{10,... | collective-permute-start | bytes 24584 | tf_op jit(solution)/shard_map/ppermute | solution.py:332
  32.4 2.1 %collective-permute-start.14 = (bf16[128,128]{1,0:T(8,128)(2,1)S(1)}, bf16[128,128]{1,0:T(8,128)(2,1)S(1)}, u32[]{:S(2)}, u32[]{:S(2)}) collective-permute-start(bf16[128,128]{1,0:T(8,128)(2,1)S(1)} %get-tuple-element.52), channel_id=1, source_target_pairs={{0,12},{1,13},{2,14},{3,15},{4,8},{5,9},{6,10},{7,11},{8,4},{9,5},... | collective-permute-start | bytes 98312 | tf_op jit(solution)/shard_map/ppermute | solution.py:332
  34.5 0.9 %collective-permute-start.15 = (bf16[128,128]{1,0:T(8,128)(2,1)S(1)}, bf16[128,128]{1,0:T(8,128)(2,1)S(1)}, u32[]{:S(2)}, u32[]{:S(2)}) collective-permute-start(bf16[128,128]{1,0:T(8,128)(2,1)S(1)} %get-tuple-element.53), channel_id=1, source_target_pairs={{0,8},{1,9},{2,10},{3,11},{4,12},{5,13},{6,14},{7,15},{8,0},{9,1},... | collective-permute-start | bytes 98312 | tf_op jit(solution)/shard_map/ppermute | solution.py:332
  35.4 1.3 %collective-permute-start.16 = (bf16[128,128]{1,0:T(8,128)(2,1)S(1)}, bf16[128,128]{1,0:T(8,128)(2,1)S(1)}, u32[]{:S(2)}, u32[]{:S(2)}) collective-permute-start(bf16[128,128]{1,0:T(8,128)(2,1)S(1)} %get-tuple-element.54), channel_id=1, source_target_pairs={{0,4},{1,5},{2,6},{3,7},{4,0},{5,1},{6,2},{7,3},{8,12},{9,13},{10,... | collective-permute-start | bytes 98312 | tf_op jit(solution)/shard_map/ppermute | solution.py:332
  36.8 0.0 collective-permute-done.13.far_ref
  36.8 1.5 %shard_map.101 = (f32[6,1024]{1,0:T(8,128)S(1)}, f32[32,128]{1,0:T(8,128)S(1)}) custom-call(f32[1,512]{1,0:T(1,128)S(1)} %get-tuple-element.29.cot_ref, f32[2,512]{1,0:T(2,128)S(1)} %get-tuple-element.36.stat_ref, f32[4,512]{1,0:T(4,128)S(1)} %get-tuple-element.45.near_ref, f32[4,512]{1,0:T(4,128)S(1)} %collective-permute-done.13.far_ref, ...), custom_call_target="tpu_custom_call" | custom-call | flops 7340032 | bytes 8388608 | tf_op jit(solution)/shard_map/pallas_call | solution.py:422
  38.3 1.6 %collective-permute-start.17 = (f32[6,1024]{1,0:T(8,128)S(1)}, f32[6,1024]{1,0:T(8,128)S(1)}, u32[]{:S(2)}, u32[]{:S(2)}) collective-permute-start(f32[6,1024]{1,0:T(8,128)S(1)} %get-tuple-element.55), channel_id=1, source_target_pairs={{0,16},{16,0},{1,17},{17,1},{2,18},{18,2},{3,19},{19,3},{4,20},{20... | collective-permute-start | bytes 73736 | tf_op jit(solution)/shard_map/ppermute | solution.py:431
  39.8 2.4 %collective-permute-done.17 = f32[6,1024]{1,0:T(8,128)S(1)} collective-permute-done((f32[6,1024]{1,0:T(8,128)S(1)}, f32[6,1024]{1,0:T(8,128)S(1)}, u32[]{:S(2)}, u32[]{:S(2)}) %collective-permute-start.17) | collective-permute-done | bytes 24608 | tf_op jit(solution)/shard_map/ppermute | solution.py:431
  42.3 0.6 %add.3 = f32[6,1024]{1,0:T(8,128)} add(f32[6,1024]{1,0:T(8,128)S(1)} %get-tuple-element.55, f32[6,1024]{1,0:T(8,128)S(1)} %collective-permute-done.17) | non-fusion elementwise | flops 6144 | bytes 73728 | tf_op jit(solution)/shard_map/add | solution.py:431
  42.9 0.0 collective-permute-done.14.refs_0_
  42.9 0.0 collective-permute-done.15.refs_1_
  42.9 0.0 collective-permute-done.16.refs_2_
  42.9 0.8 %shard_map.102 = f32[32,512]{1,0:T(8,128)} custom-call(f32[32,128]{1,0:T(8,128)S(1)} %get-tuple-element.50.gain_ref, f32[128,128]{1,0:T(8,128)S(1)} %get-tuple-element.51.own_ref, bf16[128,128]{1,0:T(8,128)(2,1)S(1)} %collective-permute-done.14.refs_0_, bf16[128,128]{1,0:T(8,128)(2,1)S(1)} %collective-permute-done.15.refs_1_, ...), custom_call_target="tpu_custom_call" | custom-call | flops 131072 | bytes 131072 | tf_op jit(solution)/shard_map/pallas_call | solution.py:434
  (1 shorter events, 0.0 us)
Async XLA Ops:
  0.6 10.2 %copy-start = (bf16[32,512]{1,0:T(8,128)(2,1)S(1)}, bf16[32,512]{1,0:T(8,128)(2,1)}, u32[]{:S(2)}) copy-start(bf16[32,512]{1,0:T(8,128)(2,1)} %refs_3_.1) | copy-start | bytes 98308
  0.6 11.9 %copy-start.1 = (f32[3,1024]{1,0:T(4,128)S(1)}, f32[3,1024]{1,0:T(4,128)}, u32[]{:S(2)}) copy-start(f32[3,1024]{1,0:T(4,128)} %quad_ref.3) | copy-start | bytes 36868
  0.7 11.9 %copy-start.2 = (f32[2,1024]{1,0:T(2,128)S(1)}, f32[2,1024]{1,0:T(2,128)}, u32[]{:S(2)}) copy-start(f32[2,1024]{1,0:T(2,128)} %lin_ref.3) | copy-start | bytes 24580
  0.7 11.9 %copy-start.4 = (s32[1024]{0:T(1024)S(1)}, s32[1024]{0:T(1024)}, u32[]{:S(2)}) copy-start(s32[1024]{0:T(1024)} %param.14) | copy-start | bytes 12292
  0.7 11.9 %copy-start.3 = (f32[1024]{0:T(1024)S(1)}, f32[1024]{0:T(1024)}, u32[]{:S(2)}) copy-start(f32[1024]{0:T(1024)} %param.13) | copy-start | bytes 12292
  0.7 8.3 %collective-permute-start = (bf16[32,512]{1,0:T(8,128)(2,1)}, bf16[32,512]{1,0:T(8,128)(2,1)S(1)}, u32[]{:S(2)}, u32[]{:S(2)}) collective-permute-start(bf16[32,512]{1,0:T(8,128)(2,1)} %refs_3_.1), channel_id=1, source_target_pairs={{0,12},{1,13},{2,14},{3,15},{4,8},{5,9},{6,10},{7,11},{8,4},{9,5},... | collective-permute-start | bytes 98312 | tf_op jit(solution)/shard_map/ppermute | solution.py:332
  5.8 5.0 %collective-permute-start.1 = (bf16[32,512]{1,0:T(8,128)(2,1)}, bf16[32,512]{1,0:T(8,128)(2,1)S(1)}, u32[]{:S(2)}, u32[]{:S(2)}) collective-permute-start(bf16[32,512]{1,0:T(8,128)(2,1)} %refs_3_.1), channel_id=1, source_target_pairs={{0,8},{1,9},{2,10},{3,11},{4,12},{5,13},{6,14},{7,15},{8,0},{9,1},... | collective-permute-start | bytes 98312 | tf_op jit(solution)/shard_map/ppermute | solution.py:332
  5.8 5.0 %collective-permute-start.2 = (bf16[32,512]{1,0:T(8,128)(2,1)}, bf16[32,512]{1,0:T(8,128)(2,1)S(1)}, u32[]{:S(2)}, u32[]{:S(2)}) collective-permute-start(bf16[32,512]{1,0:T(8,128)(2,1)} %refs_3_.1), channel_id=1, source_target_pairs={{0,4},{1,5},{2,6},{3,7},{4,0},{5,1},{6,2},{7,3},{8,12},{9,13},{10,... | collective-permute-start | bytes 98312 | tf_op jit(solution)/shard_map/ppermute | solution.py:332
  10.8 1.7 %collective-permute-start.4 = (bf16[128,512]{1,0:T(8,128)(2,1)S(1)}, bf16[128,512]{1,0:T(8,128)(2,1)S(1)}, u32[]{:S(2)}, u32[]{:S(2)}) collective-permute-start(bf16[128,512]{1,0:T(8,128)(2,1)S(1)} %shard_map.96.refs_0_), channel_id=1, source_target_pairs={{0,1},{1,0},{2,3},{3,2},{4,5},{5,4},{6,7},{7,6},{8,9},{9,8},{10,11... | collective-permute-start | bytes 393224 | tf_op jit(solution)/shard_map/ppermute | solution.py:332
  10.9 5.9 %collective-permute-start.3 = (bf16[128,512]{1,0:T(8,128)(2,1)S(1)}, bf16[128,512]{1,0:T(8,128)(2,1)S(1)}, u32[]{:S(2)}, u32[]{:S(2)}) collective-permute-start(bf16[128,512]{1,0:T(8,128)(2,1)S(1)} %shard_map.96.refs_0_), channel_id=1, source_target_pairs={{0,2},{1,3},{2,0},{3,1},{4,6},{5,7},{6,4},{7,5},{8,10},{9,11},{10,... | collective-permute-start | bytes 393224 | tf_op jit(solution)/shard_map/ppermute | solution.py:332
  16.8 1.3 %collective-permute-start.5 = (bf16[128,512]{1,0:T(8,128)(2,1)S(1)}, bf16[128,512]{1,0:T(8,128)(2,1)S(1)}, u32[]{:S(2)}, u32[]{:S(2)}) collective-permute-start(bf16[128,512]{1,0:T(8,128)(2,1)S(1)} %collective-permute-done.3.refs_0_), channel_id=1, source_target_pairs={{0,1},{1,0},{2,3},{3,2},{4,5},{5,4},{6,7},{7,6},{8,9},{9,8},{10,11... | collective-permute-start | bytes 393224 | tf_op jit(solution)/shard_map/ppermute | solution.py:332
  21.5 1.6 %collective-permute-start.6 = (f32[128,512]{1,0:T(8,128)S(1)}, f32[128,512]{1,0:T(8,128)S(1)}, u32[]{:S(2)}, u32[]{:S(2)}) collective-permute-start(f32[128,512]{1,0:T(8,128)S(1)} %get-tuple-element.39), channel_id=1, source_target_pairs={{0,1},{1,0},{2,3},{3,2},{4,5},{5,4},{6,7},{7,6},{8,9},{9,8},{10,11... | collective-permute-start | bytes 786440 | tf_op jit(solution)/shard_map/ppermute | solution.py:332
  21.7 1.4 %collective-permute-start.7 = (f32[2,512]{1,0:T(2,128)S(1)}, f32[2,512]{1,0:T(2,128)S(1)}, u32[]{:S(2)}, u32[]{:S(2)}) collective-permute-start(f32[2,512]{1,0:T(2,128)S(1)} %get-tuple-element.36.stat_ref), channel_id=1, source_target_pairs={{0,1},{1,0},{2,3},{3,2},{4,5},{5,4},{6,7},{7,6},{8,9},{9,8},{10,11... | collective-permute-start | bytes 12296 | tf_op jit(solution)/shard_map/ppermute | solution.py:332
  23.4 8.1 %collective-permute-start.8 = (f32[128,512]{1,0:T(8,128)S(1)}, f32[128,512]{1,0:T(8,128)S(1)}, u32[]{:S(2)}, u32[]{:S(2)}) collective-permute-start(f32[128,512]{1,0:T(8,128)S(1)} %get-tuple-element.42), channel_id=1, source_target_pairs={{0,1},{1,0},{2,3},{3,2},{4,5},{5,4},{6,7},{7,6},{8,9},{9,8},{10,11... | collective-permute-start | bytes 786440 | tf_op jit(solution)/shard_map/ppermute | solution.py:332
  23.6 7.9 %collective-permute-start.9 = (bf16[528,128]{1,0:T(8,128)(2,1)S(1)}, bf16[528,128]{1,0:T(8,128)(2,1)S(1)}, u32[]{:S(2)}, u32[]{:S(2)}) collective-permute-start(bf16[528,128]{1,0:T(8,128)(2,1)S(1)} %get-tuple-element.43), channel_id=1, source_target_pairs={{0,2},{1,3},{2,0},{3,1},{4,6},{5,7},{6,4},{7,5},{8,10},{9,11},{10,... | collective-permute-start | bytes 405512 | tf_op jit(solution)/shard_map/ppermute | solution.py:332
  25.1 5.4 %collective-permute-start.12 = (f32[1,512]{1,0:T(1,128)S(1)}, f32[1,512]{1,0:T(1,128)S(1)}, u32[]{:S(2)}, u32[]{:S(2)}) collective-permute-start(f32[1,512]{1,0:T(1,128)S(1)} %get-tuple-element.44.refs_0_), channel_id=1, source_target_pairs={{0,12},{1,13},{2,14},{3,15},{4,8},{5,9},{6,10},{7,11},{8,4},{9,5},... | collective-permute-start | bytes 6152 | tf_op jit(solution)/shard_map/ppermute | solution.py:332
  27.0 4.5 %collective-permute-start.11 = (f32[1,512]{1,0:T(1,128)S(1)}, f32[1,512]{1,0:T(1,128)S(1)}, u32[]{:S(2)}, u32[]{:S(2)}) collective-permute-start(f32[1,512]{1,0:T(1,128)S(1)} %get-tuple-element.44.refs_0_), channel_id=1, source_target_pairs={{0,8},{1,9},{2,10},{3,11},{4,12},{5,13},{6,14},{7,15},{8,0},{9,1},... | collective-permute-start | bytes 6152 | tf_op jit(solution)/shard_map/ppermute | solution.py:332
  27.1 4.4 %collective-permute-start.10 = (f32[1,512]{1,0:T(1,128)S(1)}, f32[1,512]{1,0:T(1,128)S(1)}, u32[]{:S(2)}, u32[]{:S(2)}) collective-permute-start(f32[1,512]{1,0:T(1,128)S(1)} %get-tuple-element.44.refs_0_), channel_id=1, source_target_pairs={{0,4},{1,5},{2,6},{3,7},{4,0},{5,1},{6,2},{7,3},{8,12},{9,13},{10,... | collective-permute-start | bytes 6152 | tf_op jit(solution)/shard_map/ppermute | solution.py:332
  31.8 5.0 %collective-permute-start.13 = (f32[4,512]{1,0:T(4,128)S(1)}, f32[4,512]{1,0:T(4,128)S(1)}, u32[]{:S(2)}, u32[]{:S(2)}) collective-permute-start(f32[4,512]{1,0:T(4,128)S(1)} %get-tuple-element.45.near_ref), channel_id=1, source_target_pairs={{0,2},{1,3},{2,0},{3,1},{4,6},{5,7},{6,4},{7,5},{8,10},{9,11},{10,... | collective-permute-start | bytes 24584 | tf_op jit(solution)/shard_map/ppermute | solution.py:332
  32.4 10.5 %collective-permute-start.14 = (bf16[128,128]{1,0:T(8,128)(2,1)S(1)}, bf16[128,128]{1,0:T(8,128)(2,1)S(1)}, u32[]{:S(2)}, u32[]{:S(2)}) collective-permute-start(bf16[128,128]{1,0:T(8,128)(2,1)S(1)} %get-tuple-element.52), channel_id=1, source_target_pairs={{0,12},{1,13},{2,14},{3,15},{4,8},{5,9},{6,10},{7,11},{8,4},{9,5},... | collective-permute-start | bytes 98312 | tf_op jit(solution)/shard_map/ppermute | solution.py:332
  34.5 8.4 %collective-permute-start.15 = (bf16[128,128]{1,0:T(8,128)(2,1)S(1)}, bf16[128,128]{1,0:T(8,128)(2,1)S(1)}, u32[]{:S(2)}, u32[]{:S(2)}) collective-permute-start(bf16[128,128]{1,0:T(8,128)(2,1)S(1)} %get-tuple-element.53), channel_id=1, source_target_pairs={{0,8},{1,9},{2,10},{3,11},{4,12},{5,13},{6,14},{7,15},{8,0},{9,1},... | collective-permute-start | bytes 98312 | tf_op jit(solution)/shard_map/ppermute | solution.py:332
  35.4 7.5 %collective-permute-start.16 = (bf16[128,128]{1,0:T(8,128)(2,1)S(1)}, bf16[128,128]{1,0:T(8,128)(2,1)S(1)}, u32[]{:S(2)}, u32[]{:S(2)}) collective-permute-start(bf16[128,128]{1,0:T(8,128)(2,1)S(1)} %get-tuple-element.54), channel_id=1, source_target_pairs={{0,4},{1,5},{2,6},{3,7},{4,0},{5,1},{6,2},{7,3},{8,12},{9,13},{10,... | collective-permute-start | bytes 98312 | tf_op jit(solution)/shard_map/ppermute | solution.py:332
  38.3 4.0 %collective-permute-start.17 = (f32[6,1024]{1,0:T(8,128)S(1)}, f32[6,1024]{1,0:T(8,128)S(1)}, u32[]{:S(2)}, u32[]{:S(2)}) collective-permute-start(f32[6,1024]{1,0:T(8,128)S(1)} %get-tuple-element.55), channel_id=1, source_target_pairs={{0,16},{16,0},{1,17},{17,1},{2,18},{18,2},{3,19},{19,3},{4,20},{20... | collective-permute-start | bytes 73736 | tf_op jit(solution)/shard_map/ppermute | solution.py:431

commit v8 on v7

--- a/solution.py
+++ b/solution.py
@@ -257,7 +257,7 @@
     own_out_ref[...] = jnp.concatenate([p[0:rows] for p in parts], axis=0)
     for m, ref in enumerate(out_refs):
         r = slice((m + 1) * rows, (m + 2) * rows)
-        ref[...] = jnp.concatenate([p[r] for p in parts], axis=0).astype(jnp.bfloat16)
+        ref[...] = jnp.concatenate([p[r] for p in parts], axis=0)
 
 
 def coef_kernel(cot_ref, stat_ref, near_ref, far_ref, s0_ref, s1_ref, w0_ref, w1_ref, coef_ref, gain_ref):
@@ -313,8 +313,7 @@
         r = slice(c * rows, (c + 1) * rows)
         value = own_ref[r, :] * gain_ref[:, 0:1]
         for m, ref in enumerate(part_refs):
-            part = ref[...].astype(jnp.float32)[r]
-            value = value + part * gain_ref[:, m + 1 : m + 2]
+            value = value + ref[r, :] * gain_ref[:, m + 1 : m + 2]
         out_ref[:, c * 128 : (c + 1) * 128] = value
 
 
@@ -410,7 +409,7 @@
     outs = vmem_call(
         functools.partial(chips_kernel, nz),
         [shape((nz, cases), f32), shape((rows * units // 128, 128), f32)]
-        + [shape((rows * units // 128, 128), bf16)] * (nz - 1),
+        + [shape((rows * units // 128, 128), f32)] * (nz - 1),
         flops=6 * quarter * units,
         nbytes=10 * quarter * units,
         n_in=5 + nz,

time: 43.8 us -> 47 us (1.073)
  waiting for transfers between devices: 9.66 us -> 12.8 us
    ppermute x17, waiting for transfers between devices: 7.24 us -> 10.4 us  [along(): return lax.ppermute(x, 'elem', [(i, i ^ bits) for i in range(n)])]
  transfers between devices with their start and end apart: 18 -> 18, of which waited for: 7 -> 8; matrix products, arithmetic and copies ran while one was open for 1% -> 1% of each run, Pallas kernels for 17% -> 16%
where the time goes in v8:
time: 47 us; the launch traced here: 46.8 us
  starting transfers between devices  20.6 us (44%)
  waiting for transfers between devices  12.8 us (27%)
  Pallas kernels  12 us (26%)
  between operations  0.78 us (2%)
  other arithmetic  0.62 us (1%)
    ppermute x17, starting transfers between devices, along(): return lax.ppermute(x, 'elem', [(i, i ^ bits) for i in range(n)])  19.1 us
    ppermute x17, waiting for transfers between devices, along(): return lax.ppermute(x, 'elem', [(i, i ^ bits) for i in range(n)])  10.4 us
    pallas_call x2, Pallas kernels, main(): vmem_call(functools.partial(main_kernel, len(blocks), len(stats)), [shape...  6.65 us
    pallas_call x1, Pallas kernels, per_device(): vmem_call(functools.partial(prep_kernel, n), [shape((units, comps * width...  2.48 us
    ppermute x1, waiting for transfers between devices, per_device(): lax.ppermute(coef, 'case', [(i, i ^ bit) for i in range(n_case)])  2.42 us
    ppermute x1, starting transfers between devices, per_device(): lax.ppermute(coef, 'case', [(i, i ^ bit) for i in range(n_case)])  1.56 us
    pallas_call x1, Pallas kernels, per_device(): vmem_call(coef_kernel, [shape((6, width), f32), shape((rows, 128), f32)],...  1.51 us
  transfers between devices with their start and end apart: 18, of which 8 were waited for; matrix products, arithmetic and copies ran while one was open for 1% of the time, Pallas kernels for 16%

profile of v8, /device:TPU:0, one launch (start us, length us, event | category | flops | bytes accessed | tf_op | source)
XLA Modules:
  0.0 46.8 jit_solution(12074489540285463293)
XLA Ops:
  0.6 0.0 copy-start
  0.6 0.0 copy-start.1
  0.7 0.0 copy-start.2
  0.7 0.0 copy-start.4
  0.7 0.0 copy-start.3
  0.7 5.1 %collective-permute-start = (bf16[32,512]{1,0:T(8,128)(2,1)}, bf16[32,512]{1,0:T(8,128)(2,1)S(1)}, u32[]{:S(2)}, u32[]{:S(2)}) collective-permute-start(bf16[32,512]{1,0:T(8,128)(2,1)} %refs_3_.1), channel_id=1, source_target_pairs={{0,12},{1,13},{2,14},{3,15},{4,8},{5,9},{6,10},{7,11},{8,4},{9,5},... | collective-permute-start | bytes 98312 | tf_op jit(solution)/shard_map/ppermute | solution.py:331
  5.8 0.0 collective-permute-start.1
  5.8 0.6 %collective-permute-start.2 = (bf16[32,512]{1,0:T(8,128)(2,1)}, bf16[32,512]{1,0:T(8,128)(2,1)S(1)}, u32[]{:S(2)}, u32[]{:S(2)}) collective-permute-start(bf16[32,512]{1,0:T(8,128)(2,1)} %refs_3_.1), channel_id=1, source_target_pairs={{0,4},{1,5},{2,6},{3,7},{4,0},{5,1},{6,2},{7,3},{8,12},{9,13},{10,... | collective-permute-start | bytes 98312 | tf_op jit(solution)/shard_map/ppermute | solution.py:331
  6.4 2.5 %shard_map.95 = (bf16[512,3072]{1,0:T(8,128)(2,1)S(1)}, f32[1,512]{1,0:T(1,128)S(1)}) custom-call(s32[1]{0:T(128)} %bitcast.me_ref, bf16[3,512,1024]{2,1,0:T(8,128)(2,1)} %bitcast.10, s32[3,8,512]{2,1,0:T(8,128)} %bitcast.11, f32[1,512]{1,0:T(1,128)} %bitcast.12), custom_call_target="tpu_custom_call" | custom-call | flops 1572864 | bytes 6291456 | tf_op jit(solution)/shard_map/pallas_call | solution.py:334
  8.9 0.0 collective-permute-done.refs_0_
  8.9 1.9 %collective-permute-done.1.refs_1_ = bf16[32,512]{1,0:T(8,128)(2,1)S(1)} collective-permute-done((bf16[32,512]{1,0:T(8,128)(2,1)}, bf16[32,512]{1,0:T(8,128)(2,1)S(1)}, u32[]{:S(2)}, u32[]{:S(2)}) %collective-permute-start.1) | collective-permute-done | bytes 32800 | tf_op jit(solution)/shard_map/ppermute | solution.py:331
  10.8 0.0 collective-permute-done.2.refs_2_
  10.8 0.0 copy-done
  10.8 0.1 collective-permute-start.4
  10.9 1.6 %collective-permute-start.3 = (bf16[128,512]{1,0:T(8,128)(2,1)S(1)}, bf16[128,512]{1,0:T(8,128)(2,1)S(1)}, u32[]{:S(2)}, u32[]{:S(2)}) collective-permute-start(bf16[128,512]{1,0:T(8,128)(2,1)S(1)} %shard_map.96.refs_0_), channel_id=1, source_target_pairs={{0,2},{1,3},{2,0},{3,1},{4,6},{5,7},{6,4},{7,5},{8,10},{9,11},{10,... | collective-permute-start | bytes 393224 | tf_op jit(solution)/shard_map/ppermute | solution.py:331
  12.5 0.0 collective-permute-done.4.refs_1_
  12.5 0.0 copy-done.1
  12.5 0.0 copy-done.2
  12.5 0.0 copy-done.4
  12.5 0.0 copy-done.3
  12.5 3.3 %shard_map.97 = (f32[128,512]{1,0:T(8,128)S(1)}, f32[128,512]{1,0:T(8,128)S(1)}, f32[2,256]{1,0:T(2,128)S(1)}, f32[256,3072]{1,0:T(8,128)S(1)}, f32[256,1024]{1,0:T(8,128)S(1)}) custom-call(bf16[512,3072]{1,0:T(8,128)(2,1)S(1)} %get-tuple-element.31.f_ref, f32[2,1024]{1,0:T(2,128)S(1)} %copy-done.2, f32[3,1024]{1,0:T(4,128)S(1)} %copy-done.1, ...), custom_call_target="tpu_custom_call" | custom-call | flops 2415919104 | bytes 7340032 | tf_op jit(solution)/shard_map/pallas_call | solution.py:363
  15.9 1.0 %collective-permute-done.3.refs_0_ = bf16[128,512]{1,0:T(8,128)(2,1)S(1)} collective-permute-done((bf16[128,512]{1,0:T(8,128)(2,1)S(1)}, bf16[128,512]{1,0:T(8,128)(2,1)S(1)}, u32[]{:S(2)}, u32[]{:S(2)}) %collective-permute-start.3) | collective-permute-done | bytes 131104 | tf_op jit(solution)/shard_map/ppermute | solution.py:331
  16.8 0.0 collective-permute-start.5
  16.8 1.3 %collective-permute-done.5.refs_1_ = bf16[128,512]{1,0:T(8,128)(2,1)S(1)} collective-permute-done((bf16[128,512]{1,0:T(8,128)(2,1)S(1)}, bf16[128,512]{1,0:T(8,128)(2,1)S(1)}, u32[]{:S(2)}, u32[]{:S(2)}) %collective-permute-start.5) | collective-permute-done | bytes 131104 | tf_op jit(solution)/shard_map/ppermute | solution.py:331
  18.2 3.3 %shard_map.98 = (f32[128,512]{1,0:T(8,128)S(1)}, f32[128,512]{1,0:T(8,128)S(1)}, f32[2,512]{1,0:T(2,128)S(1)}, f32[256,3072]{1,0:T(8,128)S(1)}, f32[256,1024]{1,0:T(8,128)S(1)}) custom-call(bf16[512,3072]{1,0:T(8,128)(2,1)S(1)} %get-tuple-element.31.f_ref, f32[2,1024]{1,0:T(2,128)S(1)} %copy-done.2, f32[3,1024]{1,0:T(4,128)S(1)} %copy-done.1, ...), custom_call_target="tpu_custom_call" | custom-call | flops 2415919104 | bytes 7340032 | tf_op jit(solution)/shard_map/pallas_call | solution.py:363
  21.5 0.2 collective-permute-start.6
  21.7 0.4 collective-permute-start.7
  22.1 1.0 %collective-permute-done.7.twin_ref = f32[2,512]{1,0:T(2,128)S(1)} collective-permute-done((f32[2,512]{1,0:T(2,128)S(1)}, f32[2,512]{1,0:T(2,128)S(1)}, u32[]{:S(2)}, u32[]{:S(2)}) %collective-permute-start.7) | collective-permute-done | bytes 4128 | tf_op jit(solution)/shard_map/ppermute | solution.py:331
  23.1 0.0 collective-permute-done.6.got_ref
  23.1 0.2 shard_map.99
  23.4 0.2 collective-permute-start.8
  23.6 1.5 %collective-permute-start.9 = (bf16[528,128]{1,0:T(8,128)(2,1)S(1)}, bf16[528,128]{1,0:T(8,128)(2,1)S(1)}, u32[]{:S(2)}, u32[]{:S(2)}) collective-permute-start(bf16[528,128]{1,0:T(8,128)(2,1)S(1)} %get-tuple-element.43), channel_id=1, source_target_pairs={{0,2},{1,3},{2,0},{3,1},{4,6},{5,7},{6,4},{7,5},{8,10},{9,11},{10,... | collective-permute-start | bytes 405512 | tf_op jit(solution)/shard_map/ppermute | solution.py:331
  25.1 1.9 %collective-permute-start.12 = (f32[1,512]{1,0:T(1,128)S(1)}, f32[1,512]{1,0:T(1,128)S(1)}, u32[]{:S(2)}, u32[]{:S(2)}) collective-permute-start(f32[1,512]{1,0:T(1,128)S(1)} %get-tuple-element.44.refs_0_), channel_id=1, source_target_pairs={{0,12},{1,13},{2,14},{3,15},{4,8},{5,9},{6,10},{7,11},{8,4},{9,5},... | collective-permute-start | bytes 6152 | tf_op jit(solution)/shard_map/ppermute | solution.py:331
  27.0 0.1 collective-permute-start.11
  27.1 2.4 %collective-permute-start.10 = (f32[1,512]{1,0:T(1,128)S(1)}, f32[1,512]{1,0:T(1,128)S(1)}, u32[]{:S(2)}, u32[]{:S(2)}) collective-permute-start(f32[1,512]{1,0:T(1,128)S(1)} %get-tuple-element.44.refs_0_), channel_id=1, source_target_pairs={{0,4},{1,5},{2,6},{3,7},{4,0},{5,1},{6,2},{7,3},{8,12},{9,13},{10,... | collective-permute-start | bytes 6152 | tf_op jit(solution)/shard_map/ppermute | solution.py:331
  29.5 1.0 %collective-permute-done.12.refs_3_ = f32[1,512]{1,0:T(1,128)S(1)} collective-permute-done((f32[1,512]{1,0:T(1,128)S(1)}, f32[1,512]{1,0:T(1,128)S(1)}, u32[]{:S(2)}, u32[]{:S(2)}) %collective-permute-start.12) | collective-permute-done | bytes 2080 | tf_op jit(solution)/shard_map/ppermute | solution.py:331
  30.5 1.0 %collective-permute-done.11.refs_2_ = f32[1,512]{1,0:T(1,128)S(1)} collective-permute-done((f32[1,512]{1,0:T(1,128)S(1)}, f32[1,512]{1,0:T(1,128)S(1)}, u32[]{:S(2)}, u32[]{:S(2)}) %collective-permute-start.11) | collective-permute-done | bytes 2080 | tf_op jit(solution)/shard_map/ppermute | solution.py:331
  31.5 0.0 collective-permute-done.10.refs_1_
  31.5 0.0 collective-permute-done.9.part_ref
  31.5 0.0 collective-permute-done.8.got_ref
  31.5 0.3 shard_map.100
  31.8 2.2 %collective-permute-start.14 = (f32[128,128]{1,0:T(8,128)S(1)}, f32[128,128]{1,0:T(8,128)S(1)}, u32[]{:S(2)}, u32[]{:S(2)}) collective-permute-start(f32[128,128]{1,0:T(8,128)S(1)} %get-tuple-element.52), channel_id=1, source_target_pairs={{0,12},{1,13},{2,14},{3,15},{4,8},{5,9},{6,10},{7,11},{8,4},{9,5},... | collective-permute-start | bytes 196616 | tf_op jit(solution)/shard_map/ppermute | solution.py:331
  34.0 0.9 %collective-permute-start.15 = (f32[128,128]{1,0:T(8,128)S(1)}, f32[128,128]{1,0:T(8,128)S(1)}, u32[]{:S(2)}, u32[]{:S(2)}) collective-permute-start(f32[128,128]{1,0:T(8,128)S(1)} %get-tuple-element.53), channel_id=1, source_target_pairs={{0,8},{1,9},{2,10},{3,11},{4,12},{5,13},{6,14},{7,15},{8,0},{9,1},... | collective-permute-start | bytes 196616 | tf_op jit(solution)/shard_map/ppermute | solution.py:331
  34.9 1.3 %collective-permute-start.16 = (f32[128,128]{1,0:T(8,128)S(1)}, f32[128,128]{1,0:T(8,128)S(1)}, u32[]{:S(2)}, u32[]{:S(2)}) collective-permute-start(f32[128,128]{1,0:T(8,128)S(1)} %get-tuple-element.54), channel_id=1, source_target_pairs={{0,4},{1,5},{2,6},{3,7},{4,0},{5,1},{6,2},{7,3},{8,12},{9,13},{10,... | collective-permute-start | bytes 196616 | tf_op jit(solution)/shard_map/ppermute | solution.py:331
  36.3 0.5 %collective-permute-start.13 = (f32[4,512]{1,0:T(4,128)S(1)}, f32[4,512]{1,0:T(4,128)S(1)}, u32[]{:S(2)}, u32[]{:S(2)}) collective-permute-start(f32[4,512]{1,0:T(4,128)S(1)} %get-tuple-element.45.near_ref), channel_id=1, source_target_pairs={{0,2},{1,3},{2,0},{3,1},{4,6},{5,7},{6,4},{7,5},{8,10},{9,11},{10,... | collective-permute-start | bytes 24584 | tf_op jit(solution)/shard_map/ppermute | solution.py:331
  36.8 3.1 %collective-permute-done.13.far_ref = f32[4,512]{1,0:T(4,128)S(1)} collective-permute-done((f32[4,512]{1,0:T(4,128)S(1)}, f32[4,512]{1,0:T(4,128)S(1)}, u32[]{:S(2)}, u32[]{:S(2)}) %collective-permute-start.13) | collective-permute-done | bytes 8224 | tf_op jit(solution)/shard_map/ppermute | solution.py:331
  39.9 1.5 %shard_map.101 = (f32[6,1024]{1,0:T(8,128)S(1)}, f32[32,128]{1,0:T(8,128)S(1)}) custom-call(f32[1,512]{1,0:T(1,128)S(1)} %get-tuple-element.29.cot_ref, f32[2,512]{1,0:T(2,128)S(1)} %get-tuple-element.36.stat_ref, f32[4,512]{1,0:T(4,128)S(1)} %get-tuple-element.45.near_ref, f32[4,512]{1,0:T(4,128)S(1)} %collective-permute-done.13.far_ref, ...), custom_call_target="tpu_custom_call" | custom-call | flops 7340032 | bytes 8388608 | tf_op jit(solution)/shard_map/pallas_call | solution.py:421
  41.4 1.6 %collective-permute-start.17 = (f32[6,1024]{1,0:T(8,128)S(1)}, f32[6,1024]{1,0:T(8,128)S(1)}, u32[]{:S(2)}, u32[]{:S(2)}) collective-permute-start(f32[6,1024]{1,0:T(8,128)S(1)} %get-tuple-element.55), channel_id=1, source_target_pairs={{0,16},{16,0},{1,17},{17,1},{2,18},{18,2},{3,19},{19,3},{4,20},{20... | collective-permute-start | bytes 73736 | tf_op jit(solution)/shard_map/ppermute | solution.py:430
  43.0 2.4 %collective-permute-done.17 = f32[6,1024]{1,0:T(8,128)S(1)} collective-permute-done((f32[6,1024]{1,0:T(8,128)S(1)}, f32[6,1024]{1,0:T(8,128)S(1)}, u32[]{:S(2)}, u32[]{:S(2)}) %collective-permute-start.17) | collective-permute-done | bytes 24608 | tf_op jit(solution)/shard_map/ppermute | solution.py:430
  45.4 0.6 %add.3 = f32[6,1024]{1,0:T(8,128)} add(f32[6,1024]{1,0:T(8,128)S(1)} %get-tuple-element.55, f32[6,1024]{1,0:T(8,128)S(1)} %collective-permute-done.17) | non-fusion elementwise | flops 6144 | bytes 73728 | tf_op jit(solution)/shard_map/add | solution.py:430
  46.0 0.0 collective-permute-done.14.refs_0_
  46.0 0.0 collective-permute-done.15.refs_1_
  46.0 0.0 collective-permute-done.16.refs_2_
  46.0 0.8 %shard_map.102 = f32[32,512]{1,0:T(8,128)} custom-call(f32[32,128]{1,0:T(8,128)S(1)} %get-tuple-element.50.gain_ref, f32[128,128]{1,0:T(8,128)S(1)} %get-tuple-element.51.own_ref, f32[128,128]{1,0:T(8,128)S(1)} %collective-permute-done.14.refs_0_, f32[128,128]{1,0:T(8,128)S(1)} %collective-permute-done.15.refs_1_, f32[128,128]{1,0:T(8,128)S(1)} %collective-permute-done.16.refs_2_), custom_call_target="tpu_custom_call" | custom-call | flops 131072 | bytes 131072 | tf_op jit(solution)/shard_map/pallas_call | solution.py:433
  (1 shorter events, 0.0 us)
Async XLA Ops:
  0.6 10.2 %copy-start = (bf16[32,512]{1,0:T(8,128)(2,1)S(1)}, bf16[32,512]{1,0:T(8,128)(2,1)}, u32[]{:S(2)}) copy-start(bf16[32,512]{1,0:T(8,128)(2,1)} %refs_3_.1) | copy-start | bytes 98308
  0.6 11.9 %copy-start.1 = (f32[3,1024]{1,0:T(4,128)S(1)}, f32[3,1024]{1,0:T(4,128)}, u32[]{:S(2)}) copy-start(f32[3,1024]{1,0:T(4,128)} %quad_ref.3) | copy-start | bytes 36868
  0.7 11.9 %copy-start.2 = (f32[2,1024]{1,0:T(2,128)S(1)}, f32[2,1024]{1,0:T(2,128)}, u32[]{:S(2)}) copy-start(f32[2,1024]{1,0:T(2,128)} %lin_ref.3) | copy-start | bytes 24580
  0.7 11.9 %copy-start.4 = (s32[1024]{0:T(1024)S(1)}, s32[1024]{0:T(1024)}, u32[]{:S(2)}) copy-start(s32[1024]{0:T(1024)} %param.14) | copy-start | bytes 12292
  0.7 11.9 %copy-start.3 = (f32[1024]{0:T(1024)S(1)}, f32[1024]{0:T(1024)}, u32[]{:S(2)}) copy-start(f32[1024]{0:T(1024)} %param.13) | copy-start | bytes 12292
  0.7 8.3 %collective-permute-start = (bf16[32,512]{1,0:T(8,128)(2,1)}, bf16[32,512]{1,0:T(8,128)(2,1)S(1)}, u32[]{:S(2)}, u32[]{:S(2)}) collective-permute-start(bf16[32,512]{1,0:T(8,128)(2,1)} %refs_3_.1), channel_id=1, source_target_pairs={{0,12},{1,13},{2,14},{3,15},{4,8},{5,9},{6,10},{7,11},{8,4},{9,5},... | collective-permute-start | bytes 98312 | tf_op jit(solution)/shard_map/ppermute | solution.py:331
  5.8 5.0 %collective-permute-start.1 = (bf16[32,512]{1,0:T(8,128)(2,1)}, bf16[32,512]{1,0:T(8,128)(2,1)S(1)}, u32[]{:S(2)}, u32[]{:S(2)}) collective-permute-start(bf16[32,512]{1,0:T(8,128)(2,1)} %refs_3_.1), channel_id=1, source_target_pairs={{0,8},{1,9},{2,10},{3,11},{4,12},{5,13},{6,14},{7,15},{8,0},{9,1},... | collective-permute-start | bytes 98312 | tf_op jit(solution)/shard_map/ppermute | solution.py:331
  5.8 5.0 %collective-permute-start.2 = (bf16[32,512]{1,0:T(8,128)(2,1)}, bf16[32,512]{1,0:T(8,128)(2,1)S(1)}, u32[]{:S(2)}, u32[]{:S(2)}) collective-permute-start(bf16[32,512]{1,0:T(8,128)(2,1)} %refs_3_.1), channel_id=1, source_target_pairs={{0,4},{1,5},{2,6},{3,7},{4,0},{5,1},{6,2},{7,3},{8,12},{9,13},{10,... | collective-permute-start | bytes 98312 | tf_op jit(solution)/shard_map/ppermute | solution.py:331
  10.8 1.7 %collective-permute-start.4 = (bf16[128,512]{1,0:T(8,128)(2,1)S(1)}, bf16[128,512]{1,0:T(8,128)(2,1)S(1)}, u32[]{:S(2)}, u32[]{:S(2)}) collective-permute-start(bf16[128,512]{1,0:T(8,128)(2,1)S(1)} %shard_map.96.refs_0_), channel_id=1, source_target_pairs={{0,1},{1,0},{2,3},{3,2},{4,5},{5,4},{6,7},{7,6},{8,9},{9,8},{10,11... | collective-permute-start | bytes 393224 | tf_op jit(solution)/shard_map/ppermute | solution.py:331
  10.9 5.9 %collective-permute-start.3 = (bf16[128,512]{1,0:T(8,128)(2,1)S(1)}, bf16[128,512]{1,0:T(8,128)(2,1)S(1)}, u32[]{:S(2)}, u32[]{:S(2)}) collective-permute-start(bf16[128,512]{1,0:T(8,128)(2,1)S(1)} %shard_map.96.refs_0_), channel_id=1, source_target_pairs={{0,2},{1,3},{2,0},{3,1},{4,6},{5,7},{6,4},{7,5},{8,10},{9,11},{10,... | collective-permute-start | bytes 393224 | tf_op jit(solution)/shard_map/ppermute | solution.py:331
  16.8 1.3 %collective-permute-start.5 = (bf16[128,512]{1,0:T(8,128)(2,1)S(1)}, bf16[128,512]{1,0:T(8,128)(2,1)S(1)}, u32[]{:S(2)}, u32[]{:S(2)}) collective-permute-start(bf16[128,512]{1,0:T(8,128)(2,1)S(1)} %collective-permute-done.3.refs_0_), channel_id=1, source_target_pairs={{0,1},{1,0},{2,3},{3,2},{4,5},{5,4},{6,7},{7,6},{8,9},{9,8},{10,11... | collective-permute-start | bytes 393224 | tf_op jit(solution)/shard_map/ppermute | solution.py:331
  21.5 1.6 %collective-permute-start.6 = (f32[128,512]{1,0:T(8,128)S(1)}, f32[128,512]{1,0:T(8,128)S(1)}, u32[]{:S(2)}, u32[]{:S(2)}) collective-permute-start(f32[128,512]{1,0:T(8,128)S(1)} %get-tuple-element.39), channel_id=1, source_target_pairs={{0,1},{1,0},{2,3},{3,2},{4,5},{5,4},{6,7},{7,6},{8,9},{9,8},{10,11... | collective-permute-start | bytes 786440 | tf_op jit(solution)/shard_map/ppermute | solution.py:331
  21.7 1.4 %collective-permute-start.7 = (f32[2,512]{1,0:T(2,128)S(1)}, f32[2,512]{1,0:T(2,128)S(1)}, u32[]{:S(2)}, u32[]{:S(2)}) collective-permute-start(f32[2,512]{1,0:T(2,128)S(1)} %get-tuple-element.36.stat_ref), channel_id=1, source_target_pairs={{0,1},{1,0},{2,3},{3,2},{4,5},{5,4},{6,7},{7,6},{8,9},{9,8},{10,11... | collective-permute-start | bytes 12296 | tf_op jit(solution)/shard_map/ppermute | solution.py:331
  23.4 8.1 %collective-permute-start.8 = (f32[128,512]{1,0:T(8,128)S(1)}, f32[128,512]{1,0:T(8,128)S(1)}, u32[]{:S(2)}, u32[]{:S(2)}) collective-permute-start(f32[128,512]{1,0:T(8,128)S(1)} %get-tuple-element.42), channel_id=1, source_target_pairs={{0,1},{1,0},{2,3},{3,2},{4,5},{5,4},{6,7},{7,6},{8,9},{9,8},{10,11... | collective-permute-start | bytes 786440 | tf_op jit(solution)/shard_map/ppermute | solution.py:331
  23.6 7.9 %collective-permute-start.9 = (bf16[528,128]{1,0:T(8,128)(2,1)S(1)}, bf16[528,128]{1,0:T(8,128)(2,1)S(1)}, u32[]{:S(2)}, u32[]{:S(2)}) collective-permute-start(bf16[528,128]{1,0:T(8,128)(2,1)S(1)} %get-tuple-element.43), channel_id=1, source_target_pairs={{0,2},{1,3},{2,0},{3,1},{4,6},{5,7},{6,4},{7,5},{8,10},{9,11},{10,... | collective-permute-start | bytes 405512 | tf_op jit(solution)/shard_map/ppermute | solution.py:331
  25.1 5.4 %collective-permute-start.12 = (f32[1,512]{1,0:T(1,128)S(1)}, f32[1,512]{1,0:T(1,128)S(1)}, u32[]{:S(2)}, u32[]{:S(2)}) collective-permute-start(f32[1,512]{1,0:T(1,128)S(1)} %get-tuple-element.44.refs_0_), channel_id=1, source_target_pairs={{0,12},{1,13},{2,14},{3,15},{4,8},{5,9},{6,10},{7,11},{8,4},{9,5},... | collective-permute-start | bytes 6152 | tf_op jit(solution)/shard_map/ppermute | solution.py:331
  27.0 4.5 %collective-permute-start.11 = (f32[1,512]{1,0:T(1,128)S(1)}, f32[1,512]{1,0:T(1,128)S(1)}, u32[]{:S(2)}, u32[]{:S(2)}) collective-permute-start(f32[1,512]{1,0:T(1,128)S(1)} %get-tuple-element.44.refs_0_), channel_id=1, source_target_pairs={{0,8},{1,9},{2,10},{3,11},{4,12},{5,13},{6,14},{7,15},{8,0},{9,1},... | collective-permute-start | bytes 6152 | tf_op jit(solution)/shard_map/ppermute | solution.py:331
  27.1 4.4 %collective-permute-start.10 = (f32[1,512]{1,0:T(1,128)S(1)}, f32[1,512]{1,0:T(1,128)S(1)}, u32[]{:S(2)}, u32[]{:S(2)}) collective-permute-start(f32[1,512]{1,0:T(1,128)S(1)} %get-tuple-element.44.refs_0_), channel_id=1, source_target_pairs={{0,4},{1,5},{2,6},{3,7},{4,0},{5,1},{6,2},{7,3},{8,12},{9,13},{10,... | collective-permute-start | bytes 6152 | tf_op jit(solution)/shard_map/ppermute | solution.py:331
  31.8 14.2 %collective-permute-start.14 = (f32[128,128]{1,0:T(8,128)S(1)}, f32[128,128]{1,0:T(8,128)S(1)}, u32[]{:S(2)}, u32[]{:S(2)}) collective-permute-start(f32[128,128]{1,0:T(8,128)S(1)} %get-tuple-element.52), channel_id=1, source_target_pairs={{0,12},{1,13},{2,14},{3,15},{4,8},{5,9},{6,10},{7,11},{8,4},{9,5},... | collective-permute-start | bytes 196616 | tf_op jit(solution)/shard_map/ppermute | solution.py:331
  34.0 12.0 %collective-permute-start.15 = (f32[128,128]{1,0:T(8,128)S(1)}, f32[128,128]{1,0:T(8,128)S(1)}, u32[]{:S(2)}, u32[]{:S(2)}) collective-permute-start(f32[128,128]{1,0:T(8,128)S(1)} %get-tuple-element.53), channel_id=1, source_target_pairs={{0,8},{1,9},{2,10},{3,11},{4,12},{5,13},{6,14},{7,15},{8,0},{9,1},... | collective-permute-start | bytes 196616 | tf_op jit(solution)/shard_map/ppermute | solution.py:331
  34.9 11.1 %collective-permute-start.16 = (f32[128,128]{1,0:T(8,128)S(1)}, f32[128,128]{1,0:T(8,128)S(1)}, u32[]{:S(2)}, u32[]{:S(2)}) collective-permute-start(f32[128,128]{1,0:T(8,128)S(1)} %get-tuple-element.54), channel_id=1, source_target_pairs={{0,4},{1,5},{2,6},{3,7},{4,0},{5,1},{6,2},{7,3},{8,12},{9,13},{10,... | collective-permute-start | bytes 196616 | tf_op jit(solution)/shard_map/ppermute | solution.py:331
  36.3 3.7 %collective-permute-start.13 = (f32[4,512]{1,0:T(4,128)S(1)}, f32[4,512]{1,0:T(4,128)S(1)}, u32[]{:S(2)}, u32[]{:S(2)}) collective-permute-start(f32[4,512]{1,0:T(4,128)S(1)} %get-tuple-element.45.near_ref), channel_id=1, source_target_pairs={{0,2},{1,3},{2,0},{3,1},{4,6},{5,7},{6,4},{7,5},{8,10},{9,11},{10,... | collective-permute-start | bytes 24584 | tf_op jit(solution)/shard_map/ppermute | solution.py:331
  41.4 4.0 %collective-permute-start.17 = (f32[6,1024]{1,0:T(8,128)S(1)}, f32[6,1024]{1,0:T(8,128)S(1)}, u32[]{:S(2)}, u32[]{:S(2)}) collective-permute-start(f32[6,1024]{1,0:T(8,128)S(1)} %get-tuple-element.55), channel_id=1, source_target_pairs={{0,16},{16,0},{1,17},{17,1},{2,18},{18,2},{3,19},{19,3},{4,20},{20... | collective-permute-start | bytes 73736 | tf_op jit(solution)/shard_map/ppermute | solution.py:430

commit v9 on v7

--- a/solution.py
+++ b/solution.py
@@ -426,11 +426,6 @@
         nbytes=16 * cases * width,
         n_in=8,
     )(cot, stat, stack, stack_far, s0, s1, w0, w1)
-    bit = 1
-    while bit < n_case:
-        coef = coef + lax.ppermute(coef, "case", [(i, i ^ bit) for i in range(n_case)])
-        bit *= 2
-
     load_grad = vmem_call(
         combine_kernel,
         shape((rows, units), f32),
@@ -438,6 +433,12 @@
         nbytes=2 * nz * rows * units,
         n_in=2 + len(parts),
     )(gain, own, *parts)
+    bit = 1
+    while bit < n_case:
+        got = lax.ppermute(coef, "case", [(i, i ^ bit) for i in range(n_case)])
+        load_grad, got = lax.optimization_barrier((load_grad, got))
+        coef = coef + got
+        bit *= 2
     return (load_grad, coef)
 
 

time: 43.8 us -> 43 us (0.982)
  waiting for transfers between devices: 9.66 us -> 8.86 us
    ppermute x1, waiting for transfers between devices: 2.43 us -> 1.62 us  [per_device(): got = lax.ppermute(coef, 'case', [(i, i ^ bit) for i in range(n_case)])]
  transfers between devices with their start and end apart: 18 -> 18, of which waited for: 7 -> 7; matrix products, arithmetic and copies ran while one was open for 1% -> 0% of each run, Pallas kernels for 17% -> 19%
where the time goes in v9:
time: 43 us; the launch traced here: 42.9 us
  starting transfers between devices  20.6 us (48%)
  Pallas kernels  12 us (28%)
  waiting for transfers between devices  8.86 us (21%)
  between operations  0.78 us (2%)
  other arithmetic  0.62 us (1%)
    ppermute x17, starting transfers between devices, along(): return lax.ppermute(x, 'elem', [(i, i ^ bits) for i in range(n)])  19.1 us
    ppermute x17, waiting for transfers between devices, along(): return lax.ppermute(x, 'elem', [(i, i ^ bits) for i in range(n)])  7.24 us
    pallas_call x2, Pallas kernels, main(): vmem_call(functools.partial(main_kernel, len(blocks), len(stats)), [shape...  6.65 us
    pallas_call x1, Pallas kernels, per_device(): vmem_call(functools.partial(prep_kernel, n), [shape((units, comps * width...  2.48 us
    ppermute x1, waiting for transfers between devices, per_device(): got = lax.ppermute(coef, 'case', [(i, i ^ bit) for i in range(n_case)])  1.62 us
    ppermute x1, starting transfers between devices, per_device(): got = lax.ppermute(coef, 'case', [(i, i ^ bit) for i in range(n_case)])  1.55 us
    pallas_call x1, Pallas kernels, per_device(): vmem_call(coef_kernel, [shape((6, width), f32), shape((rows, 128), f32)],...  1.51 us
  transfers between devices with their start and end apart: 18, of which 7 were waited for; matrix products, arithmetic and copies ran while one was open for 0% of the time, Pallas kernels for 19%

profile of v9, /device:TPU:0, one launch (start us, length us, event | category | flops | bytes accessed | tf_op | source)
XLA Modules:
  0.0 42.9 jit_solution(1918494433587251390)
XLA Ops:
  0.6 0.0 copy-start
  0.6 0.0 copy-start.1
  0.7 0.0 copy-start.2
  0.7 0.0 copy-start.4
  0.7 0.0 copy-start.3
  0.7 5.1 %collective-permute-start = (bf16[32,512]{1,0:T(8,128)(2,1)}, bf16[32,512]{1,0:T(8,128)(2,1)S(1)}, u32[]{:S(2)}, u32[]{:S(2)}) collective-permute-start(bf16[32,512]{1,0:T(8,128)(2,1)} %refs_3_.1), channel_id=1, source_target_pairs={{0,12},{1,13},{2,14},{3,15},{4,8},{5,9},{6,10},{7,11},{8,4},{9,5},... | collective-permute-start | bytes 98312 | tf_op jit(solution)/shard_map/ppermute | solution.py:332
  5.8 0.0 collective-permute-start.1
  5.8 0.6 %collective-permute-start.2 = (bf16[32,512]{1,0:T(8,128)(2,1)}, bf16[32,512]{1,0:T(8,128)(2,1)S(1)}, u32[]{:S(2)}, u32[]{:S(2)}) collective-permute-start(bf16[32,512]{1,0:T(8,128)(2,1)} %refs_3_.1), channel_id=1, source_target_pairs={{0,4},{1,5},{2,6},{3,7},{4,0},{5,1},{6,2},{7,3},{8,12},{9,13},{10,... | collective-permute-start | bytes 98312 | tf_op jit(solution)/shard_map/ppermute | solution.py:332
  6.4 2.5 %shard_map.95 = (bf16[512,3072]{1,0:T(8,128)(2,1)S(1)}, f32[1,512]{1,0:T(1,128)S(1)}) custom-call(s32[1]{0:T(128)} %bitcast.me_ref, bf16[3,512,1024]{2,1,0:T(8,128)(2,1)} %bitcast.10, s32[3,8,512]{2,1,0:T(8,128)} %bitcast.11, f32[1,512]{1,0:T(1,128)} %bitcast.12), custom_call_target="tpu_custom_call" | custom-call | flops 1572864 | bytes 6291456 | tf_op jit(solution)/shard_map/pallas_call | solution.py:335
  8.9 0.0 collective-permute-done.refs_0_
  8.9 1.9 %collective-permute-done.1.refs_1_ = bf16[32,512]{1,0:T(8,128)(2,1)S(1)} collective-permute-done((bf16[32,512]{1,0:T(8,128)(2,1)}, bf16[32,512]{1,0:T(8,128)(2,1)S(1)}, u32[]{:S(2)}, u32[]{:S(2)}) %collective-permute-start.1) | collective-permute-done | bytes 32800 | tf_op jit(solution)/shard_map/ppermute | solution.py:332
  10.8 0.0 collective-permute-done.2.refs_2_
  10.8 0.0 copy-done
  10.8 0.1 collective-permute-start.4
  10.9 1.6 %collective-permute-start.3 = (bf16[128,512]{1,0:T(8,128)(2,1)S(1)}, bf16[128,512]{1,0:T(8,128)(2,1)S(1)}, u32[]{:S(2)}, u32[]{:S(2)}) collective-permute-start(bf16[128,512]{1,0:T(8,128)(2,1)S(1)} %shard_map.96.refs_0_), channel_id=1, source_target_pairs={{0,2},{1,3},{2,0},{3,1},{4,6},{5,7},{6,4},{7,5},{8,10},{9,11},{10,... | collective-permute-start | bytes 393224 | tf_op jit(solution)/shard_map/ppermute | solution.py:332
  12.5 0.0 collective-permute-done.4.refs_1_
  12.5 0.0 copy-done.1
  12.5 0.0 copy-done.2
  12.5 0.0 copy-done.4
  12.5 0.0 copy-done.3
  12.5 3.3 %shard_map.97 = (f32[128,512]{1,0:T(8,128)S(1)}, f32[128,512]{1,0:T(8,128)S(1)}, f32[2,256]{1,0:T(2,128)S(1)}, f32[256,3072]{1,0:T(8,128)S(1)}, f32[256,1024]{1,0:T(8,128)S(1)}) custom-call(bf16[512,3072]{1,0:T(8,128)(2,1)S(1)} %get-tuple-element.33.f_ref, f32[2,1024]{1,0:T(2,128)S(1)} %copy-done.2, f32[3,1024]{1,0:T(4,128)S(1)} %copy-done.1, ...), custom_call_target="tpu_custom_call" | custom-call | flops 2415919104 | bytes 7340032 | tf_op jit(solution)/shard_map/pallas_call | solution.py:364
  15.9 1.0 %collective-permute-done.3.refs_0_ = bf16[128,512]{1,0:T(8,128)(2,1)S(1)} collective-permute-done((bf16[128,512]{1,0:T(8,128)(2,1)S(1)}, bf16[128,512]{1,0:T(8,128)(2,1)S(1)}, u32[]{:S(2)}, u32[]{:S(2)}) %collective-permute-start.3) | collective-permute-done | bytes 131104 | tf_op jit(solution)/shard_map/ppermute | solution.py:332
  16.8 0.0 collective-permute-start.5
  16.8 1.3 %collective-permute-done.5.refs_1_ = bf16[128,512]{1,0:T(8,128)(2,1)S(1)} collective-permute-done((bf16[128,512]{1,0:T(8,128)(2,1)S(1)}, bf16[128,512]{1,0:T(8,128)(2,1)S(1)}, u32[]{:S(2)}, u32[]{:S(2)}) %collective-permute-start.5) | collective-permute-done | bytes 131104 | tf_op jit(solution)/shard_map/ppermute | solution.py:332
  18.2 3.3 %shard_map.98 = (f32[128,512]{1,0:T(8,128)S(1)}, f32[128,512]{1,0:T(8,128)S(1)}, f32[2,512]{1,0:T(2,128)S(1)}, f32[256,3072]{1,0:T(8,128)S(1)}, f32[256,1024]{1,0:T(8,128)S(1)}) custom-call(bf16[512,3072]{1,0:T(8,128)(2,1)S(1)} %get-tuple-element.33.f_ref, f32[2,1024]{1,0:T(2,128)S(1)} %copy-done.2, f32[3,1024]{1,0:T(4,128)S(1)} %copy-done.1, ...), custom_call_target="tpu_custom_call" | custom-call | flops 2415919104 | bytes 7340032 | tf_op jit(solution)/shard_map/pallas_call | solution.py:364
  21.5 0.2 collective-permute-start.6
  21.7 0.4 collective-permute-start.7
  22.1 1.0 %collective-permute-done.7.twin_ref = f32[2,512]{1,0:T(2,128)S(1)} collective-permute-done((f32[2,512]{1,0:T(2,128)S(1)}, f32[2,512]{1,0:T(2,128)S(1)}, u32[]{:S(2)}, u32[]{:S(2)}) %collective-permute-start.7) | collective-permute-done | bytes 4128 | tf_op jit(solution)/shard_map/ppermute | solution.py:332
  23.1 0.0 collective-permute-done.6.got_ref
  23.1 0.2 shard_map.99
  23.4 0.2 collective-permute-start.8
  23.6 1.5 %collective-permute-start.9 = (bf16[528,128]{1,0:T(8,128)(2,1)S(1)}, bf16[528,128]{1,0:T(8,128)(2,1)S(1)}, u32[]{:S(2)}, u32[]{:S(2)}) collective-permute-start(bf16[528,128]{1,0:T(8,128)(2,1)S(1)} %get-tuple-element.45), channel_id=1, source_target_pairs={{0,2},{1,3},{2,0},{3,1},{4,6},{5,7},{6,4},{7,5},{8,10},{9,11},{10,... | collective-permute-start | bytes 405512 | tf_op jit(solution)/shard_map/ppermute | solution.py:332
  25.1 1.9 %collective-permute-start.12 = (f32[1,512]{1,0:T(1,128)S(1)}, f32[1,512]{1,0:T(1,128)S(1)}, u32[]{:S(2)}, u32[]{:S(2)}) collective-permute-start(f32[1,512]{1,0:T(1,128)S(1)} %get-tuple-element.46.refs_0_), channel_id=1, source_target_pairs={{0,12},{1,13},{2,14},{3,15},{4,8},{5,9},{6,10},{7,11},{8,4},{9,5},... | collective-permute-start | bytes 6152 | tf_op jit(solution)/shard_map/ppermute | solution.py:332
  27.0 0.1 collective-permute-start.11
  27.1 2.4 %collective-permute-start.10 = (f32[1,512]{1,0:T(1,128)S(1)}, f32[1,512]{1,0:T(1,128)S(1)}, u32[]{:S(2)}, u32[]{:S(2)}) collective-permute-start(f32[1,512]{1,0:T(1,128)S(1)} %get-tuple-element.46.refs_0_), channel_id=1, source_target_pairs={{0,4},{1,5},{2,6},{3,7},{4,0},{5,1},{6,2},{7,3},{8,12},{9,13},{10,... | collective-permute-start | bytes 6152 | tf_op jit(solution)/shard_map/ppermute | solution.py:332
  29.5 1.0 %collective-permute-done.12.refs_3_ = f32[1,512]{1,0:T(1,128)S(1)} collective-permute-done((f32[1,512]{1,0:T(1,128)S(1)}, f32[1,512]{1,0:T(1,128)S(1)}, u32[]{:S(2)}, u32[]{:S(2)}) %collective-permute-start.12) | collective-permute-done | bytes 2080 | tf_op jit(solution)/shard_map/ppermute | solution.py:332
  30.5 1.0 %collective-permute-done.11.refs_2_ = f32[1,512]{1,0:T(1,128)S(1)} collective-permute-done((f32[1,512]{1,0:T(1,128)S(1)}, f32[1,512]{1,0:T(1,128)S(1)}, u32[]{:S(2)}, u32[]{:S(2)}) %collective-permute-start.11) | collective-permute-done | bytes 2080 | tf_op jit(solution)/shard_map/ppermute | solution.py:332
  31.5 0.0 collective-permute-done.10.refs_1_
  31.5 0.0 collective-permute-done.9.part_ref
  31.5 0.0 collective-permute-done.8.got_ref
  31.5 0.3 shard_map.100
  31.8 0.6 %collective-permute-start.13 = (f32[4,512]{1,0:T(4,128)S(1)}, f32[4,512]{1,0:T(4,128)S(1)}, u32[]{:S(2)}, u32[]{:S(2)}) collective-permute-start(f32[4,512]{1,0:T(4,128)S(1)} %get-tuple-element.47.near_ref), channel_id=1, source_target_pairs={{0,2},{1,3},{2,0},{3,1},{4,6},{5,7},{6,4},{7,5},{8,10},{9,11},{10,... | collective-permute-start | bytes 24584 | tf_op jit(solution)/shard_map/ppermute | solution.py:332
  32.4 2.1 %collective-permute-start.14 = (bf16[128,128]{1,0:T(8,128)(2,1)S(1)}, bf16[128,128]{1,0:T(8,128)(2,1)S(1)}, u32[]{:S(2)}, u32[]{:S(2)}) collective-permute-start(bf16[128,128]{1,0:T(8,128)(2,1)S(1)} %get-tuple-element.54), channel_id=1, source_target_pairs={{0,12},{1,13},{2,14},{3,15},{4,8},{5,9},{6,10},{7,11},{8,4},{9,5},... | collective-permute-start | bytes 98312 | tf_op jit(solution)/shard_map/ppermute | solution.py:332
  34.5 0.9 %collective-permute-start.15 = (bf16[128,128]{1,0:T(8,128)(2,1)S(1)}, bf16[128,128]{1,0:T(8,128)(2,1)S(1)}, u32[]{:S(2)}, u32[]{:S(2)}) collective-permute-start(bf16[128,128]{1,0:T(8,128)(2,1)S(1)} %get-tuple-element.55), channel_id=1, source_target_pairs={{0,8},{1,9},{2,10},{3,11},{4,12},{5,13},{6,14},{7,15},{8,0},{9,1},... | collective-permute-start | bytes 98312 | tf_op jit(solution)/shard_map/ppermute | solution.py:332
  35.4 1.3 %collective-permute-start.16 = (bf16[128,128]{1,0:T(8,128)(2,1)S(1)}, bf16[128,128]{1,0:T(8,128)(2,1)S(1)}, u32[]{:S(2)}, u32[]{:S(2)}) collective-permute-start(bf16[128,128]{1,0:T(8,128)(2,1)S(1)} %get-tuple-element.56), channel_id=1, source_target_pairs={{0,4},{1,5},{2,6},{3,7},{4,0},{5,1},{6,2},{7,3},{8,12},{9,13},{10,... | collective-permute-start | bytes 98312 | tf_op jit(solution)/shard_map/ppermute | solution.py:332
  36.8 0.0 collective-permute-done.13.far_ref
  36.8 1.5 %shard_map.101 = (f32[6,1024]{1,0:T(8,128)S(1)}, f32[32,128]{1,0:T(8,128)S(1)}) custom-call(f32[1,512]{1,0:T(1,128)S(1)} %get-tuple-element.31.cot_ref, f32[2,512]{1,0:T(2,128)S(1)} %get-tuple-element.38.stat_ref, f32[4,512]{1,0:T(4,128)S(1)} %get-tuple-element.47.near_ref, f32[4,512]{1,0:T(4,128)S(1)} %collective-permute-done.13.far_ref, ...), custom_call_target="tpu_custom_call" | custom-call | flops 7340032 | bytes 8388608 | tf_op jit(solution)/shard_map/pallas_call | solution.py:422
  38.3 1.6 %collective-permute-start.17 = (f32[6,1024]{1,0:T(8,128)S(1)}, f32[6,1024]{1,0:T(8,128)S(1)}, u32[]{:S(2)}, u32[]{:S(2)}) collective-permute-start(f32[6,1024]{1,0:T(8,128)S(1)} %get-tuple-element.57), channel_id=1, source_target_pairs={{0,16},{16,0},{1,17},{17,1},{2,18},{18,2},{3,19},{19,3},{4,20},{20... | collective-permute-start | bytes 73736 | tf_op jit(solution)/shard_map/ppermute | solution.py:438
  39.8 0.0 collective-permute-done.14.refs_0_
  39.8 0.0 collective-permute-done.15.refs_1_
  39.9 0.0 collective-permute-done.16.refs_2_
  39.9 0.8 %shard_map.102 = f32[32,512]{1,0:T(8,128)} custom-call(f32[32,128]{1,0:T(8,128)S(1)} %get-tuple-element.52.gain_ref, f32[128,128]{1,0:T(8,128)S(1)} %get-tuple-element.53.own_ref, bf16[128,128]{1,0:T(8,128)(2,1)S(1)} %collective-permute-done.14.refs_0_, bf16[128,128]{1,0:T(8,128)(2,1)S(1)} %collective-permute-done.15.refs_1_, ...), custom_call_target="tpu_custom_call" | custom-call | flops 131072 | bytes 131072 | tf_op jit(solution)/shard_map/pallas_call | solution.py:429
  40.6 1.6 %collective-permute-done.17 = f32[6,1024]{1,0:T(8,128)S(1)} collective-permute-done((f32[6,1024]{1,0:T(8,128)S(1)}, f32[6,1024]{1,0:T(8,128)S(1)}, u32[]{:S(2)}, u32[]{:S(2)}) %collective-permute-start.17) | collective-permute-done | bytes 24608 | tf_op jit(solution)/shard_map/ppermute | solution.py:438
  42.3 0.6 %add.3 = f32[6,1024]{1,0:T(8,128)} add(f32[6,1024]{1,0:T(8,128)S(1)} %get-tuple-element.57, f32[6,1024]{1,0:T(8,128)S(1)} %collective-permute-done.17) | non-fusion elementwise | flops 6144 | bytes 73728 | tf_op jit(solution)/shard_map/add | solution.py:440
  (1 shorter events, 0.0 us)
Async XLA Ops:
  0.6 10.2 %copy-start = (bf16[32,512]{1,0:T(8,128)(2,1)S(1)}, bf16[32,512]{1,0:T(8,128)(2,1)}, u32[]{:S(2)}) copy-start(bf16[32,512]{1,0:T(8,128)(2,1)} %refs_3_.1) | copy-start | bytes 98308
  0.6 11.9 %copy-start.1 = (f32[3,1024]{1,0:T(4,128)S(1)}, f32[3,1024]{1,0:T(4,128)}, u32[]{:S(2)}) copy-start(f32[3,1024]{1,0:T(4,128)} %quad_ref.3) | copy-start | bytes 36868
  0.7 11.9 %copy-start.2 = (f32[2,1024]{1,0:T(2,128)S(1)}, f32[2,1024]{1,0:T(2,128)}, u32[]{:S(2)}) copy-start(f32[2,1024]{1,0:T(2,128)} %lin_ref.3) | copy-start | bytes 24580
  0.7 11.9 %copy-start.4 = (s32[1024]{0:T(1024)S(1)}, s32[1024]{0:T(1024)}, u32[]{:S(2)}) copy-start(s32[1024]{0:T(1024)} %param.14) | copy-start | bytes 12292
  0.7 11.9 %copy-start.3 = (f32[1024]{0:T(1024)S(1)}, f32[1024]{0:T(1024)}, u32[]{:S(2)}) copy-start(f32[1024]{0:T(1024)} %param.13) | copy-start | bytes 12292
  0.7 8.3 %collective-permute-start = (bf16[32,512]{1,0:T(8,128)(2,1)}, bf16[32,512]{1,0:T(8,128)(2,1)S(1)}, u32[]{:S(2)}, u32[]{:S(2)}) collective-permute-start(bf16[32,512]{1,0:T(8,128)(2,1)} %refs_3_.1), channel_id=1, source_target_pairs={{0,12},{1,13},{2,14},{3,15},{4,8},{5,9},{6,10},{7,11},{8,4},{9,5},... | collective-permute-start | bytes 98312 | tf_op jit(solution)/shard_map/ppermute | solution.py:332
  5.8 5.0 %collective-permute-start.1 = (bf16[32,512]{1,0:T(8,128)(2,1)}, bf16[32,512]{1,0:T(8,128)(2,1)S(1)}, u32[]{:S(2)}, u32[]{:S(2)}) collective-permute-start(bf16[32,512]{1,0:T(8,128)(2,1)} %refs_3_.1), channel_id=1, source_target_pairs={{0,8},{1,9},{2,10},{3,11},{4,12},{5,13},{6,14},{7,15},{8,0},{9,1},... | collective-permute-start | bytes 98312 | tf_op jit(solution)/shard_map/ppermute | solution.py:332
  5.8 5.0 %collective-permute-start.2 = (bf16[32,512]{1,0:T(8,128)(2,1)}, bf16[32,512]{1,0:T(8,128)(2,1)S(1)}, u32[]{:S(2)}, u32[]{:S(2)}) collective-permute-start(bf16[32,512]{1,0:T(8,128)(2,1)} %refs_3_.1), channel_id=1, source_target_pairs={{0,4},{1,5},{2,6},{3,7},{4,0},{5,1},{6,2},{7,3},{8,12},{9,13},{10,... | collective-permute-start | bytes 98312 | tf_op jit(solution)/shard_map/ppermute | solution.py:332
  10.8 1.7 %collective-permute-start.4 = (bf16[128,512]{1,0:T(8,128)(2,1)S(1)}, bf16[128,512]{1,0:T(8,128)(2,1)S(1)}, u32[]{:S(2)}, u32[]{:S(2)}) collective-permute-start(bf16[128,512]{1,0:T(8,128)(2,1)S(1)} %shard_map.96.refs_0_), channel_id=1, source_target_pairs={{0,1},{1,0},{2,3},{3,2},{4,5},{5,4},{6,7},{7,6},{8,9},{9,8},{10,11... | collective-permute-start | bytes 393224 | tf_op jit(solution)/shard_map/ppermute | solution.py:332
  10.9 5.9 %collective-permute-start.3 = (bf16[128,512]{1,0:T(8,128)(2,1)S(1)}, bf16[128,512]{1,0:T(8,128)(2,1)S(1)}, u32[]{:S(2)}, u32[]{:S(2)}) collective-permute-start(bf16[128,512]{1,0:T(8,128)(2,1)S(1)} %shard_map.96.refs_0_), channel_id=1, source_target_pairs={{0,2},{1,3},{2,0},{3,1},{4,6},{5,7},{6,4},{7,5},{8,10},{9,11},{10,... | collective-permute-start | bytes 393224 | tf_op jit(solution)/shard_map/ppermute | solution.py:332
  16.8 1.3 %collective-permute-start.5 = (bf16[128,512]{1,0:T(8,128)(2,1)S(1)}, bf16[128,512]{1,0:T(8,128)(2,1)S(1)}, u32[]{:S(2)}, u32[]{:S(2)}) collective-permute-start(bf16[128,512]{1,0:T(8,128)(2,1)S(1)} %collective-permute-done.3.refs_0_), channel_id=1, source_target_pairs={{0,1},{1,0},{2,3},{3,2},{4,5},{5,4},{6,7},{7,6},{8,9},{9,8},{10,11... | collective-permute-start | bytes 393224 | tf_op jit(solution)/shard_map/ppermute | solution.py:332
  21.5 1.6 %collective-permute-start.6 = (f32[128,512]{1,0:T(8,128)S(1)}, f32[128,512]{1,0:T(8,128)S(1)}, u32[]{:S(2)}, u32[]{:S(2)}) collective-permute-start(f32[128,512]{1,0:T(8,128)S(1)} %get-tuple-element.41), channel_id=1, source_target_pairs={{0,1},{1,0},{2,3},{3,2},{4,5},{5,4},{6,7},{7,6},{8,9},{9,8},{10,11... | collective-permute-start | bytes 786440 | tf_op jit(solution)/shard_map/ppermute | solution.py:332
  21.7 1.4 %collective-permute-start.7 = (f32[2,512]{1,0:T(2,128)S(1)}, f32[2,512]{1,0:T(2,128)S(1)}, u32[]{:S(2)}, u32[]{:S(2)}) collective-permute-start(f32[2,512]{1,0:T(2,128)S(1)} %get-tuple-element.38.stat_ref), channel_id=1, source_target_pairs={{0,1},{1,0},{2,3},{3,2},{4,5},{5,4},{6,7},{7,6},{8,9},{9,8},{10,11... | collective-permute-start | bytes 12296 | tf_op jit(solution)/shard_map/ppermute | solution.py:332
  23.4 8.1 %collective-permute-start.8 = (f32[128,512]{1,0:T(8,128)S(1)}, f32[128,512]{1,0:T(8,128)S(1)}, u32[]{:S(2)}, u32[]{:S(2)}) collective-permute-start(f32[128,512]{1,0:T(8,128)S(1)} %get-tuple-element.44), channel_id=1, source_target_pairs={{0,1},{1,0},{2,3},{3,2},{4,5},{5,4},{6,7},{7,6},{8,9},{9,8},{10,11... | collective-permute-start | bytes 786440 | tf_op jit(solution)/shard_map/ppermute | solution.py:332
  23.6 7.9 %collective-permute-start.9 = (bf16[528,128]{1,0:T(8,128)(2,1)S(1)}, bf16[528,128]{1,0:T(8,128)(2,1)S(1)}, u32[]{:S(2)}, u32[]{:S(2)}) collective-permute-start(bf16[528,128]{1,0:T(8,128)(2,1)S(1)} %get-tuple-element.45), channel_id=1, source_target_pairs={{0,2},{1,3},{2,0},{3,1},{4,6},{5,7},{6,4},{7,5},{8,10},{9,11},{10,... | collective-permute-start | bytes 405512 | tf_op jit(solution)/shard_map/ppermute | solution.py:332
  25.1 5.4 %collective-permute-start.12 = (f32[1,512]{1,0:T(1,128)S(1)}, f32[1,512]{1,0:T(1,128)S(1)}, u32[]{:S(2)}, u32[]{:S(2)}) collective-permute-start(f32[1,512]{1,0:T(1,128)S(1)} %get-tuple-element.46.refs_0_), channel_id=1, source_target_pairs={{0,12},{1,13},{2,14},{3,15},{4,8},{5,9},{6,10},{7,11},{8,4},{9,5},... | collective-permute-start | bytes 6152 | tf_op jit(solution)/shard_map/ppermute | solution.py:332
  27.0 4.5 %collective-permute-start.11 = (f32[1,512]{1,0:T(1,128)S(1)}, f32[1,512]{1,0:T(1,128)S(1)}, u32[]{:S(2)}, u32[]{:S(2)}) collective-permute-start(f32[1,512]{1,0:T(1,128)S(1)} %get-tuple-element.46.refs_0_), channel_id=1, source_target_pairs={{0,8},{1,9},{2,10},{3,11},{4,12},{5,13},{6,14},{7,15},{8,0},{9,1},... | collective-permute-start | bytes 6152 | tf_op jit(solution)/shard_map/ppermute | solution.py:332
  27.1 4.4 %collective-permute-start.10 = (f32[1,512]{1,0:T(1,128)S(1)}, f32[1,512]{1,0:T(1,128)S(1)}, u32[]{:S(2)}, u32[]{:S(2)}) collective-permute-start(f32[1,512]{1,0:T(1,128)S(1)} %get-tuple-element.46.refs_0_), channel_id=1, source_target_pairs={{0,4},{1,5},{2,6},{3,7},{4,0},{5,1},{6,2},{7,3},{8,12},{9,13},{10,... | collective-permute-start | bytes 6152 | tf_op jit(solution)/shard_map/ppermute | solution.py:332
  31.8 5.0 %collective-permute-start.13 = (f32[4,512]{1,0:T(4,128)S(1)}, f32[4,512]{1,0:T(4,128)S(1)}, u32[]{:S(2)}, u32[]{:S(2)}) collective-permute-start(f32[4,512]{1,0:T(4,128)S(1)} %get-tuple-element.47.near_ref), channel_id=1, source_target_pairs={{0,2},{1,3},{2,0},{3,1},{4,6},{5,7},{6,4},{7,5},{8,10},{9,11},{10,... | collective-permute-start | bytes 24584 | tf_op jit(solution)/shard_map/ppermute | solution.py:332
  32.4 7.5 %collective-permute-start.14 = (bf16[128,128]{1,0:T(8,128)(2,1)S(1)}, bf16[128,128]{1,0:T(8,128)(2,1)S(1)}, u32[]{:S(2)}, u32[]{:S(2)}) collective-permute-start(bf16[128,128]{1,0:T(8,128)(2,1)S(1)} %get-tuple-element.54), channel_id=1, source_target_pairs={{0,12},{1,13},{2,14},{3,15},{4,8},{5,9},{6,10},{7,11},{8,4},{9,5},... | collective-permute-start | bytes 98312 | tf_op jit(solution)/shard_map/ppermute | solution.py:332
  34.5 5.3 %collective-permute-start.15 = (bf16[128,128]{1,0:T(8,128)(2,1)S(1)}, bf16[128,128]{1,0:T(8,128)(2,1)S(1)}, u32[]{:S(2)}, u32[]{:S(2)}) collective-permute-start(bf16[128,128]{1,0:T(8,128)(2,1)S(1)} %get-tuple-element.55), channel_id=1, source_target_pairs={{0,8},{1,9},{2,10},{3,11},{4,12},{5,13},{6,14},{7,15},{8,0},{9,1},... | collective-permute-start | bytes 98312 | tf_op jit(solution)/shard_map/ppermute | solution.py:332
  35.4 4.4 %collective-permute-start.16 = (bf16[128,128]{1,0:T(8,128)(2,1)S(1)}, bf16[128,128]{1,0:T(8,128)(2,1)S(1)}, u32[]{:S(2)}, u32[]{:S(2)}) collective-permute-start(bf16[128,128]{1,0:T(8,128)(2,1)S(1)} %get-tuple-element.56), channel_id=1, source_target_pairs={{0,4},{1,5},{2,6},{3,7},{4,0},{5,1},{6,2},{7,3},{8,12},{9,13},{10,... | collective-permute-start | bytes 98312 | tf_op jit(solution)/shard_map/ppermute | solution.py:332
  38.3 4.0 %collective-permute-start.17 = (f32[6,1024]{1,0:T(8,128)S(1)}, f32[6,1024]{1,0:T(8,128)S(1)}, u32[]{:S(2)}, u32[]{:S(2)}) collective-permute-start(f32[6,1024]{1,0:T(8,128)S(1)} %get-tuple-element.57), channel_id=1, source_target_pairs={{0,16},{16,0},{1,17},{17,1},{2,18},{18,2},{3,19},{19,3},{4,20},{20... | collective-permute-start | bytes 73736 | tf_op jit(solution)/shard_map/ppermute | solution.py:438
